TPU v7x, 256 devices: a whole 4x4x8 slice. The times are simulated.
256 devices in a mesh: group: 8 (over z), dom: 32 (over x, y, core).
Axes of the slice: x: 4, y: 4, z: 8, core: 2. Of those that a mesh axis runs over, the one named last changes fastest.
Arguments:
- query_rows: bfloat16 [196608, 256], P(('group', 'dom')), may hold values from -64 to 64
- key_rows: bfloat16 [196608, 256], P(('group', 'dom')), may hold values from -6 to 6
- value_rows: bfloat16 [196608, 256], P(('group', 'dom')), may hold values from -6 to 6
- out_weight: bfloat16 [256, 256], replicated, may hold values from -1.5 to 1.5
- grad_update: bfloat16 [196608, 256], P(('group', 'dom')), may hold values from -6 to 6
- expander_bias: float32 [8], replicated, may hold values from 1 to 5
- tile_block: int32 [256, 6, 8], P(('group', 'dom')), may hold values from 0 to 37, as said below
- tile_count: int32 [256, 6], P(('group', 'dom')), may hold values from 5 to 8, as said below
- send_block: int32 [256, 32], P(('group', 'dom')), may hold values from 0 to 5
- matching: int32 [256, 3, 768], P(('group', 'dom')), may hold values from 0 to 767, each once within a row
Outputs:
- update: bfloat16 [196608, 256], P(('group', 'dom'))
- query_grad: float32 [196608, 256], P(('group', 'dom'))
- key_grad: float32 [196608, 256], P(('group', 'dom'))
- value_grad: float32 [196608, 256], P(('group', 'dom'))
- weight_grad: float32 [256, 256], replicated
Inputs may be any that keep to these rules, and one draw needn't show every extreme that they name: `tile_block`: slot 0 of block b names entry b, the block itself. `tile_count`: some block has all 8 slots in use. `matching`: each row is a permutation of the 768 nodes.
All inputs are finite; a program needn't handle non-finite values.
Results may differ from a plain program's by a relative error of at most 0.035.
Values may be sent and summed in bfloat16 or wider, within the bound.
No kernel may reach another device: no remote copies, remote signals or barrier semaphores. Data moves between devices by JAX's collectives and lax.ppermute only.
A program may use at most 128 MiB of HBM per device.

v0:
```python
import jax
import jax.numpy as jnp
from jax import lax
from jax.sharding import PartitionSpec as P


def from_partner(array, axis, apart):
    return lax.ppermute(array, axis, [(i, i ^ 1 << apart) for i in range(lax.axis_size(axis))])


def outgoing(key_rows, value_rows, send_block, block_rows):
    feature_width = key_rows.shape[1]
    key_blocks = key_rows.reshape(-1, block_rows, feature_width)[send_block]
    value_blocks = value_rows.reshape(-1, block_rows, feature_width)[send_block]
    return (key_blocks, value_blocks)


def block_table(own_rows, received, block_rows):
    feature_width = own_rows.shape[1]
    return jnp.concatenate([own_rows.reshape(-1, block_rows, feature_width), received], axis=0)


def pick_blocks(table, tile_block, slot_index, template):
    return table[tile_block[:, slot_index]].reshape(template.shape)


def tile_scores(query_heads, picked_keys, tile_count, slot_index, score_scale):
    scores = (
        jnp.einsum("bqhd,bkhd->bqhk", query_heads, picked_keys, preferred_element_type=jnp.float32)
        * score_scale
    )
    live_blocks = slot_index < tile_count
    return jnp.where(live_blocks[:, None, None, None], scores, -jnp.inf)


def shards(
    query_rows,
    key_rows,
    value_rows,
    out_weight,
    grad_update,
    expander_bias,
    tile_block,
    tile_count,
    send_block,
    matching,
):
    node_count, feature_width = query_rows.shape
    head_count = expander_bias.shape[0]
    head_dim = feature_width // head_count
    score_scale = head_dim ** (-0.5)
    tile_block = tile_block[0]
    tile_count = tile_count[0]
    send_block = send_block[0]
    matching = matching[0]
    block_count, slot_count = tile_block.shape
    block_rows = node_count // block_count
    devices = lax.axis_size(("group", "dom"))
    top_bit = devices.bit_length() - 1
    query_heads = query_rows.reshape(block_count, block_rows, head_count, head_dim)
    query_flat = query_rows.reshape(node_count, head_count, head_dim)
    sent_keys, sent_values = outgoing(key_rows, value_rows, send_block, block_rows)
    got_keys, got_values = (
        lax.all_to_all(sent_keys, "dom", split_axis=0, concat_axis=0, tiled=True),
        lax.all_to_all(sent_values, "dom", split_axis=0, concat_axis=0, tiled=True),
    )
    table_keys = block_table(key_rows, got_keys, block_rows)
    far_keys = []
    far_values = []
    for turn in range(3):
        moved_keys, moved_values = from_partner(
            (key_rows, value_rows), ("group", "dom"), top_bit - 1 - turn
        )
        far_keys.append(moved_keys[matching[turn]].reshape(node_count, head_count, head_dim))
        far_values.append(moved_values[matching[turn]].reshape(node_count, head_count, head_dim))
    far_keys = jnp.stack(far_keys)
    far_values = jnp.stack(far_values)
    edge_scores = (
        jnp.einsum("nhd,mnhd->nhm", query_flat, far_keys, preferred_element_type=jnp.float32)
        * score_scale
    )
    edge_scores = edge_scores + expander_bias[None, :, None]
    edge_top = edge_scores.max(axis=2)
    start_top = edge_top.reshape(block_count, block_rows, head_count)
    start_total = (
        jnp.exp(edge_scores - edge_top[..., None])
        .sum(axis=2)
        .reshape(block_count, block_rows, head_count)
    )

    def first_pass(slot_index, running):
        row_top, row_total = running
        picked_keys = pick_blocks(table_keys, tile_block, slot_index, query_heads)
        scores = tile_scores(query_heads, picked_keys, tile_count, slot_index, score_scale)
        newer = jnp.maximum(row_top, scores.max(axis=3))
        row_total = row_total * jnp.exp(row_top - newer) + jnp.exp(scores - newer[..., None]).sum(
            axis=3
        )
        return (newer, row_total)

    row_top, row_total = lax.fori_loop(0, slot_count, first_pass, (start_top, start_total))
    table_values = block_table(value_rows, got_values, block_rows)
    flat_top = row_top.reshape(node_count, head_count)
    flat_total = row_total.reshape(node_count, head_count)
    edge_prob = jnp.exp(edge_scores - flat_top[..., None]) / flat_total[..., None]
    edge_weight = edge_prob.astype(jnp.bfloat16)
    start_mix = jnp.einsum(
        "nhm,mnhd->nhd", edge_weight, far_values, preferred_element_type=jnp.float32
    )
    start_mix = start_mix.reshape(block_count, block_rows, head_count, head_dim)

    def second_pass(slot_index, accumulated):
        picked_keys = pick_blocks(table_keys, tile_block, slot_index, query_heads)
        picked_values = pick_blocks(table_values, tile_block, slot_index, query_heads)
        scores = tile_scores(query_heads, picked_keys, tile_count, slot_index, score_scale)
        weight = (jnp.exp(scores - row_top[..., None]) / row_total[..., None]).astype(jnp.bfloat16)
        return accumulated + jnp.einsum(
            "bqhk,bkhd->bqhd", weight, picked_values, preferred_element_type=jnp.float32
        )

    mixed = lax.fori_loop(0, slot_count, second_pass, start_mix)
    attended = mixed.reshape(node_count, feature_width).astype(jnp.bfloat16)
    update = jnp.dot(attended, out_weight, preferred_element_type=jnp.float32).astype(jnp.bfloat16)
    grad_attended = jnp.dot(grad_update, out_weight.T, preferred_element_type=jnp.float32).astype(
        jnp.bfloat16
    )
    weight_term = jnp.dot(attended.T, grad_update, preferred_element_type=jnp.float32)
    weight_grad = lax.psum(weight_term, ("group", "dom")) * (node_count * devices) ** (-0.5)
    grad_flat = grad_attended.reshape(node_count, head_count, head_dim)
    grad_heads = grad_attended.reshape(block_count, block_rows, head_count, head_dim)
    row_delta = jnp.sum(
        (grad_attended.astype(jnp.float32) * attended.astype(jnp.float32)).reshape(
            node_count, head_count, head_dim
        ),
        axis=2,
    )
    delta_heads = row_delta.reshape(block_count, block_rows, head_count)
    edge_gprob = jnp.einsum(
        "nhd,mnhd->nhm", grad_flat, far_values, preferred_element_type=jnp.float32
    )
    edge_gscore = (edge_prob * (edge_gprob - row_delta[..., None]) * score_scale).astype(
        jnp.bfloat16
    )
    edge_query_grad = jnp.einsum(
        "nhm,mnhd->nhd", edge_gscore, far_keys, preferred_element_type=jnp.float32
    )
    edge_kterms = jnp.einsum(
        "nhm,nhd->mnhd", edge_gscore, query_flat, preferred_element_type=jnp.float32
    )
    edge_vterms = jnp.einsum(
        "nhm,nhd->mnhd", edge_weight, grad_flat, preferred_element_type=jnp.float32
    )
    entries = block_count + send_block.shape[0]
    empty_table = jnp.zeros((entries, block_rows, feature_width), jnp.float32)
    empty_query = jnp.zeros((block_count, block_rows, head_count, head_dim), jnp.float32)

    def backward_slot(slot_index, running):
        query_accum, key_table, value_table = running
        picked_keys = pick_blocks(table_keys, tile_block, slot_index, query_heads)
        picked_values = pick_blocks(table_values, tile_block, slot_index, query_heads)
        scores = tile_scores(query_heads, picked_keys, tile_count, slot_index, score_scale)
        probability = jnp.exp(scores - row_top[..., None]) / row_total[..., None]
        weight = probability.astype(jnp.bfloat16)
        grad_prob = jnp.einsum(
            "bqhd,bkhd->bqhk", grad_heads, picked_values, preferred_element_type=jnp.float32
        )
        grad_score = (probability * (grad_prob - delta_heads[..., None]) * score_scale).astype(
            jnp.bfloat16
        )
        query_accum = query_accum + jnp.einsum(
            "bqhk,bkhd->bqhd", grad_score, picked_keys, preferred_element_type=jnp.float32
        )
        key_slot = jnp.einsum(
            "bqhk,bqhd->bkhd", grad_score, query_heads, preferred_element_type=jnp.float32
        )
        value_slot = jnp.einsum(
            "bqhk,bqhd->bkhd", weight, grad_heads, preferred_element_type=jnp.float32
        )
        targets = tile_block[:, slot_index]
        key_table = key_table.at[targets].add(
            key_slot.reshape(block_count, block_rows, feature_width)
        )
        value_table = value_table.at[targets].add(
            value_slot.reshape(block_count, block_rows, feature_width)
        )
        return (query_accum, key_table, value_table)

    query_accum, table_kgrad, table_vgrad = lax.fori_loop(
        0, slot_count, backward_slot, (empty_query, empty_table, empty_table)
    )
    return_key = table_kgrad[block_count:].astype(jnp.bfloat16)
    return_value = table_vgrad[block_count:].astype(jnp.bfloat16)
    home_key, home_value = (
        lax.all_to_all(return_key, "dom", split_axis=0, concat_axis=0, tiled=True),
        lax.all_to_all(return_value, "dom", split_axis=0, concat_axis=0, tiled=True),
    )
    key_grad = table_kgrad[:block_count].at[send_block].add(home_key.astype(jnp.float32))
    value_grad = table_vgrad[:block_count].at[send_block].add(home_value.astype(jnp.float32))
    key_grad = key_grad.reshape(node_count, feature_width)
    value_grad = value_grad.reshape(node_count, feature_width)
    for turn in range(3):
        placed_key = (
            jnp.zeros((node_count, feature_width), jnp.bfloat16)
            .at[matching[turn]]
            .set(edge_kterms[turn].reshape(node_count, feature_width).astype(jnp.bfloat16))
        )
        placed_value = (
            jnp.zeros((node_count, feature_width), jnp.bfloat16)
            .at[matching[turn]]
            .set(edge_vterms[turn].reshape(node_count, feature_width).astype(jnp.bfloat16))
        )
        owned_key, owned_value = from_partner(
            (placed_key, placed_value), ("group", "dom"), top_bit - 1 - turn
        )
        key_grad = key_grad + owned_key.astype(jnp.float32)
        value_grad = value_grad + owned_value.astype(jnp.float32)
    query_grad = query_accum.reshape(node_count, feature_width) + edge_query_grad.reshape(
        node_count, feature_width
    )
    return (update, query_grad, key_grad, value_grad, weight_grad)


def solution(mesh):
    in_specs = (
        P(("group", "dom"), None),
        P(("group", "dom"), None),
        P(("group", "dom"), None),
        P(),
        P(("group", "dom"), None),
        P(),
        P(("group", "dom"), None, None),
        P(("group", "dom"), None),
        P(("group", "dom"), None),
        P(("group", "dom"), None, None),
    )
    out_specs = (
        P(("group", "dom"), None),
        P(("group", "dom"), None),
        P(("group", "dom"), None),
        P(("group", "dom"), None),
        P(),
    )
    return jax.shard_map(shards, mesh=mesh, in_specs=in_specs, out_specs=out_specs, check_vma=False)
```

profile of v0, /device:TPU:8, one launch (start us, length us, event | category | flops | bytes accessed | tf_op | source)
XLA Modules:
  0.0 817.0 jit_solution(2056804167866280250)
XLA Ops:
  10.9 7.7 all-to-all-start
  18.7 3.4 collective-permute-start.1
  22.0 5.4 collective-permute-start
  30.1 27.8 %collective-permute-done.1 = bf16[768,256]{1,0:T(8,128)(2,1)S(1)} collective-permute-done((bf16[768,256]{1,0:T(8,128)(2,1)S(1)}, bf16[768,256]{1,0:T(8,128)(2,1)S(1)}, u32[]{:S(2)}, u32[]{:S(2)}) %collective-permute-start.1) | collective-permute-done | bytes 393248 | tf_op jit(solution)/shard_map/ppermute | solution.py:8
  74.6 3.3 gather_fusion.5
  83.4 7.2 collective-permute-done.4
  93.5 3.3 gather_fusion.9
  98.0 3.3 gather_fusion.11
  105.6 7.8 all-to-all-start.1
  116.7 65.4 %while.46 = (s32[]{:T(128)}, f32[6,128,8]{1,2,0:T(8,128)}, f32[6,128,8]{1,2,0:T(8,128)S(1)}, s32[6]{0:T(128)S(1)}, s32[6,8]{0,1:T(8,128)}, /*index=5*/bf16[38,12...) while((s32[]{:T(128)}, f32[6,128,8]{1,2,0:T(8,128)}, f32[6,128,8]{1,2,0:T(8,128)S(1)}, ...), condition=%wide.region_5.6_spmd, body=%wide.region_2.5_spmd.sunk | while | flops 55850008 | bytes 8974575 | solution.py:101
  183.3 3.3 pad_maximum_fusion.1
  186.6 67.0 %while.47 = (s32[]{:T(128)}, f32[6,128,8,32]{1,3,2,0:T(8,128)S(1)}, s32[6,8]{0,1:T(8,128)}, bf16[38,128,256]{2,1,0:T(8,128)(2,1)}, s32[6]{0:T(128)S(1)}, /*index...) while((s32[]{:T(128)}, f32[6,128,8,32]{1,3,2,0:T(8,128)S(1)}, ...), condition=%wide.region_7.8_spmd, body=%wide.region_6.7_spmd.sunk | while | flops 104793112 | bytes 5951761 | solution.py:121
  261.9 191.0 %while.48 = (s32[]{:T(128)}, f32[6,128,8,32]{1,3,2,0:T(8,128)}, f32[38,128,256]{2,1,0:T(8,128)}, f32[38,128,256]{2,1,0:T(8,128)}, s32[6,8]{0,1:T(8,128)}, /*inde...) while((s32[]{:T(128)}, f32[6,128,8,32]{1,3,2,0:T(8,128)}, ...), condition=%wide.region_12.0_spmd.clone, body=%wide.region_9.12_spmd.clone.sunk | while | flops 259523616 | bytes 34484704 | solution.py:188
  452.9 3.8 slice.112
  456.7 7.5 all-to-all-start.2
  465.6 3.9 slice.111
  472.6 18.7 %all-to-all-done.2 = bf16[32,128,256]{2,1,0:T(8,128)(2,1)} async-done(((bf16[32,128,256]{2,1,0:T(8,128)(2,1)}), bf16[32,128,256]{2,1,0:T(8,128)(2,1)}, u32[]{:S(2)}, u32[]{:S(2)}) %all-to-all-start.2) | async-done | bytes 2097184 | tf_op jit(solution)/shard_map/all_to_all | solution.py:194
  491.3 6.6 all-to-all-start.3
  506.1 6.5 scatter_custom_fusion.3
  512.6 6.5 scatter_custom_fusion.5
  521.3 6.6 scatter_custom_fusion.7
  528.9 6.6 scatter_custom_fusion.9
  537.4 6.5 scatter_custom_fusion.8
  545.8 6.5 scatter_custom_fusion.4
  557.3 7.0 collective-permute-start.6
  568.2 14.5 %collective-permute-done.7 = bf16[768,256]{1,0:T(8,128)(2,1)} collective-permute-done((bf16[768,256]{1,0:T(8,128)(2,1)}, bf16[768,256]{1,0:T(8,128)(2,1)}, u32[]{:S(2)}, u32[]{:S(2)}) %collective-permute-start.7) | collective-permute-done | bytes 393248 | tf_op jit(solution)/shard_map/ppermute | solution.py:8
  582.8 5.7 collective-permute-start.9
  588.5 194.2 %all-reduce.2.cloned.1.call-done = f32[256,256]{1,0:T(8,128)} async-done(((f32[256,256]{1,0:T(8,128)}), f32[256,256]{1,0:T(8,128)}) %all-reduce.2.cloned.1.call-update) | async-done | bytes 262160 | tf_op jit(solution)/shard_map/psum | solution.py:128
  784.4 4.1 convert_element_type.103
  788.5 6.4 scatter_fusion.2
  794.9 4.1 convert_element_type.110
  799.0 6.4 scatter_fusion.3
  (487 shorter events, 406.0 us)
Async XLA Ops:
  7.2 246.9 %copy-start = (bf16[768,256]{1,0:T(8,128)(2,1)S(1)}, bf16[768,256]{1,0:T(8,128)(2,1)}, u32[]{:S(2)}) copy-start(bf16[768,256]{1,0:T(8,128)(2,1)} %param.20) | copy-start | bytes 1179652
  10.9 17.5 %copy-start.5 = (bf16[768,256]{1,0:T(8,128)(2,1)S(1)}, bf16[768,256]{1,0:T(8,128)(2,1)}, u32[]{:S(2)}) copy-start(bf16[768,256]{1,0:T(8,128)(2,1)} %param.18) | copy-start | bytes 1179652
  10.9 19.1 %copy-start.32 = (s32[1,3,768]{2,0,1:T(1,128)S(1)}, s32[1,3,768]{2,0,1:T(1,128)}, u32[]{:S(2)}) copy-start(s32[1,3,768]{2,0,1:T(1,128)} %param.25) | copy-start | bytes 27652
  10.9 94.7 %all-to-all-start = ((bf16[32,128,256]{2,1,0:T(8,128)(2,1)}), bf16[32,128,256]{2,1,0:T(8,128)(2,1)}, u32[]{:S(2)}, u32[]{:S(2)}) async-start(bf16[32,128,256]{2,1,0:T(8,128)(2,1)} %gather_fusion.8), calls=%async_computation | async-start | bytes 4194304 | tf_op jit(solution)/shard_map/all_to_all | solution.py:64
  18.7 39.2 %collective-permute-start.1 = (bf16[768,256]{1,0:T(8,128)(2,1)S(1)}, bf16[768,256]{1,0:T(8,128)(2,1)S(1)}, u32[]{:S(2)}, u32[]{:S(2)}) collective-permute-start(bf16[768,256]{1,0:T(8,128)(2,1)S(1)} %copy-done.4), channel_id=1, source_target_pairs={{0,64},{1,65},{2,66},{3,67},{4,68},{5,69},{6,70},{7,71},{8,72},{9,... | collective-permute-start | bytes 1179656 | tf_op jit(solution)/shard_map/ppermute | solution.py:8
  22.0 52.6 %collective-permute-start = (bf16[768,256]{1,0:T(8,128)(2,1)S(1)}, bf16[768,256]{1,0:T(8,128)(2,1)S(1)}, u32[]{:S(2)}, u32[]{:S(2)}) collective-permute-start(bf16[768,256]{1,0:T(8,128)(2,1)S(1)} %copy-done.4), channel_id=1, source_target_pairs={{0,128},{1,129},{2,130},{3,131},{4,132},{5,133},{6,134},{7,135},{8... | collective-permute-start | bytes 1179656 | tf_op jit(solution)/shard_map/ppermute | solution.py:8
  27.4 52.4 %collective-permute-start.2 = (bf16[768,256]{1,0:T(8,128)(2,1)S(1)}, bf16[768,256]{1,0:T(8,128)(2,1)S(1)}, u32[]{:S(2)}, u32[]{:S(2)}) collective-permute-start(bf16[768,256]{1,0:T(8,128)(2,1)S(1)} %copy-done.4), channel_id=1, source_target_pairs={{0,32},{1,33},{2,34},{3,35},{4,36},{5,37},{6,38},{7,39},{8,40},{9,... | collective-permute-start | bytes 1179656 | tf_op jit(solution)/shard_map/ppermute | solution.py:8
  28.5 62.2 %collective-permute-start.4 = (bf16[768,256]{1,0:T(8,128)(2,1)S(1)}, bf16[768,256]{1,0:T(8,128)(2,1)S(1)}, u32[]{:S(2)}, u32[]{:S(2)}) collective-permute-start(bf16[768,256]{1,0:T(8,128)(2,1)S(1)} %copy-done.5), channel_id=1, source_target_pairs={{0,64},{1,65},{2,66},{3,67},{4,68},{5,69},{6,70},{7,71},{8,72},{9,... | collective-permute-start | bytes 1179656 | tf_op jit(solution)/shard_map/ppermute | solution.py:8
  29.9 63.5 %collective-permute-start.3 = (bf16[768,256]{1,0:T(8,128)(2,1)S(1)}, bf16[768,256]{1,0:T(8,128)(2,1)S(1)}, u32[]{:S(2)}, u32[]{:S(2)}) collective-permute-start(bf16[768,256]{1,0:T(8,128)(2,1)S(1)} %copy-done.5), channel_id=1, source_target_pairs={{0,128},{1,129},{2,130},{3,131},{4,132},{5,133},{6,134},{7,135},{8... | collective-permute-start | bytes 1179656 | tf_op jit(solution)/shard_map/ppermute | solution.py:8
  30.0 28.7 %copy-start.31 = (s32[768]{0:T(1024)}, s32[768]{0:T(1024)S(1)}, u32[]{:S(2)}) copy-start(s32[768]{0:T(1024)S(1)} %get-tuple-element.645) | copy-start | bytes 9220
  30.0 38.2 %copy-start.30 = (s32[768]{0:T(1024)}, s32[768]{0:T(1024)S(1)}, u32[]{:S(2)}) copy-start(s32[768]{0:T(1024)S(1)} %get-tuple-element.646) | copy-start | bytes 9220
  57.8 40.2 %collective-permute-start.5 = (bf16[768,256]{1,0:T(8,128)(2,1)S(1)}, bf16[768,256]{1,0:T(8,128)(2,1)S(1)}, u32[]{:S(2)}, u32[]{:S(2)}) collective-permute-start(bf16[768,256]{1,0:T(8,128)(2,1)S(1)} %copy-done.5), channel_id=1, source_target_pairs={{0,32},{1,33},{2,34},{3,35},{4,36},{5,37},{6,38},{7,39},{8,40},{9,... | collective-permute-start | bytes 1179656 | tf_op jit(solution)/shard_map/ppermute | solution.py:8
  74.6 27.9 %copy-start.12 = (bf16[768,256]{0,1:T(8,128)(2,1)}, bf16[768,256]{0,1:T(8,128)(2,1)S(1)}, u32[]{:S(2)}) copy-start(bf16[768,256]{0,1:T(8,128)(2,1)S(1)} %copy.76) | copy-start | bytes 1179652
  93.4 89.5 %copy-start.8 = (bf16[768,256]{0,1:T(8,128)(2,1)}, bf16[768,256]{0,1:T(8,128)(2,1)S(1)}, u32[]{:S(2)}) copy-start(bf16[768,256]{0,1:T(8,128)(2,1)S(1)} %copy.83) | copy-start | bytes 1179652
  98.0 85.0 %copy-start.10 = (bf16[768,256]{0,1:T(8,128)(2,1)}, bf16[768,256]{0,1:T(8,128)(2,1)S(1)}, u32[]{:S(2)}) copy-start(bf16[768,256]{0,1:T(8,128)(2,1)S(1)} %copy.82) | copy-start | bytes 1179652
  102.5 80.5 %copy-start.11 = (bf16[768,256]{0,1:T(8,128)(2,1)}, bf16[768,256]{0,1:T(8,128)(2,1)S(1)}, u32[]{:S(2)}) copy-start(bf16[768,256]{0,1:T(8,128)(2,1)S(1)} %copy.84) | copy-start | bytes 1179652
  105.6 77.7 %all-to-all-start.1 = ((bf16[32,128,256]{2,1,0:T(8,128)(2,1)}), bf16[32,128,256]{2,1,0:T(8,128)(2,1)}, u32[]{:S(2)}, u32[]{:S(2)}) async-start(bf16[32,128,256]{2,1,0:T(8,128)(2,1)} %gather_fusion.12), calls=%async_computation.1 | async-start | bytes 4194304 | tf_op jit(solution)/shard_map/all_to_all | solution.py:65
  116.7 65.4 %copy-start.18 = (f32[768,8,3]{0,1,2:T(8,128)S(1)}, f32[768,8,3]{0,1,2:T(8,128)}, u32[]{:S(2)}) copy-start(f32[768,8,3]{0,1,2:T(8,128)} %copy-done.17) | copy-start | bytes 221188
  186.6 67.4 %copy-start.37 = (bf16[256,256]{1,0:T(8,128)(2,1)S(1)}, bf16[256,256]{1,0:T(8,128)(2,1)}, u32[]{:S(2)}) copy-start(bf16[256,256]{1,0:T(8,128)(2,1)} %param.19) | copy-start | bytes 393220
  456.7 34.5 %all-to-all-start.2 = ((bf16[32,128,256]{2,1,0:T(8,128)(2,1)}), bf16[32,128,256]{2,1,0:T(8,128)(2,1)}, u32[]{:S(2)}, u32[]{:S(2)}) async-start(bf16[32,128,256]{2,1,0:T(8,128)(2,1)} %slice.112), calls=%async_computation.2 | async-start | bytes 4194304 | tf_op jit(solution)/shard_map/all_to_all | solution.py:194
  464.3 318.5 %all-reduce.2.cloned.1.call-start = ((), (), s32[]{:S(2)}) async-start(), calls=%async_computation.4 | async-start | bytes 524288 | tf_op jit(solution)/shard_map/psum | solution.py:128
  471.7 26.2 %copy-start.9 = (bf16[768,256]{0,1:T(8,128)(2,1)S(1)}, bf16[768,256]{0,1:T(8,128)(2,1)}, u32[]{:S(2)}) copy-start(bf16[768,256]{0,1:T(8,128)(2,1)} %copy-done.8) | copy-start | bytes 1179652
  491.3 303.7 %all-to-all-start.3 = ((bf16[32,128,256]{2,1,0:T(8,128)(2,1)}), bf16[32,128,256]{2,1,0:T(8,128)(2,1)}, u32[]{:S(2)}, u32[]{:S(2)}) async-start(bf16[32,128,256]{2,1,0:T(8,128)(2,1)} %slice.111), calls=%async_computation.3 | async-start | bytes 4194304 | tf_op jit(solution)/shard_map/all_to_all | solution.py:195
  520.1 44.2 %copy-start.3 = (f32[6,128,8,32]{1,3,2,0:T(8,128)S(1)}, f32[6,128,8,32]{1,3,2,0:T(8,128)}, u32[]{:S(2)}) copy-start(f32[6,128,8,32]{1,3,2,0:T(8,128)} %get-tuple-element.503) | copy-start | bytes 2359300
  528.9 35.8 %copy-start.16 = (f32[768,8,32]{0,2,1:T(8,128)S(1)}, f32[768,8,32]{0,2,1:T(8,128)}, u32[]{:S(2)}) copy-start(f32[768,8,32]{0,2,1:T(8,128)} %get-tuple-element.717) | copy-start | bytes 2359300
  552.3 30.4 %collective-permute-start.7 = (bf16[768,256]{1,0:T(8,128)(2,1)}, bf16[768,256]{1,0:T(8,128)(2,1)}, u32[]{:S(2)}, u32[]{:S(2)}) collective-permute-start(bf16[768,256]{1,0:T(8,128)(2,1)} %scatter_custom_fusion.4), channel_id=1, source_target_pairs={{0,64},{1,65},{2,66},{3,67},{4,68},{5,69},{6,70},{7,71},{8,72},{9,... | collective-permute-start | bytes 1179656 | tf_op jit(solution)/shard_map/ppermute | solution.py:8
  552.3 255.4 %collective-permute-start.10 = (bf16[768,256]{1,0:T(8,128)(2,1)}, bf16[768,256]{1,0:T(8,128)(2,1)}, u32[]{:S(2)}, u32[]{:S(2)}) collective-permute-start(bf16[768,256]{1,0:T(8,128)(2,1)} %scatter_custom_fusion.8), channel_id=1, source_target_pairs={{0,64},{1,65},{2,66},{3,67},{4,68},{5,69},{6,70},{7,71},{8,72},{9,... | collective-permute-start | bytes 1179656 | tf_op jit(solution)/shard_map/ppermute | solution.py:8
  555.3 252.5 %collective-permute-start.11 = (bf16[768,256]{1,0:T(8,128)(2,1)}, bf16[768,256]{1,0:T(8,128)(2,1)}, u32[]{:S(2)}, u32[]{:S(2)}) collective-permute-start(bf16[768,256]{1,0:T(8,128)(2,1)} %scatter_custom_fusion.9), channel_id=1, source_target_pairs={{0,32},{1,33},{2,34},{3,35},{4,36},{5,37},{6,38},{7,39},{8,40},{9,... | collective-permute-start | bytes 1179656 | tf_op jit(solution)/shard_map/ppermute | solution.py:8
  556.6 248.8 %collective-permute-start.8 = (bf16[768,256]{1,0:T(8,128)(2,1)}, bf16[768,256]{1,0:T(8,128)(2,1)}, u32[]{:S(2)}, u32[]{:S(2)}) collective-permute-start(bf16[768,256]{1,0:T(8,128)(2,1)} %scatter_custom_fusion.5), channel_id=1, source_target_pairs={{0,32},{1,33},{2,34},{3,35},{4,36},{5,37},{6,38},{7,39},{8,40},{9,... | collective-permute-start | bytes 1179656 | tf_op jit(solution)/shard_map/ppermute | solution.py:8
  557.3 248.2 %collective-permute-start.6 = (bf16[768,256]{1,0:T(8,128)(2,1)}, bf16[768,256]{1,0:T(8,128)(2,1)}, u32[]{:S(2)}, u32[]{:S(2)}) collective-permute-start(bf16[768,256]{1,0:T(8,128)(2,1)} %scatter_custom_fusion.3), channel_id=1, source_target_pairs={{0,128},{1,129},{2,130},{3,131},{4,132},{5,133},{6,134},{7,135},{8... | collective-permute-start | bytes 1179656 | tf_op jit(solution)/shard_map/ppermute | solution.py:8
  564.9 17.8 %copy-start.29 = (bf16[768,256]{1,0:T(8,128)(2,1)S(1)}, bf16[768,256]{1,0:T(8,128)(2,1)}, u32[]{:S(2)}) copy-start(bf16[768,256]{1,0:T(8,128)(2,1)} %scatter_custom_fusion.7) | copy-start | bytes 1179652
  582.8 225.0 %collective-permute-start.9 = (bf16[768,256]{1,0:T(8,128)(2,1)S(1)}, bf16[768,256]{1,0:T(8,128)(2,1)S(1)}, u32[]{:S(2)}, u32[]{:S(2)}) collective-permute-start(bf16[768,256]{1,0:T(8,128)(2,1)S(1)} %copy-done.29), channel_id=1, source_target_pairs={{0,128},{1,129},{2,130},{3,131},{4,132},{5,133},{6,134},{7,135},{8... | collective-permute-start | bytes 1179656 | tf_op jit(solution)/shard_map/ppermute | solution.py:8
  (52 other events, 223.7 us)
Sparse Core Ops, SparseCore 0:
  471.8 310.9 all-reduce.1
where the time goes:
time: 832 us; the launch traced here: 817 us
  waiting for transfers between devices  262 us (31%)
  local copies, waits for them, and re-layouts  221 us (27%)
  other arithmetic  132 us (16%)
  matrix products  126 us (15%)
  starting transfers between devices  59.5 us (7%)
  between operations  14.9 us (2%)
    psum x1, waiting for transfers between devices, shards(): lax.psum(weight_term, ('group', 'dom')) * (node_count * devices) ** (-0.5)  194 us
    gather x80, local copies, waits for them, and re-layouts, pick_blocks(): return table[tile_block[:, slot_index]].reshape(template.shape)  105 us
    ppermute x12, waiting for transfers between devices, from_partner(): lax.ppermute(array, axis, [(i, i ^ 1 << apart) for i in range(lax.axis_si...  49.6 us
    dot_general x16, matrix products, tile_scores(): jnp.einsum('bqhd,bkhd->bqhk', query_heads, picked_keys, preferred_element...  33.7 us
    ppermute x12, starting transfers between devices, from_partner(): lax.ppermute(array, axis, [(i, i ^ 1 << apart) for i in range(lax.axis_si...  29.8 us
    scatter-add x8, other arithmetic, backward_slot(): value_table.at[targets]  24.8 us
    scatter-add x8, other arithmetic, backward_slot(): key_table.at[targets]  24.8 us
    dot_general x8, matrix products, backward_slot(): jnp.einsum('bqhk,bkhd->bqhd', grad_score, picked_keys, preferred_element_...  21.1 us
  transfers between devices with their start and end apart: 17, of which 5 were waited for; matrix products, arithmetic and copies ran while one was open for 25% of the time, Pallas kernels for 0%

commit v1 on v0

v1 whole, which is shorter than its diff:
```python
import functools

import jax
import jax.numpy as jnp
from jax import lax
from jax.experimental import pallas as pl
from jax.experimental.pallas import tpu as pltpu
from jax.sharding import PartitionSpec as P

F32, BF16 = jnp.float32, jnp.bfloat16
LOG2E = 1.4426950408889634
GATHER, PREPARE, FORWARD, MERGE, BACKWARD, COLLECT, FINISH = (
    round(1.15e9 * us) for us in (0.5, 1, 2, 2, 14, 1, 1)
)
BUFFERS = 2
VMEM_LIMIT = 56 * 1024 * 1024
ROWS_ACROSS = (((1,), (1,)), ((), ()))
ROWS_DOWN = (((0,), (0,)), ((), ()))


def whole(shape):
    return pl.BlockSpec(shape, lambda *_: (0,) * len(shape), pipeline_mode=pl.Buffered(1))


def params():
    return pltpu.CompilerParams(vmem_limit_bytes=VMEM_LIMIT)


def cost(flops, moved):
    return pl.CostEstimate(flops=flops, bytes_accessed=moved, transcendentals=0)


def dot(a, b, dims=(((1,), (0,)), ((), ()))):
    return lax.dot_general(a, b, dims, preferred_element_type=F32)


def gather_kernel(send_block, key_ref, value_ref, sent_ref, rows, sems):
    width = key_ref.shape[1]
    block_rows = sent_ref.shape[1]
    rows[:, :width] = key_ref[...]
    rows[:, width:] = value_ref[...]
    copies = []
    for slot in range(sent_ref.shape[0]):
        start = pl.multiple_of(send_block[slot] * block_rows, block_rows)
        copy = pltpu.make_async_copy(
            rows.at[pl.ds(start, block_rows)], sent_ref.at[slot], sems.at[slot]
        )
        copy.start()
        copies.append(copy)
    for copy in copies:
        copy.wait()


def outgoing(send_block, key_rows, value_rows, block_rows):
    nodes, width = key_rows.shape
    slots = send_block.shape[0]
    return pl.pallas_call(
        gather_kernel,
        grid_spec=pltpu.PrefetchScalarGridSpec(
            num_scalar_prefetch=1,
            grid=(1,),
            in_specs=[whole((nodes, width)), whole((nodes, width))],
            out_specs=[pl.BlockSpec(memory_space=pl.ANY), whole((nodes, 2 * width))],
            scratch_shapes=[
                pltpu.SemaphoreType.DMA((slots,)),
            ],
        ),
        out_shape=[
            jax.ShapeDtypeStruct((slots, block_rows, 2 * width), BF16),
            jax.ShapeDtypeStruct((nodes, 2 * width), BF16),
        ],
        compiler_params=params(),
        cost_estimate=cost(GATHER, 1 << 10),
        name="gather_out",
    )(send_block, key_rows, value_rows)


def prepare_kernel(query_ref, grad_ref, weight_ref, match_ref, attended_ref, *placed):
    nodes, width = query_ref.shape
    grads = dot(grad_ref[...], weight_ref[...], ROWS_ACROSS).astype(BF16)
    attended_ref[...] = grads
    both = jnp.concatenate([query_ref[...], grads], axis=1)
    target = lax.broadcasted_iota(jnp.int32, (nodes, nodes), 0)
    for turn, placed_ref in enumerate(placed):
        chosen = (target == match_ref[turn : turn + 1, :]).astype(F32).astype(BF16)
        placed_ref[...] = dot(chosen, both).astype(BF16)


def prepare(query_rows, grad_update, out_weight, matching):
    nodes, width = query_rows.shape
    turns = matching.shape[0]
    return pl.pallas_call(
        prepare_kernel,
        grid=(1,),
        in_specs=[
            whole((nodes, width)),
            whole((nodes, width)),
            whole((width, width)),
            whole((turns, nodes)),
        ],
        out_specs=[whole((nodes, width))] + [whole((nodes, 2 * width))] * turns,
        out_shape=[jax.ShapeDtypeStruct((nodes, width), BF16)]
        + [jax.ShapeDtypeStruct((nodes, 2 * width), BF16)] * turns,
        compiler_params=params(),
        cost_estimate=cost(1150 * 10**6, 1 << 10),
        name="prepare",
    )(query_rows, grad_update, out_weight, matching)


def head_rows(lanes, heads, per):
    return jnp.concatenate([lanes[:, h * per : (h + 1) * per] for h in range(heads)], axis=0)


def head_lanes(stacked, heads, dim):
    return jnp.concatenate(
        [
            jnp.sum(stacked[h * dim : (h + 1) * dim], axis=0, keepdims=True)
            for h in range(heads)
        ],
        axis=1,
    )


def spread(lanes, heads, dim, per):
    return jnp.concatenate(
        [
            jnp.broadcast_to(lanes[:, h * per : (h + 1) * per], (dim, per))
            for h in range(heads)
        ],
        axis=0,
    )


def diagonal(product, heads, dim, per):
    return jnp.concatenate(
        [
            product[h * dim : (h + 1) * dim, h * per : (h + 1) * per]
            for h in range(heads)
        ],
        axis=0,
    )


def masked_heads(rows, heads, dim):
    lane = lax.broadcasted_iota(jnp.int32, rows.shape, 1) // dim
    wide = rows.astype(F32)
    return jnp.concatenate(
        [jnp.where(lane == h, wide, 0.0) for h in range(heads)], axis=0
    ).astype(BF16)


def fill_table(table, key_ref, value_ref, halo_ref, sem):
    blocks = table.shape[0] - halo_ref.shape[0]
    per, width = table.shape[1], key_ref.shape[1]
    copy = pltpu.make_async_copy(halo_ref, table.at[pl.ds(blocks, halo_ref.shape[0])], sem)
    copy.start()
    for block in range(blocks):
        table[block, :, :width] = key_ref[block * per : (block + 1) * per, :]
        table[block, :, width:] = value_ref[block * per : (block + 1) * per, :]
    return copy


def live(values, start, rows):
    if start + values.shape[0] <= 5 * values.shape[1] // 4:
        return values
    row = lax.broadcasted_iota(jnp.int32, values.shape, 0) + start
    return jnp.where(row < rows, values, -jnp.inf)


def forward_kernel(
    heads, dim, tile_block, tile_count, key_ref, value_ref, halo_ref, query_ref,
    stats_out, mixed_out, table, picked, scores, raised, sem,
):
    blocks, slots = tile_count.shape[0], tile_block.shape[0] // tile_count.shape[0]
    nodes, features = query_ref.shape
    per = nodes // blocks
    width = heads * dim
    scale2 = dim**-0.5 * LOG2E
    span = slots // 2 * per
    parts = [slice(0, span), slice(span, 2 * span)]
    fill_table(table, key_ref, value_ref, halo_ref, sem).wait()

    def block_step(step, _):
        buffer = 0
        at = pl.ds(pl.multiple_of(step * per, per), per)
        for slot in range(slots):
            picked[buffer, slot * per : (slot + 1) * per, :] = table[tile_block[step * slots + slot]]
        live_rows = tile_count[step] * per
        for half in range(2):
            unit = step * 2 + half
            place = half
            keys = slice(half * width, (half + 1) * width)
            values = slice(features + half * width, features + (half + 1) * width)
            query_masked = masked_heads(query_ref[at, keys], heads, dim)
            top = None
            for part in parts:
                block = dot(picked[buffer, part, keys], query_masked, ROWS_ACROSS)
                block = live(block, part.start, live_rows)
                scores[place, part, :] = block
                part_top = jnp.max(block.reshape(span // 8, 8, heads * per), axis=0)
                top = part_top if top is None else jnp.maximum(top, part_top)
            top = jnp.max(top, axis=0, keepdims=True) * scale2
            total = jnp.zeros((8, heads * per), F32)
            for part in parts:
                block = jnp.exp2(scores[place, part, :] * scale2 - top)
                raised[place, part, :] = block.astype(BF16)
                total = total + jnp.sum(block.reshape(span // 8, 8, heads * per), axis=0)
            total = jnp.sum(total, axis=0, keepdims=True)
            mixed = dot(picked[buffer, :, values], raised[place], ROWS_DOWN)
            mixed_out[unit] = diagonal(mixed, heads, dim, per)
            stats_out[unit] = jnp.concatenate(
                [top, total, jnp.zeros((6, heads * per), F32)], axis=0
            )
        return 0

    lax.fori_loop(0, blocks, block_step, 0)


def merge_kernel(
    heads, dim, bias_ref, group_ref, below_1, above_1, below_2, above_2, below_4, above_4, match_ref,
    query_ref, grad_ref, update_grad_ref, out_weight, stats_ref, mixed_ref,
    update_out, weight_out, stats_out, query_grad_out, edge_out, weight_sum, far, sems,
):
    units = stats_ref.shape[0]
    blocks = units // 2
    nodes, features = query_ref.shape
    per = nodes // blocks
    width = heads * dim
    scale = dim**-0.5
    scale2 = scale * LOG2E
    lane_node = lax.broadcasted_iota(jnp.int32, (per, nodes), 1)
    place = group_ref[0]
    half_rows = nodes // 2

    def bring(turn, distance, below, above):
        below_is_partner = lax.rem(place // distance, 2) == 1

        @pl.when(below_is_partner)
        def _():
            pltpu.make_async_copy(below, far.at[turn], sems.at[turn]).start()

        @pl.when(jnp.logical_not(below_is_partner))
        def _():
            pltpu.make_async_copy(above, far.at[turn], sems.at[turn]).start()

    bring(2, 1, below_1, above_1)
    bring(1, 2, below_2, above_2)
    upper = pltpu.make_async_copy(below_4, far.at[0, pl.ds(0, half_rows)], sems.at[0])
    lower = pltpu.make_async_copy(above_4, far.at[0, pl.ds(half_rows, half_rows)], sems.at[3])
    upper.start()
    lower.start()
    weight_sum[...] = jnp.zeros_like(weight_sum)
    edge_out[...] = jnp.zeros_like(edge_out)
    for turn in (1, 2):
        pltpu.make_async_copy(below_1, far.at[turn], sems.at[turn]).wait()
    upper.wait()
    lower.wait()

    def block_step(step, _):
        at = pl.ds(pl.multiple_of(step * per, per), per)
        query_t = query_ref[at, :].astype(F32).T
        grad_t = grad_ref[at, :].astype(F32).T
        chosen, far_keys, far_values = [], [], []
        for turn in range(3):
            pick = (lane_node == match_ref[at, turn : turn + 1]).astype(F32).astype(BF16)
            chosen.append(pick)
            found = dot(pick, far[turn])
            far_keys.append(found[:, :features].T)
            far_values.append(found[:, features:].T)
        attended_t = []
        rows = [[], [], []]
        for half in range(2):
            unit = step * 2 + half
            of = slice(half * width, (half + 1) * width)
            bias = jnp.concatenate(
                [jnp.full((1, per), bias_ref[half * heads + h] * LOG2E, F32) for h in range(heads)],
                axis=1,
            )
            scores = [
                head_lanes(query_t[of] * far_keys[turn][of], heads, dim) * scale2 + bias
                for turn in range(3)
            ]
            tile_top, tile_total = stats_ref[unit, 0:1, :], stats_ref[unit, 1:2, :]
            top = jnp.maximum(jnp.maximum(tile_top, scores[0]), jnp.maximum(scores[1], scores[2]))
            shrink = jnp.exp2(tile_top - top)
            raised = [jnp.exp2(scores[turn] - top) for turn in range(3)]
            total = tile_total * shrink + (raised[0] + raised[1] + raised[2])
            inverse = 1.0 / total
            probs = [raised[turn] * inverse for turn in range(3)]
            weights = [probs[turn].astype(BF16).astype(F32) for turn in range(3)]
            mixed = mixed_ref[unit] * spread(shrink * inverse, heads, dim, per)
            for turn in range(3):
                mixed = mixed + spread(weights[turn], heads, dim, per) * far_values[turn][of]
            attended = mixed.astype(BF16)
            attended_t.append(attended)
            delta = head_lanes(grad_t[of] * attended.astype(F32), heads, dim)
            stats_out[unit] = jnp.concatenate(
                [top + jnp.log2(total), delta, jnp.zeros((6, heads * per), F32)], axis=0
            )
            query_grad = jnp.zeros((width, per), F32)
            for turn in range(3):
                grad_prob = head_lanes(grad_t[of] * far_values[turn][of], heads, dim)
                dscore = (probs[turn] * (grad_prob - delta) * scale).astype(BF16).astype(F32)
                query_grad = query_grad + spread(dscore, heads, dim, per) * far_keys[turn][of]
                rows[turn] += [head_rows(dscore, heads, per), head_rows(weights[turn], heads, per)]
            query_grad_out[unit] = query_grad
        both = jnp.concatenate(attended_t, axis=0)
        update_out[at, :] = dot(both, out_weight[...], ROWS_DOWN).astype(BF16)
        product = dot(both, update_grad_ref[at, :])
        weight_sum[...] += product
        for turn in range(3):
            edge_out[turn] += dot(jnp.concatenate(rows[turn], axis=0).astype(BF16), chosen[turn])
        return 0

    lax.fori_loop(0, blocks, block_step, 0)
    for piece in range(weight_out.shape[0]):
        rows_each = weight_out.shape[1]
        weight_out[piece] = weight_sum[piece * rows_each : (piece + 1) * rows_each, :].astype(BF16)


def backward_kernel(
    heads, dim, tile_block, tile_count, key_ref, value_ref, halo_ref, query_ref, grad_ref,
    stats_ref, edge_ref, returned_ref, own_terms_ref, query_out,
    table, picked, weights, dscores, terms, sem,
):
    blocks, slots = tile_count.shape[0], tile_block.shape[0] // tile_count.shape[0]
    nodes, features = query_ref.shape
    per = nodes // blocks
    width = heads * dim
    scale = dim**-0.5
    scale2 = scale * LOG2E
    span = slots // 2 * per
    parts = [slice(0, span), slice(span, 2 * span)]
    halo_copy = fill_table(table, key_ref, value_ref, halo_ref, sem)
    terms[...] = jnp.zeros_like(terms)
    returned_ref[:, per:, :] = jnp.zeros_like(returned_ref[:, per:, :])
    halo_copy.wait()

    def block_step(step, _):
        buffer = 0
        at = pl.ds(pl.multiple_of(step * per, per), per)
        entries = [tile_block[step * slots + slot] for slot in range(slots)]
        for slot in range(slots):
            picked[buffer, slot * per : (slot + 1) * per, :] = table[entries[slot]]
        live_rows = tile_count[step] * per
        for half in range(2):
            unit = step * 2 + half
            place = half
            keys = slice(half * width, (half + 1) * width)
            values = slice(features + half * width, features + (half + 1) * width)
            query_masked = masked_heads(query_ref[at, keys], heads, dim)
            grad_masked = masked_heads(grad_ref[at, keys], heads, dim)
            log_total, delta = stats_ref[unit, 0:1, :], stats_ref[unit, 1:2, :]
            for part in parts:
                block = dot(picked[buffer, part, keys], query_masked, ROWS_ACROSS)
                block = live(block, part.start, live_rows)
                prob = jnp.exp2(block * scale2 - log_total)
                weights[place, part, :] = prob.astype(BF16)
                grad_prob = dot(picked[buffer, part, values], grad_masked, ROWS_ACROSS)
                dscores[place, part, :] = (prob * scale * (grad_prob - delta)).astype(BF16)
            query_grad = dot(picked[buffer, :, keys], dscores[place], ROWS_DOWN)
            query_grad = diagonal(query_grad, heads, dim, per) + edge_ref[unit]
            query_out[at, keys] = query_grad.T
            key_terms = dot(dscores[place], query_masked)
            value_terms = dot(weights[place], grad_masked)
            for slot in range(slots):
                rows = slice(slot * per, (slot + 1) * per)
                terms[entries[slot], :, keys] += key_terms[rows]
                terms[entries[slot], :, values] += value_terms[rows]
        return 0

    lax.fori_loop(0, blocks, block_step, 0)
    own_terms_ref[...] = terms[:blocks]
    returned_ref[:, :per, :] = terms[blocks:].astype(BF16)


def run(kernel, scalars, ins, outs, scratch, estimate, name):
    specs = [whole(array.shape) if spec is None else spec for array, spec in ins]
    return pl.pallas_call(
        kernel,
        grid_spec=pltpu.PrefetchScalarGridSpec(
            num_scalar_prefetch=len(scalars),
            grid=(1,),
            in_specs=specs,
            out_specs=[whole(shape) for shape, _ in outs],
            scratch_shapes=scratch,
        ),
        out_shape=[jax.ShapeDtypeStruct(shape, dtype) for shape, dtype in outs],
        compiler_params=params(),
        cost_estimate=cost(estimate, 1 << 10),
        name=name,
    )(*scalars, *(array for array, _ in ins))


ANYWHERE = pl.BlockSpec(memory_space=pl.ANY)


def forward(scalars, key_rows, value_rows, halo, query_rows, heads):
    tile_block, tile_count = scalars
    nodes, features = query_rows.shape
    blocks, slots = tile_count.shape[0], tile_block.shape[0] // tile_count.shape[0]
    per, width = nodes // blocks, features // 2
    columns = heads // 2 * per
    return run(
        functools.partial(forward_kernel, heads // 2, features // heads),
        scalars,
        [(key_rows, None), (value_rows, None), (halo, ANYWHERE), (query_rows, None)],
        [((2 * blocks, 8, columns), F32), ((2 * blocks, width, per), F32)],
        [
            pltpu.VMEM((blocks + halo.shape[0], per, 2 * features), BF16),
            pltpu.VMEM((1, slots * per, 2 * features), BF16),
            pltpu.VMEM((BUFFERS, slots * per, columns), F32),
            pltpu.VMEM((BUFFERS, slots * per, columns), BF16),
            pltpu.SemaphoreType.DMA,
        ],
        FORWARD,
        "forward",
    )


def merge(bias, group, far, match_columns, query_rows, attended_grad, grad_update, out_weight, stats, mixed):
    nodes, features = query_rows.shape
    heads = bias.shape[0]
    arrays = [match_columns, query_rows, attended_grad, grad_update, out_weight, stats, mixed]
    return run(
        functools.partial(merge_kernel, heads // 2, features // heads),
        (bias, group),
        [(array, ANYWHERE) for array in far] + [(array, None) for array in arrays],
        [
            ((nodes, features), BF16),
            ((8, features // 8, features), BF16),
            (stats.shape, F32),
            (mixed.shape, F32),
            ((3, 2 * heads, nodes), F32),
        ],
        [
            pltpu.VMEM((features, features), F32),
            pltpu.VMEM((3, nodes, 2 * features), BF16),
            pltpu.SemaphoreType.DMA((4,)),
        ],
        MERGE,
        "merge",
    )


def backward(scalars, key_rows, value_rows, halo, query_rows, attended_grad, stats, edge_part, spare, heads):
    tile_block, tile_count = scalars
    nodes, features = query_rows.shape
    blocks, slots = tile_count.shape[0], tile_block.shape[0] // tile_count.shape[0]
    per = nodes // blocks
    columns = heads // 2 * per
    count = halo.shape[0]
    return run(
        functools.partial(backward_kernel, heads // 2, features // heads),
        scalars,
        [(key_rows, None), (value_rows, None), (halo, ANYWHERE), (query_rows, None)]
        + [(attended_grad, None), (stats, None), (edge_part, None)],
        [
            ((count, per + spare, 2 * features), BF16),
            ((blocks, per, 2 * features), F32),
            ((nodes, features), F32),
        ],
        [
            pltpu.VMEM((blocks + count, per, 2 * features), BF16),
            pltpu.VMEM((1, slots * per, 2 * features), BF16),
            pltpu.VMEM((BUFFERS, slots * per, columns), BF16),
            pltpu.VMEM((BUFFERS, slots * per, columns), BF16),
            pltpu.VMEM((blocks + count, per, 2 * features), F32),
            pltpu.SemaphoreType.DMA,
        ],
        BACKWARD,
        "backward",
    )


def collect_kernel(heads, own_ref, *refs):
    placed, edges = refs[:3], refs[3:6]
    key_ref, value_ref = refs[6:]
    blocks, per, both = own_ref.shape
    two = both // 2
    width = two // 2
    dim = width // heads
    for block in range(blocks):
        key_ref[block * per : (block + 1) * per, :] = own_ref[block, :, :two]
        value_ref[block * per : (block + 1) * per, :] = own_ref[block, :, two:]
    row = lax.broadcasted_iota(jnp.int32, (4 * heads, two), 0)
    lane = lax.broadcasted_iota(jnp.int32, (4 * heads, two), 1)
    key_row = (lane // width) * (2 * heads) + lax.rem(lane, width) // dim
    key_spread = (row == key_row).astype(F32).astype(BF16)
    value_spread = (row == key_row + heads).astype(F32).astype(BF16)
    for turn in range(3):
        scalars = edges[turn][...].astype(BF16)
        dscore = dot(scalars, key_spread, ROWS_DOWN)
        weight = dot(scalars, value_spread, ROWS_DOWN)
        key_term = dscore * placed[turn][:, :two].astype(F32)
        value_term = weight * placed[turn][:, two:].astype(F32)
        key_ref[...] += key_term.astype(BF16).astype(F32)
        value_ref[...] += value_term.astype(BF16).astype(F32)


def collect(own, placed, edges, heads):
    blocks, per, both = own.shape
    out = ((blocks * per, both // 2), F32)
    arrays = [own, *placed, *edges]
    return run(
        functools.partial(collect_kernel, heads // 2),
        (),
        [(array, None) for array in arrays],
        [out, out],
        [],
        COLLECT,
        "collect",
    )


def finish_kernel(send_block, home_ref, key_in, value_in, key_ref, value_ref):
    slots, _, both = home_ref.shape
    two = both // 2
    per = home_ref.shape[1]
    key_ref[...] = key_in[...]
    value_ref[...] = value_in[...]
    for slot in range(slots):
        start = pl.multiple_of(send_block[slot] * per, per)
        key_ref[pl.ds(start, per), :] += home_ref[slot, :, :two].astype(F32)
        value_ref[pl.ds(start, per), :] += home_ref[slot, :, two:].astype(F32)


def finish(send_block, home, key_sum, value_sum, per):
    slots, _, both = home.shape
    out = (key_sum.shape, F32)
    part = pl.BlockSpec((slots, per, both), lambda *_: (0, 0, 0), pipeline_mode=pl.Buffered(1))
    return run(
        finish_kernel,
        (send_block,),
        [(home, part), (key_sum, None), (value_sum, None)],
        [out, out],
        [],
        FINISH,
        "finish",
    )


def from_partner(array, apart):
    axes = ("group", "dom")
    return lax.ppermute(array, axes, [(i, i ^ 1 << apart) for i in range(lax.axis_size(axes))])


def ahead(array, steps):
    count = lax.axis_size("group")
    return lax.ppermute(array, "group", [(i, (i + steps) % count) for i in range(count)])


def exchange(array, axis):
    return lax.all_to_all(array, axis, split_axis=0, concat_axis=0, tiled=True)


def shards(
    query_rows,
    key_rows,
    value_rows,
    out_weight,
    grad_update,
    expander_bias,
    tile_block,
    tile_count,
    send_block,
    matching,
):
    nodes, features = query_rows.shape
    heads = expander_bias.shape[0]
    tile_block = tile_block[0]
    tile_count = tile_count[0]
    send_block = send_block[0]
    matching = matching[0]
    per = nodes // tile_block.shape[0]
    devices = lax.axis_size(("group", "dom"))
    top_bit = devices.bit_length() - 1
    groups = lax.axis_size("group")

    sent, own_rows = outgoing(send_block, key_rows, value_rows, per)
    halo = exchange(sent, "dom")
    below_1, above_1 = ahead(own_rows, 1), ahead(own_rows, -1)
    attended_grad, *placed = prepare(query_rows, grad_update, out_weight, matching)
    below_1, above_1, attended_grad = lax.optimization_barrier((below_1, above_1, attended_grad))
    below_2, above_2 = ahead(below_1, 1), ahead(above_1, -1)
    below_4 = ahead(ahead(below_2[: nodes // 2], 1), 1)
    above_4 = ahead(ahead(above_2[nodes // 2 :], -1), -1)
    far = [below_1, above_1, below_2, above_2, below_4, above_4]
    group = lax.axis_index("group").astype(jnp.int32).reshape(1)
    placed = [from_partner(placed[turn], top_bit - 1 - turn) for turn in range(3)]

    scalars = (tile_block.reshape(-1), tile_count)
    stats, mixed = forward(scalars, key_rows, value_rows, halo, query_rows, heads)
    update, pieces, stats, edge_part, edges = merge(
        expander_bias, group, far, matching.T, query_rows, attended_grad, grad_update, out_weight, stats, mixed
    )
    edges = [from_partner(edges[turn], top_bit - 1 - turn) for turn in range(3)]
    pieces = exchange(pieces, "group")
    spare = features // 8 // 2
    back, own, query_grad = backward(
        scalars, key_rows, value_rows, halo, query_rows, attended_grad, stats, edge_part, spare, heads
    )
    part = pieces.astype(F32).sum(axis=0).astype(BF16)
    part = jnp.concatenate([part[:spare], part[spare:]], axis=1)
    back = back.at[:, per:, :].set(part[None])
    back, placed[1], placed[2] = lax.optimization_barrier((back, placed[1], placed[2]))
    home = exchange(back, "dom")
    key_sum, value_sum = collect(own, placed, edges, heads)
    home, key_sum, value_sum = lax.optimization_barrier((home, key_sum, value_sum))
    key_grad, value_grad = finish(send_block, home, key_sum, value_sum, per)

    summed = home[:, per:, :].astype(F32).sum(axis=0) * (nodes * devices) ** (-0.5)
    summed = jnp.concatenate([summed[:, :features], summed[:, features:]], axis=0)
    copies = jnp.broadcast_to(summed[None], (groups,) + summed.shape)
    weight_grad = exchange(copies, "group").reshape(features, features)
    return (update, query_grad, key_grad, value_grad, weight_grad)


def solution(mesh):
    rows = P(("group", "dom"), None)
    in_specs = (
        rows,
        rows,
        rows,
        P(),
        rows,
        P(),
        P(("group", "dom"), None, None),
        rows,
        rows,
        P(("group", "dom"), None, None),
    )
    out_specs = (rows, rows, rows, rows, P())
    return jax.shard_map(shards, mesh=mesh, in_specs=in_specs, out_specs=out_specs, check_vma=False)
```

time: 832 us -> 231 us (0.28); the launches traced: 817 us -> 230 us
  local copies, waits for them, and re-layouts: 221 us -> 5.78 us
  waiting for transfers between devices: 262 us -> 93.1 us
  other arithmetic: 132 us -> 1.19 us
  matrix products: 126 us -> 0 us
  Pallas kernels: 0 us -> 73.1 us
  between operations: 14.9 us -> 0.93 us
    psum x1 -> x0, waiting for transfers between devices: 194 us -> none  [shards(): lax.psum(weight_term, ('group', 'dom')) * (node_count * devices) ** (-0.5)]
    gather x94 -> x0, local copies, waits for them, and re-layouts: 135 us -> none  [the longest x80 105 us: pick_blocks(): return table[tile_block[:, slot_index]].reshape(template.shape)]
    dot_general x59 -> x0, matrix products: 126 us -> none  [the longest x16 33.7 us: tile_scores(): jnp.einsum('bqhd,bkhd->bqhk', query_heads, picked_keys, preferred_element...]
    pallas_call x0 -> x7, Pallas kernels: none -> 73.1 us  [the longest x5 63.9 us: run(): pl.pallas_call(kernel, grid_spec=pltpu.PrefetchScalarGridSpec(num_scalar_...]
    scatter-add x18 -> x0, other arithmetic: 62.5 us -> none  [the longest x8 24.8 us: backward_slot(): value_table.at[targets]]
    scatter x6 -> x1, local copies, waits for them, and re-layouts: 39.3 us -> 0.88 us  [shards(): back = back.at[:, per:, :].set(part[None])]
    ppermute x12 -> x14, waiting for transfers between devices: 49.6 us -> 73.1 us  [the longest x8 39.3 us: ahead(): lax.ppermute(array, 'group', [(i, (i + steps) % count) for i in range(cou...]
    select_n x26 -> x0, other arithmetic: 17.2 us -> none  [the longest x24 16.4 us: pick_blocks(): return table[tile_block[:, slot_index]].reshape(template.shape)]
  transfers between devices with their start and end apart: 17 -> 18, of which waited for: 5 -> 9; matrix products, arithmetic and copies ran while one was open for 25% -> 1% of each run, Pallas kernels for 0% -> 30%
where the time goes in v1:
time: 231 us; the launch traced here: 230 us
  waiting for transfers between devices  93.1 us (40%)
  Pallas kernels  73.1 us (32%)
  starting transfers between devices  56.1 us (24%)
  local copies, waits for them, and re-layouts  5.78 us (3%)
    pallas_call x5, Pallas kernels, run(): pl.pallas_call(kernel, grid_spec=pltpu.PrefetchScalarGridSpec(num_scalar_...  63.9 us
    ppermute x8, waiting for transfers between devices, ahead(): lax.ppermute(array, 'group', [(i, (i + steps) % count) for i in range(cou...  39.3 us
    ppermute x6, waiting for transfers between devices, from_partner(): lax.ppermute(array, axes, [(i, i ^ 1 << apart) for i in range(lax.axis_si...  33.8 us
    all_to_all x4, starting transfers between devices, exchange(): return lax.all_to_all(array, axis, split_axis=0, concat_axis=0, tiled=True)  29.6 us
    all_to_all x4, waiting for transfers between devices, exchange(): return lax.all_to_all(array, axis, split_axis=0, concat_axis=0, tiled=True)  20.1 us
    ppermute x8, starting transfers between devices, ahead(): lax.ppermute(array, 'group', [(i, (i + steps) % count) for i in range(cou...  15.8 us
    ppermute x6, starting transfers between devices, from_partner(): lax.ppermute(array, axes, [(i, i ^ 1 << apart) for i in range(lax.axis_si...  10.8 us
    pallas_call x1, Pallas kernels, outgoing(): pl.pallas_call(gather_kernel, grid_spec=pltpu.PrefetchScalarGridSpec(num_...  5.02 us
  transfers between devices with their start and end apart: 18, of which 9 were waited for; matrix products, arithmetic and copies ran while one was open for 1% of the time, Pallas kernels for 30%

profile of v1, /device:TPU:8, one launch (start us, length us, event | category | flops | bytes accessed | tf_op | source)
XLA Modules:
  0.0 230.2 jit_solution(18331634595615456834)
XLA Ops:
  0.6 5.0 %gather_out.1 = (bf16[32,128,512]{2,1,0:T(8,128)(2,1)}, bf16[768,512]{1,0:T(8,128)(2,1)}) custom-call(s32[32]{0:T(128)} %bitcast.16, bf16[768,256]{1,0:T(8,128)(2,1)} %key_ref.5, bf16[768,256]{1,0:T(8,128)(2,1)} %value_ref.5), custom_call_target="tpu_custom_call" | custom-call | flops 575000000 | bytes 1024 | tf_op jit(solution)/shard_map/gather_out/pallas_call | solution.py:57
  5.7 7.7 %all-to-all-start = ((bf16[32,128,512]{2,1,0:T(8,128)(2,1)}), bf16[32,128,512]{2,1,0:T(8,128)(2,1)}, u32[]{:S(2)}, u32[]{:S(2)}) async-start(bf16[32,128,512]{2,1,0:T(8,128)(2,1)} %get-tuple-element.51), calls=%async_computation | async-start | bytes 8388608 | tf_op jit(solution)/shard_map/all_to_all | solution.py:554
  13.4 5.9 %collective-permute-start.1 = (bf16[768,512]{1,0:T(8,128)(2,1)S(1)}, bf16[768,512]{1,0:T(8,128)(2,1)S(1)}, u32[]{:S(2)}, u32[]{:S(2)}) collective-permute-start(bf16[768,512]{1,0:T(8,128)(2,1)S(1)} %copy-done.12), channel_id=1, source_target_pairs={{0,224},{32,0},{64,32},{96,64},{128,96},{160,128},{192,160},{224,1... | collective-permute-start | bytes 2359304 | tf_op jit(solution)/shard_map/ppermute | solution.py:550
  19.6 0.8 copy.16.match_ref
  20.3 4.1 %prepare.1 = (bf16[768,256]{1,0:T(8,128)(2,1)}, bf16[768,512]{1,0:T(8,128)(2,1)}, bf16[768,512]{1,0:T(8,128)(2,1)}, bf16[768,512]{1,0:T(8,128)(2,1)}) custom-call(bf16[768,256]{1,0:T(8,128)(2,1)} %query_ref.7, bf16[768,256]{1,0:T(8,128)(2,1)} %update_grad_ref.1, bf16[256,256]{1,0:T(8,128)(2,1)} %out_weight.1, s32[3,768]{1,0:T(4,128)} %copy.16.match_ref), custom_call_target="tpu_custom_call" | custom-call | flops 1150000000 | bytes 1024 | tf_op jit(solution)/shard_map/prepare/pallas_call | solution.py:92
  24.5 12.0 %collective-permute-done.1.above_1 = bf16[768,512]{1,0:T(8,128)(2,1)S(1)} collective-permute-done((bf16[768,512]{1,0:T(8,128)(2,1)S(1)}, bf16[768,512]{1,0:T(8,128)(2,1)S(1)}, u32[]{:S(2)}, u32[]{:S(2)}) %collective-permute-start.1) | collective-permute-done | bytes 786464 | tf_op jit(solution)/shard_map/ppermute | solution.py:550
  36.5 3.4 %collective-permute-done.below_1 = bf16[768,512]{1,0:T(8,128)(2,1)S(1)} collective-permute-done((bf16[768,512]{1,0:T(8,128)(2,1)S(1)}, bf16[768,512]{1,0:T(8,128)(2,1)S(1)}, u32[]{:S(2)}, u32[]{:S(2)}) %collective-permute-start) | collective-permute-done | bytes 786464 | tf_op jit(solution)/shard_map/ppermute | solution.py:550
  39.9 3.2 %collective-permute-start.3 = (bf16[768,512]{1,0:T(8,128)(2,1)S(1)}, bf16[768,512]{1,0:T(8,128)(2,1)S(1)}, u32[]{:S(2)}, u32[]{:S(2)}) collective-permute-start(bf16[768,512]{1,0:T(8,128)(2,1)S(1)} %collective-permute-done.1.above_1), channel_id=1, source_target_pairs={{0,224},{32,0},{64,32},{96,64},{128,96},{160,128},{192,160},{224,1... | collective-permute-start | bytes 2359304 | tf_op jit(solution)/shard_map/ppermute | solution.py:550
  43.1 16.5 %collective-permute-done.2.below_2 = bf16[768,512]{1,0:T(8,128)(2,1)S(1)} collective-permute-done((bf16[768,512]{1,0:T(8,128)(2,1)S(1)}, bf16[768,512]{1,0:T(8,128)(2,1)S(1)}, u32[]{:S(2)}, u32[]{:S(2)}) %collective-permute-start.2) | collective-permute-done | bytes 786464 | tf_op jit(solution)/shard_map/ppermute | solution.py:550
  59.9 3.3 %collective-permute-start.6 = (bf16[384,512]{1,0:T(8,128)(2,1)S(1)}, bf16[384,512]{1,0:T(8,128)(2,1)}, u32[]{:S(2)}, u32[]{:S(2)}) collective-permute-start(bf16[384,512]{1,0:T(8,128)(2,1)S(1)} %slice.63), channel_id=1, source_target_pairs={{0,224},{32,0},{64,32},{96,64},{128,96},{160,128},{192,160},{224,1... | collective-permute-start | bytes 1179656 | tf_op jit(solution)/shard_map/ppermute | solution.py:550
  63.1 7.3 %collective-permute-done.4 = bf16[384,512]{1,0:T(8,128)(2,1)} collective-permute-done((bf16[384,512]{1,0:T(8,128)(2,1)S(1)}, bf16[384,512]{1,0:T(8,128)(2,1)}, u32[]{:S(2)}, u32[]{:S(2)}) %collective-permute-start.4) | collective-permute-done | bytes 393248 | tf_op jit(solution)/shard_map/ppermute | solution.py:550
  70.4 3.2 %collective-permute-start.7 = (bf16[384,512]{1,0:T(8,128)(2,1)}, bf16[384,512]{1,0:T(8,128)(2,1)}, u32[]{:S(2)}, u32[]{:S(2)}) collective-permute-start(bf16[384,512]{1,0:T(8,128)(2,1)} %collective-permute-done.6), channel_id=1, source_target_pairs={{0,224},{32,0},{64,32},{96,64},{128,96},{160,128},{192,160},{224,1... | collective-permute-start | bytes 1179656 | tf_op jit(solution)/shard_map/ppermute | solution.py:550
  74.0 0.7 reshape_squeeze.3.tile_block
  74.6 17.1 %forward.1 = (f32[12,8,512]{2,1,0:T(8,128)}, f32[12,128,128]{2,1,0:T(8,128)}) custom-call(s32[48]{0:T(128)} %reshape_squeeze.3.tile_block, s32[6]{0:T(128)} %bitcast.18, bf16[768,256]{1,0:T(8,128)(2,1)} %key_ref.5, bf16[768,256]{1,0:T(8,128)(2,1)} %value_ref.5, bf16[32,128,512]{2,1,0:T(8,128)(2,1)} %all-to-all-done.halo_ref, bf16[768,256]{1,0:T(8,128)(2,1)} %query_ref.7), custom_call_target="tpu_custom_call" | custom-call | flops 2300000000 | bytes 1024 | tf_op jit(solution)/shard_map/forward/pallas_call | solution.py:379
  91.9 11.5 %merge.1 = (bf16[768,256]{1,0:T(8,128)(2,1)}, bf16[8,32,256]{2,1,0:T(8,128)(2,1)}, f32[12,8,512]{2,1,0:T(8,128)}, f32[12,128,128]{2,1,0:T(8,128)}, f32[3,16,768]{2,1,0:T(8,128)}) custom-call(f32[8]{0:T(128)} %bias_ref.1, s32[1]{0:T(128)} %bitcast.group_ref, bf16[768,512]{1,0:T(8,128)(2,1)} %copy-done.10, bf16[768,512]{1,0:T(8,128)(2,1)} %copy-done.9, ...), custom_call_target="tpu_custom_call" | custom-call | flops 2300000000 | bytes 1024 | tf_op jit(solution)/shard_map/merge/pallas_call | solution.py:379
  103.4 7.5 %all-to-all-start.1 = ((bf16[8,32,256]{2,1,0:T(8,128)(2,1)}), bf16[8,32,256]{2,1,0:T(8,128)(2,1)S(1)}, u32[]{:S(2)}, u32[]{:S(2)}) async-start(bf16[8,32,256]{2,1,0:T(8,128)(2,1)} %get-tuple-element.59), calls=%async_computation.1 | async-start | bytes 262144 | tf_op jit(solution)/shard_map/all_to_all | solution.py:554
  110.8 25.9 %backward.1 = (bf16[32,144,512]{2,1,0:T(8,128)(2,1)}, f32[6,128,512]{2,1,0:T(8,128)}, f32[768,256]{1,0:T(8,128)}) custom-call(s32[48]{0:T(128)} %reshape_squeeze.3.tile_block, s32[6]{0:T(128)} %bitcast.19, bf16[768,256]{1,0:T(8,128)(2,1)} %key_ref.5, bf16[768,256]{1,0:T(8,128)(2,1)} %value_ref.5, bf16[32,128,512]{2,1,0:T(8,128)(2,1)} %all-to-all-done.halo_ref, ...), custom_call_target="tpu_custom_call" | custom-call | flops 16099999744 | bytes 1024 | tf_op jit(solution)/shard_map/backward/pallas_call | solution.py:379
  136.8 0.9 broadcast_dynamic-update-slice_fusion
  137.7 0.9 copy-done.7
  138.8 7.2 %all-to-all-start.2 = ((bf16[32,144,512]{2,1,0:T(8,128)(2,1)}), bf16[32,144,512]{2,1,0:T(8,128)(2,1)}, u32[]{:S(2)}, u32[]{:S(2)}) async-start(bf16[32,144,512]{2,1,0:T(8,128)(2,1)} %broadcast_dynamic-update-slice_fusion), calls=%async_computation.2 | async-start | bytes 9437184 | tf_op jit(solution)/shard_map/all_to_all | solution.py:554
  146.1 6.0 %collective-permute-start.10 = (bf16[768,512]{1,0:T(8,128)(2,1)S(1)}, bf16[768,512]{1,0:T(8,128)(2,1)S(1)}, u32[]{:S(2)}, u32[]{:S(2)}) collective-permute-start(bf16[768,512]{1,0:T(8,128)(2,1)S(1)} %copy-done.6), channel_id=1, source_target_pairs={{0,128},{1,129},{2,130},{3,131},{4,132},{5,133},{6,134},{7,135},{8... | collective-permute-start | bytes 2359304 | tf_op jit(solution)/shard_map/ppermute | solution.py:545
  153.3 3.3 %collective-permute-start.11 = (f32[16,768]{1,0:T(8,128)S(1)}, f32[16,768]{1,0:T(8,128)S(1)}, u32[]{:S(2)}, u32[]{:S(2)}) collective-permute-start(f32[16,768]{1,0:T(8,128)S(1)} %get-tuple-element.77), channel_id=1, source_target_pairs={{0,128},{1,129},{2,130},{3,131},{4,132},{5,133},{6,134},{7,135},{8... | collective-permute-start | bytes 147464 | tf_op jit(solution)/shard_map/ppermute | solution.py:545
  156.6 23.8 %collective-permute-done.10.refs_0_ = bf16[768,512]{1,0:T(8,128)(2,1)S(1)} collective-permute-done((bf16[768,512]{1,0:T(8,128)(2,1)S(1)}, bf16[768,512]{1,0:T(8,128)(2,1)S(1)}, u32[]{:S(2)}, u32[]{:S(2)}) %collective-permute-start.10) | collective-permute-done | bytes 786464 | tf_op jit(solution)/shard_map/ppermute | solution.py:545
  180.3 9.9 %collective-permute-done.13.refs_5_ = f32[16,768]{1,0:T(8,128)S(1)} collective-permute-done((f32[16,768]{1,0:T(8,128)S(1)}, f32[16,768]{1,0:T(8,128)S(1)}, u32[]{:S(2)}, u32[]{:S(2)}) %collective-permute-start.13) | collective-permute-done | bytes 49184 | tf_op jit(solution)/shard_map/ppermute | solution.py:545
  191.0 4.2 %collect.1 = (f32[768,256]{1,0:T(8,128)}, f32[768,256]{1,0:T(8,128)}) custom-call(f32[6,128,512]{2,1,0:T(8,128)} %get-tuple-element.63.own_ref, bf16[768,512]{1,0:T(8,128)(2,1)} %copy-done.11, bf16[768,512]{1,0:T(8,128)(2,1)} %copy-done.7, bf16[768,512]{1,0:T(8,128)(2,1)} %copy-done.8, f32[16,768]{1,0:T(8,128)} %copy-done.15, f32[16,768]{1,0:T(8,128)} %copy-done.14, ...), custom_call_target="tpu_custom_call" | custom-call | flops 1150000000 | bytes 1024 | tf_op jit(solution)/shard_map/collect/pallas_call | solution.py:379
  195.2 13.6 %all-to-all-done.2.home_ref = bf16[32,144,512]{2,1,0:T(8,128)(2,1)} async-done(((bf16[32,144,512]{2,1,0:T(8,128)(2,1)}), bf16[32,144,512]{2,1,0:T(8,128)(2,1)}, u32[]{:S(2)}, u32[]{:S(2)}) %all-to-all-start.2) | async-done | bytes 4718624 | tf_op jit(solution)/shard_map/all_to_all | solution.py:554
  208.7 1.1 convert_reduce_fusion
  209.9 0.7 broadcast_in_dim.2
  210.6 7.2 %all-to-all-start.3 = ((f32[8,32,256]{2,1,0:T(8,128)}), f32[8,32,256]{2,1,0:T(8,128)S(1)}, u32[]{:S(2)}, u32[]{:S(2)}) async-start(f32[8,32,256]{2,1,0:T(8,128)} %broadcast_in_dim.2), calls=%async_computation.3 | async-start | bytes 524288 | tf_op jit(solution)/shard_map/all_to_all | solution.py:554
  217.8 5.2 %finish.1 = (f32[768,256]{1,0:T(8,128)}, f32[768,256]{1,0:T(8,128)}) custom-call(s32[32]{0:T(128)} %bitcast.17, bf16[32,144,512]{2,1,0:T(8,128)(2,1)} %all-to-all-done.2.home_ref, f32[768,256]{1,0:T(8,128)} %get-tuple-element.71.key_in, f32[768,256]{1,0:T(8,128)} %get-tuple-element.72.value_in), custom_call_target="tpu_custom_call" | custom-call | flops 1150000000 | bytes 1024 | tf_op jit(solution)/shard_map/finish/pallas_call | solution.py:379
  223.1 6.5 %all-to-all-done.3 = f32[8,32,256]{2,1,0:T(8,128)S(1)} async-done(((f32[8,32,256]{2,1,0:T(8,128)}), f32[8,32,256]{2,1,0:T(8,128)S(1)}, u32[]{:S(2)}, u32[]{:S(2)}) %all-to-all-start.3) | async-done | bytes 262176 | tf_op jit(solution)/shard_map/all_to_all | solution.py:554
  229.5 0.7 copy.19
  (60 shorter events, 3.0 us)
Async XLA Ops:
  5.7 7.8 %copy-start.12 = (bf16[768,512]{1,0:T(8,128)(2,1)S(1)}, bf16[768,512]{1,0:T(8,128)(2,1)}, u32[]{:S(2)}) copy-start(bf16[768,512]{1,0:T(8,128)(2,1)} %get-tuple-element.46) | copy-start | bytes 2359300
  5.7 13.7 %copy-start.4 = (s32[1,3,768]{2,0,1:T(1,128)S(1)}, s32[1,3,768]{2,0,1:T(1,128)}, u32[]{:S(2)}) copy-start(s32[1,3,768]{2,0,1:T(1,128)} %param.21) | copy-start | bytes 27652
  5.7 69.0 %all-to-all-start = ((bf16[32,128,512]{2,1,0:T(8,128)(2,1)}), bf16[32,128,512]{2,1,0:T(8,128)(2,1)}, u32[]{:S(2)}, u32[]{:S(2)}) async-start(bf16[32,128,512]{2,1,0:T(8,128)(2,1)} %get-tuple-element.51), calls=%async_computation | async-start | bytes 8388608 | tf_op jit(solution)/shard_map/all_to_all | solution.py:554
  13.4 60.5 %copy-start.5 = (s32[1,6,8]{2,0,1:T(1,128)S(1)}, s32[1,6,8]{2,0,1:T(1,128)}, u32[]{:S(2)}) copy-start(s32[1,6,8]{2,0,1:T(1,128)} %param.18) | copy-start | bytes 580
  13.4 23.0 %collective-permute-start.1 = (bf16[768,512]{1,0:T(8,128)(2,1)S(1)}, bf16[768,512]{1,0:T(8,128)(2,1)S(1)}, u32[]{:S(2)}, u32[]{:S(2)}) collective-permute-start(bf16[768,512]{1,0:T(8,128)(2,1)S(1)} %copy-done.12), channel_id=1, source_target_pairs={{0,224},{32,0},{64,32},{96,64},{128,96},{160,128},{192,160},{224,1... | collective-permute-start | bytes 2359304 | tf_op jit(solution)/shard_map/ppermute | solution.py:550
  19.4 20.5 %collective-permute-start = (bf16[768,512]{1,0:T(8,128)(2,1)S(1)}, bf16[768,512]{1,0:T(8,128)(2,1)S(1)}, u32[]{:S(2)}, u32[]{:S(2)}) collective-permute-start(bf16[768,512]{1,0:T(8,128)(2,1)S(1)} %copy-done.12), channel_id=1, source_target_pairs={{0,32},{32,64},{64,96},{96,128},{128,160},{160,192},{192,224},{224... | collective-permute-start | bytes 2359304 | tf_op jit(solution)/shard_map/ppermute | solution.py:550
  19.6 72.2 %copy-start = (s32[1,3,768]{1,2,0:T(8,128)}, s32[1,3,768]{1,2,0:T(8,128)S(1)}, u32[]{:S(2)}) copy-start(s32[1,3,768]{1,2,0:T(8,128)S(1)} %copy.15) | copy-start | bytes 27652
  36.5 37.2 %copy-start.9 = (bf16[768,512]{1,0:T(8,128)(2,1)}, bf16[768,512]{1,0:T(8,128)(2,1)S(1)}, u32[]{:S(2)}) copy-start(bf16[768,512]{1,0:T(8,128)(2,1)S(1)} %collective-permute-done.1.above_1) | copy-start | bytes 2359300
  39.9 33.8 %copy-start.10 = (bf16[768,512]{1,0:T(8,128)(2,1)}, bf16[768,512]{1,0:T(8,128)(2,1)S(1)}, u32[]{:S(2)}) copy-start(bf16[768,512]{1,0:T(8,128)(2,1)S(1)} %collective-permute-done.below_1) | copy-start | bytes 2359300
  39.9 19.8 %collective-permute-start.2 = (bf16[768,512]{1,0:T(8,128)(2,1)S(1)}, bf16[768,512]{1,0:T(8,128)(2,1)S(1)}, u32[]{:S(2)}, u32[]{:S(2)}) collective-permute-start(bf16[768,512]{1,0:T(8,128)(2,1)S(1)} %collective-permute-done.below_1), channel_id=1, source_target_pairs={{0,32},{32,64},{64,96},{96,128},{128,160},{160,192},{192,224},{224... | collective-permute-start | bytes 2359304 | tf_op jit(solution)/shard_map/ppermute | solution.py:550
  39.9 19.9 %collective-permute-start.3 = (bf16[768,512]{1,0:T(8,128)(2,1)S(1)}, bf16[768,512]{1,0:T(8,128)(2,1)S(1)}, u32[]{:S(2)}, u32[]{:S(2)}) collective-permute-start(bf16[768,512]{1,0:T(8,128)(2,1)S(1)} %collective-permute-done.1.above_1), channel_id=1, source_target_pairs={{0,224},{32,0},{64,32},{96,64},{128,96},{160,128},{192,160},{224,1... | collective-permute-start | bytes 2359304 | tf_op jit(solution)/shard_map/ppermute | solution.py:550
  59.7 32.1 %copy-start.1 = (bf16[768,512]{1,0:T(8,128)(2,1)}, bf16[768,512]{1,0:T(8,128)(2,1)S(1)}, u32[]{:S(2)}) copy-start(bf16[768,512]{1,0:T(8,128)(2,1)S(1)} %collective-permute-done.2.below_2) | copy-start | bytes 2359300
  59.7 10.7 %collective-permute-start.4 = (bf16[384,512]{1,0:T(8,128)(2,1)S(1)}, bf16[384,512]{1,0:T(8,128)(2,1)}, u32[]{:S(2)}, u32[]{:S(2)}) collective-permute-start(bf16[384,512]{1,0:T(8,128)(2,1)S(1)} %slice.62), channel_id=1, source_target_pairs={{0,32},{32,64},{64,96},{96,128},{128,160},{160,192},{192,224},{224... | collective-permute-start | bytes 1179656 | tf_op jit(solution)/shard_map/ppermute | solution.py:550
  59.8 32.0 %copy-start.2 = (bf16[768,512]{1,0:T(8,128)(2,1)}, bf16[768,512]{1,0:T(8,128)(2,1)S(1)}, u32[]{:S(2)}) copy-start(bf16[768,512]{1,0:T(8,128)(2,1)S(1)} %collective-permute-done.3.above_2) | copy-start | bytes 2359300
  59.9 10.6 %collective-permute-start.6 = (bf16[384,512]{1,0:T(8,128)(2,1)S(1)}, bf16[384,512]{1,0:T(8,128)(2,1)}, u32[]{:S(2)}, u32[]{:S(2)}) collective-permute-start(bf16[384,512]{1,0:T(8,128)(2,1)S(1)} %slice.63), channel_id=1, source_target_pairs={{0,224},{32,0},{64,32},{96,64},{128,96},{160,128},{192,160},{224,1... | collective-permute-start | bytes 1179656 | tf_op jit(solution)/shard_map/ppermute | solution.py:550
  70.4 21.4 %collective-permute-start.5 = (bf16[384,512]{1,0:T(8,128)(2,1)}, bf16[384,512]{1,0:T(8,128)(2,1)}, u32[]{:S(2)}, u32[]{:S(2)}) collective-permute-start(bf16[384,512]{1,0:T(8,128)(2,1)} %collective-permute-done.4), channel_id=1, source_target_pairs={{0,32},{32,64},{64,96},{96,128},{128,160},{160,192},{192,224},{224... | collective-permute-start | bytes 1179656 | tf_op jit(solution)/shard_map/ppermute | solution.py:550
  70.4 21.4 %collective-permute-start.7 = (bf16[384,512]{1,0:T(8,128)(2,1)}, bf16[384,512]{1,0:T(8,128)(2,1)}, u32[]{:S(2)}, u32[]{:S(2)}) collective-permute-start(bf16[384,512]{1,0:T(8,128)(2,1)} %collective-permute-done.6), channel_id=1, source_target_pairs={{0,224},{32,0},{64,32},{96,64},{128,96},{160,128},{192,160},{224,1... | collective-permute-start | bytes 1179656 | tf_op jit(solution)/shard_map/ppermute | solution.py:550
  73.7 64.0 %collective-permute-start.8 = (bf16[768,512]{1,0:T(8,128)(2,1)}, bf16[768,512]{1,0:T(8,128)(2,1)S(1)}, u32[]{:S(2)}, u32[]{:S(2)}) collective-permute-start(bf16[768,512]{1,0:T(8,128)(2,1)} %get-tuple-element.60), channel_id=1, source_target_pairs={{0,64},{1,65},{2,66},{3,67},{4,68},{5,69},{6,70},{7,71},{8,72},{9,... | collective-permute-start | bytes 2359304 | tf_op jit(solution)/shard_map/ppermute | solution.py:545
  73.7 64.0 %collective-permute-start.9 = (bf16[768,512]{1,0:T(8,128)(2,1)}, bf16[768,512]{1,0:T(8,128)(2,1)S(1)}, u32[]{:S(2)}, u32[]{:S(2)}) collective-permute-start(bf16[768,512]{1,0:T(8,128)(2,1)} %get-tuple-element.61), channel_id=1, source_target_pairs={{0,32},{1,33},{2,34},{3,35},{4,36},{5,37},{6,38},{7,39},{8,40},{9,... | collective-permute-start | bytes 2359304 | tf_op jit(solution)/shard_map/ppermute | solution.py:545
  103.4 33.4 %all-to-all-start.1 = ((bf16[8,32,256]{2,1,0:T(8,128)(2,1)}), bf16[8,32,256]{2,1,0:T(8,128)(2,1)S(1)}, u32[]{:S(2)}, u32[]{:S(2)}) async-start(bf16[8,32,256]{2,1,0:T(8,128)(2,1)} %get-tuple-element.59), calls=%async_computation.1 | async-start | bytes 262144 | tf_op jit(solution)/shard_map/all_to_all | solution.py:554
  137.7 8.4 %copy-start.6 = (bf16[768,512]{1,0:T(8,128)(2,1)S(1)}, bf16[768,512]{1,0:T(8,128)(2,1)}, u32[]{:S(2)}) copy-start(bf16[768,512]{1,0:T(8,128)(2,1)} %get-tuple-element.64) | copy-start | bytes 2359300
  137.7 14.4 %copy-start.3 = (f32[3,16,768]{2,1,0:T(8,128)S(1)}, f32[3,16,768]{2,1,0:T(8,128)}, u32[]{:S(2)}) copy-start(f32[3,16,768]{2,1,0:T(8,128)} %get-tuple-element.67) | copy-start | bytes 442372
  137.7 0.9 copy-start.7
  137.7 1.1 copy-start.8
  138.8 69.9 %all-to-all-start.2 = ((bf16[32,144,512]{2,1,0:T(8,128)(2,1)}), bf16[32,144,512]{2,1,0:T(8,128)(2,1)}, u32[]{:S(2)}, u32[]{:S(2)}) async-start(bf16[32,144,512]{2,1,0:T(8,128)(2,1)} %broadcast_dynamic-update-slice_fusion), calls=%async_computation.2 | async-start | bytes 9437184 | tf_op jit(solution)/shard_map/all_to_all | solution.py:554
  146.1 34.3 %collective-permute-start.10 = (bf16[768,512]{1,0:T(8,128)(2,1)S(1)}, bf16[768,512]{1,0:T(8,128)(2,1)S(1)}, u32[]{:S(2)}, u32[]{:S(2)}) collective-permute-start(bf16[768,512]{1,0:T(8,128)(2,1)S(1)} %copy-done.6), channel_id=1, source_target_pairs={{0,128},{1,129},{2,130},{3,131},{4,132},{5,133},{6,134},{7,135},{8... | collective-permute-start | bytes 2359304 | tf_op jit(solution)/shard_map/ppermute | solution.py:545
  152.1 38.2 %collective-permute-start.13 = (f32[16,768]{1,0:T(8,128)S(1)}, f32[16,768]{1,0:T(8,128)S(1)}, u32[]{:S(2)}, u32[]{:S(2)}) collective-permute-start(f32[16,768]{1,0:T(8,128)S(1)} %get-tuple-element.75), channel_id=1, source_target_pairs={{0,32},{1,33},{2,34},{3,35},{4,36},{5,37},{6,38},{7,39},{8,40},{9,... | collective-permute-start | bytes 147464 | tf_op jit(solution)/shard_map/ppermute | solution.py:545
  152.7 37.5 %collective-permute-start.12 = (f32[16,768]{1,0:T(8,128)S(1)}, f32[16,768]{1,0:T(8,128)S(1)}, u32[]{:S(2)}, u32[]{:S(2)}) collective-permute-start(f32[16,768]{1,0:T(8,128)S(1)} %get-tuple-element.76), channel_id=1, source_target_pairs={{0,64},{1,65},{2,66},{3,67},{4,68},{5,69},{6,70},{7,71},{8,72},{9,... | collective-permute-start | bytes 147464 | tf_op jit(solution)/shard_map/ppermute | solution.py:545
  153.3 37.1 %collective-permute-start.11 = (f32[16,768]{1,0:T(8,128)S(1)}, f32[16,768]{1,0:T(8,128)S(1)}, u32[]{:S(2)}, u32[]{:S(2)}) collective-permute-start(f32[16,768]{1,0:T(8,128)S(1)} %get-tuple-element.77), channel_id=1, source_target_pairs={{0,128},{1,129},{2,130},{3,131},{4,132},{5,133},{6,134},{7,135},{8... | collective-permute-start | bytes 147464 | tf_op jit(solution)/shard_map/ppermute | solution.py:545
  180.3 10.0 %copy-start.11 = (bf16[768,512]{1,0:T(8,128)(2,1)}, bf16[768,512]{1,0:T(8,128)(2,1)S(1)}, u32[]{:S(2)}) copy-start(bf16[768,512]{1,0:T(8,128)(2,1)S(1)} %collective-permute-done.10.refs_0_) | copy-start | bytes 2359300
  190.3 0.6 copy-start.14
  210.6 18.9 %all-to-all-start.3 = ((f32[8,32,256]{2,1,0:T(8,128)}), f32[8,32,256]{2,1,0:T(8,128)S(1)}, u32[]{:S(2)}, u32[]{:S(2)}) async-start(f32[8,32,256]{2,1,0:T(8,128)} %broadcast_in_dim.2), calls=%async_computation.3 | async-start | bytes 524288 | tf_op jit(solution)/shard_map/all_to_all | solution.py:554
  (2 other events, 1.2 us)

commit v2 on v1

--- a/solution.py
+++ b/solution.py
@@ -9,11 +9,10 @@
 
 F32, BF16 = jnp.float32, jnp.bfloat16
 LOG2E = 1.4426950408889634
-GATHER, PREPARE, FORWARD, MERGE, BACKWARD, COLLECT, FINISH = (
-    round(1.15e9 * us) for us in (0.5, 1, 2, 2, 14, 1, 1)
+GATHER, PREPARE, FETCH, FORWARD, BACKWARD, PLACE, COLLECT, FINISH = (
+    round(1.15e9 * us) for us in (0.5, 1, 1, 3, 20, 1, 1, 1)
 )
 BUFFERS = 2
-VMEM_LIMIT = 56 * 1024 * 1024
 ROWS_ACROSS = (((1,), (1,)), ((), ()))
 ROWS_DOWN = (((0,), (0,)), ((), ()))
 
@@ -22,8 +21,11 @@
     return pl.BlockSpec(shape, lambda *_: (0,) * len(shape), pipeline_mode=pl.Buffered(1))
 
 
-def params():
-    return pltpu.CompilerParams(vmem_limit_bytes=VMEM_LIMIT)
+ANYWHERE = pl.BlockSpec(memory_space=pl.ANY)
+
+
+def params(mebibytes=60):
+    return pltpu.CompilerParams(vmem_limit_bytes=mebibytes << 20)
 
 
 def cost(flops, moved):
@@ -60,15 +62,13 @@
             num_scalar_prefetch=1,
             grid=(1,),
             in_specs=[whole((nodes, width)), whole((nodes, width))],
-            out_specs=[pl.BlockSpec(memory_space=pl.ANY), whole((nodes, 2 * width))],
+            out_specs=pl.BlockSpec(memory_space=pl.ANY),
             scratch_shapes=[
+                pltpu.VMEM((nodes, 2 * width), BF16),
                 pltpu.SemaphoreType.DMA((slots,)),
             ],
         ),
-        out_shape=[
-            jax.ShapeDtypeStruct((slots, block_rows, 2 * width), BF16),
-            jax.ShapeDtypeStruct((nodes, 2 * width), BF16),
-        ],
+        out_shape=jax.ShapeDtypeStruct((slots, block_rows, 2 * width), BF16),
         compiler_params=params(),
         cost_estimate=cost(GATHER, 1 << 10),
         name="gather_out",
@@ -149,15 +149,20 @@
     ).astype(BF16)
 
 
-def fill_table(table, key_ref, value_ref, halo_ref, sem):
+def fill_table(table, key_ref, value_ref, halo_ref, sems):
     blocks = table.shape[0] - halo_ref.shape[0]
     per, width = table.shape[1], key_ref.shape[1]
-    copy = pltpu.make_async_copy(halo_ref, table.at[pl.ds(blocks, halo_ref.shape[0])], sem)
-    copy.start()
+    copies = [
+        pltpu.make_async_copy(halo_ref, table.at[pl.ds(blocks, halo_ref.shape[0])], sems.at[2 * blocks])
+    ]
     for block in range(blocks):
-        table[block, :, :width] = key_ref[block * per : (block + 1) * per, :]
-        table[block, :, width:] = value_ref[block * per : (block + 1) * per, :]
-    return copy
+        for which, ref in enumerate((key_ref, value_ref)):
+            source = ref.at[pl.ds(block * per, per)]
+            target = table.at[block, :, pl.ds(which * width, width)]
+            copies.append(pltpu.make_async_copy(source, target, sems.at[2 * block + which]))
+    for copy in copies:
+        copy.start()
+    return copies
 
 
 def live(values, start, rows):
@@ -167,18 +172,43 @@
     return jnp.where(row < rows, values, -jnp.inf)
 
 
+def bring_halves(k_below, k_above, v_below, v_above, rows, sems):
+    half, features = k_below.shape
+    copies = []
+    for which, pair in enumerate(((k_below, k_above), (v_below, v_above))):
+        for end, ref in enumerate(pair):
+            target = rows.at[pl.ds(end * half, half), pl.ds(which * features, features)]
+            copies.append(pltpu.make_async_copy(ref, target, sems.at[2 * end + which]))
+    for copy in copies:
+        copy.start()
+    return copies
+
+
 def forward_kernel(
-    heads, dim, tile_block, tile_count, key_ref, value_ref, halo_ref, query_ref,
-    stats_out, mixed_out, table, picked, scores, raised, sem,
+    heads, dim, tile_block, tile_count, bias_ref, halo_ref, key_ref, value_ref,
+    k_below, k_above, v_below, v_above, match_ref, far_1, far_2, query_ref, grad_ref, update_grad_ref,
+    out_weight, update_out, weight_out, stats_out, query_grad_out, edge_out,
+    table, picked, scores, raised, weight_sum, rows_4, far_0, sem, sems,
 ):
     blocks, slots = tile_count.shape[0], tile_block.shape[0] // tile_count.shape[0]
     nodes, features = query_ref.shape
     per = nodes // blocks
     width = heads * dim
-    scale2 = dim**-0.5 * LOG2E
+    scale = dim**-0.5
+    scale2 = scale * LOG2E
     span = slots // 2 * per
     parts = [slice(0, span), slice(span, 2 * span)]
-    fill_table(table, key_ref, value_ref, halo_ref, sem).wait()
+    far = (far_0, far_1, far_2)
+    first = bring_halves(k_below, k_above, v_below, v_above, rows_4, sems)
+    copies = fill_table(table, key_ref, value_ref, halo_ref, sem)
+    target_node = lax.broadcasted_iota(jnp.int32, (nodes, nodes), 0)
+    chosen = (target_node == match_ref[...]).astype(F32).astype(BF16)
+    for copy in first:
+        copy.wait()
+    far_0[...] = dot(rows_4[...], chosen, ROWS_DOWN).astype(BF16)
+    weight_sum[...] = jnp.zeros_like(weight_sum)
+    for copy in copies:
+        copy.wait()
 
     def block_step(step, _):
         buffer = 0
@@ -186,109 +216,48 @@
         for slot in range(slots):
             picked[buffer, slot * per : (slot + 1) * per, :] = table[tile_block[step * slots + slot]]
         live_rows = tile_count[step] * per
-        for half in range(2):
-            unit = step * 2 + half
-            place = half
-            keys = slice(half * width, (half + 1) * width)
-            values = slice(features + half * width, features + (half + 1) * width)
-            query_masked = masked_heads(query_ref[at, keys], heads, dim)
-            top = None
-            for part in parts:
-                block = dot(picked[buffer, part, keys], query_masked, ROWS_ACROSS)
-                block = live(block, part.start, live_rows)
-                scores[place, part, :] = block
-                part_top = jnp.max(block.reshape(span // 8, 8, heads * per), axis=0)
-                top = part_top if top is None else jnp.maximum(top, part_top)
-            top = jnp.max(top, axis=0, keepdims=True) * scale2
-            total = jnp.zeros((8, heads * per), F32)
-            for part in parts:
-                block = jnp.exp2(scores[place, part, :] * scale2 - top)
-                raised[place, part, :] = block.astype(BF16)
-                total = total + jnp.sum(block.reshape(span // 8, 8, heads * per), axis=0)
-            total = jnp.sum(total, axis=0, keepdims=True)
-            mixed = dot(picked[buffer, :, values], raised[place], ROWS_DOWN)
-            mixed_out[unit] = diagonal(mixed, heads, dim, per)
-            stats_out[unit] = jnp.concatenate(
-                [top, total, jnp.zeros((6, heads * per), F32)], axis=0
-            )
-        return 0
-
-    lax.fori_loop(0, blocks, block_step, 0)
-
-
-def merge_kernel(
-    heads, dim, bias_ref, group_ref, below_1, above_1, below_2, above_2, below_4, above_4, match_ref,
-    query_ref, grad_ref, update_grad_ref, out_weight, stats_ref, mixed_ref,
-    update_out, weight_out, stats_out, query_grad_out, edge_out, weight_sum, far, sems,
-):
-    units = stats_ref.shape[0]
-    blocks = units // 2
-    nodes, features = query_ref.shape
-    per = nodes // blocks
-    width = heads * dim
-    scale = dim**-0.5
-    scale2 = scale * LOG2E
-    lane_node = lax.broadcasted_iota(jnp.int32, (per, nodes), 1)
-    place = group_ref[0]
-    half_rows = nodes // 2
-
-    def bring(turn, distance, below, above):
-        below_is_partner = lax.rem(place // distance, 2) == 1
-
-        @pl.when(below_is_partner)
-        def _():
-            pltpu.make_async_copy(below, far.at[turn], sems.at[turn]).start()
-
-        @pl.when(jnp.logical_not(below_is_partner))
-        def _():
-            pltpu.make_async_copy(above, far.at[turn], sems.at[turn]).start()
-
-    bring(2, 1, below_1, above_1)
-    bring(1, 2, below_2, above_2)
-    upper = pltpu.make_async_copy(below_4, far.at[0, pl.ds(0, half_rows)], sems.at[0])
-    lower = pltpu.make_async_copy(above_4, far.at[0, pl.ds(half_rows, half_rows)], sems.at[3])
-    upper.start()
-    lower.start()
-    weight_sum[...] = jnp.zeros_like(weight_sum)
-    edge_out[...] = jnp.zeros_like(edge_out)
-    for turn in (1, 2):
-        pltpu.make_async_copy(below_1, far.at[turn], sems.at[turn]).wait()
-    upper.wait()
-    lower.wait()
-
-    def block_step(step, _):
-        at = pl.ds(pl.multiple_of(step * per, per), per)
         query_t = query_ref[at, :].astype(F32).T
         grad_t = grad_ref[at, :].astype(F32).T
-        chosen, far_keys, far_values = [], [], []
-        for turn in range(3):
-            pick = (lane_node == match_ref[at, turn : turn + 1]).astype(F32).astype(BF16)
-            chosen.append(pick)
-            found = dot(pick, far[turn])
-            far_keys.append(found[:, :features].T)
-            far_values.append(found[:, features:].T)
+        far_keys = [far[turn][:features, at].astype(F32) for turn in range(3)]
+        far_values = [far[turn][features:, at].astype(F32) for turn in range(3)]
         attended_t = []
         rows = [[], [], []]
         for half in range(2):
             unit = step * 2 + half
             of = slice(half * width, (half + 1) * width)
+            values = slice(features + half * width, features + (half + 1) * width)
             bias = jnp.concatenate(
                 [jnp.full((1, per), bias_ref[half * heads + h] * LOG2E, F32) for h in range(heads)],
                 axis=1,
             )
-            scores = [
+            edge_scores = [
                 head_lanes(query_t[of] * far_keys[turn][of], heads, dim) * scale2 + bias
                 for turn in range(3)
             ]
-            tile_top, tile_total = stats_ref[unit, 0:1, :], stats_ref[unit, 1:2, :]
-            top = jnp.maximum(jnp.maximum(tile_top, scores[0]), jnp.maximum(scores[1], scores[2]))
-            shrink = jnp.exp2(tile_top - top)
-            raised = [jnp.exp2(scores[turn] - top) for turn in range(3)]
-            total = tile_total * shrink + (raised[0] + raised[1] + raised[2])
+            query_masked = masked_heads(query_ref[at, of], heads, dim)
+            top = None
+            for part in parts:
+                block = dot(picked[buffer, part, of], query_masked, ROWS_ACROSS)
+                block = live(block, part.start, live_rows)
+                scores[half, part, :] = block
+                part_top = jnp.max(block.reshape(span // 8, 8, heads * per), axis=0)
+                top = part_top if top is None else jnp.maximum(top, part_top)
+            top = jnp.max(top, axis=0, keepdims=True) * scale2
+            for turn in range(3):
+                top = jnp.maximum(top, edge_scores[turn])
+            total = jnp.zeros((8, heads * per), F32)
+            for part in parts:
+                block = jnp.exp2(scores[half, part, :] * scale2 - top)
+                raised[half, part, :] = block.astype(BF16)
+                total = total + jnp.sum(block.reshape(span // 8, 8, heads * per), axis=0)
+            total = jnp.sum(total, axis=0, keepdims=True)
+            edge_raised = [jnp.exp2(edge_scores[turn] - top) for turn in range(3)]
+            total = total + (edge_raised[0] + edge_raised[1] + edge_raised[2])
             inverse = 1.0 / total
-            probs = [raised[turn] * inverse for turn in range(3)]
+            probs = [edge_raised[turn] * inverse for turn in range(3)]
             weights = [probs[turn].astype(BF16).astype(F32) for turn in range(3)]
-            mixed = mixed_ref[unit] * spread(shrink * inverse, heads, dim, per)
+            mixed = dot(picked[buffer, :, values], raised[half], ROWS_DOWN)
+            mixed = diagonal(mixed, heads, dim, per) * spread(inverse, heads, dim, per)
             for turn in range(3):
                 mixed = mixed + spread(weights[turn], heads, dim, per) * far_values[turn][of]
             attended = mixed.astype(BF16)
@@ -306,10 +275,9 @@
             query_grad_out[unit] = query_grad
         both = jnp.concatenate(attended_t, axis=0)
         update_out[at, :] = dot(both, out_weight[...], ROWS_DOWN).astype(BF16)
-        product = dot(both, update_grad_ref[at, :])
-        weight_sum[...] += product
+        weight_sum[...] += dot(both, update_grad_ref[at, :])
         for turn in range(3):
-            edge_out[turn] += dot(jnp.concatenate(rows[turn], axis=0).astype(BF16), chosen[turn])
+            edge_out[turn, :, at] = jnp.concatenate(rows[turn], axis=0)
         return 0
 
     lax.fori_loop(0, blocks, block_step, 0)
@@ -321,7 +289,7 @@
 def backward_kernel(
     heads, dim, tile_block, tile_count, key_ref, value_ref, halo_ref, query_ref, grad_ref,
     stats_ref, edge_ref, returned_ref, own_terms_ref, query_out,
-    table, picked, weights, dscores, terms, sem,
+    table, picked, weights, dscores, terms, packed, sem, out_sems,
 ):
     blocks, slots = tile_count.shape[0], tile_block.shape[0] // tile_count.shape[0]
     nodes, features = query_ref.shape
@@ -331,10 +299,10 @@
     scale2 = scale * LOG2E
     span = slots // 2 * per
     parts = [slice(0, span), slice(span, 2 * span)]
-    halo_copy = fill_table(table, key_ref, value_ref, halo_ref, sem)
+    copies = fill_table(table, key_ref, value_ref, halo_ref, sem)
     terms[...] = jnp.zeros_like(terms)
-    returned_ref[:, per:, :] = jnp.zeros_like(returned_ref[:, per:, :])
-    halo_copy.wait()
+    for copy in copies:
+        copy.wait()
 
     def block_step(step, _):
         buffer = 0
@@ -370,11 +338,24 @@
         return 0
 
     lax.fori_loop(0, blocks, block_step, 0)
-    own_terms_ref[...] = terms[:blocks]
-    returned_ref[:, :per, :] = terms[blocks:].astype(BF16)
-
-
-def run(kernel, scalars, ins, outs, scratch, estimate, name):
+    copies = [pltpu.make_async_copy(terms.at[pl.ds(0, blocks)], own_terms_ref, out_sems.at[0])]
+    copies[0].start()
+    count = packed.shape[0]
+    chunk = count // 8
+    for start in range(0, count, chunk):
+        packed[start : start + chunk] = terms[blocks + start : blocks + start + chunk].astype(BF16)
+        copy = pltpu.make_async_copy(
+            packed.at[pl.ds(start, chunk)],
+            returned_ref.at[pl.ds(start, chunk), pl.ds(0, per)],
+            out_sems.at[1 + start // chunk],
+        )
+        copy.start()
+        copies.append(copy)
+    for copy in copies:
+        copy.wait()
+
+
+def run(kernel, scalars, ins, outs, scratch, estimate, name, mebibytes, elsewhere=()):
     specs = [whole(array.shape) if spec is None else spec for array, spec in ins]
     return pl.pallas_call(
         kernel,
@@ -382,65 +363,106 @@
             num_scalar_prefetch=len(scalars),
             grid=(1,),
             in_specs=specs,
-            out_specs=[whole(shape) for shape, _ in outs],
+            out_specs=[
+                ANYWHERE if place in elsewhere else whole(shape) for place, (shape, _) in enumerate(outs)
+            ],
             scratch_shapes=scratch,
         ),
         out_shape=[jax.ShapeDtypeStruct(shape, dtype) for shape, dtype in outs],
-        compiler_params=params(),
+        compiler_params=params(mebibytes),
         cost_estimate=cost(estimate, 1 << 10),
         name=name,
     )(*scalars, *(array for array, _ in ins))
 
 
-ANYWHERE = pl.BlockSpec(memory_space=pl.ANY)
-
-
-def forward(scalars, key_rows, value_rows, halo, query_rows, heads):
+def forward(scalars, bias, halo, fourth, match_row, far, key_rows, value_rows, query_rows,
+            attended_grad, grad_update, out_weight):
     tile_block, tile_count = scalars
     nodes, features = query_rows.shape
+    heads = bias.shape[0]
     blocks, slots = tile_count.shape[0], tile_block.shape[0] // tile_count.shape[0]
     per, width = nodes // blocks, features // 2
     columns = heads // 2 * per
+    arrays = [match_row, *far, query_rows, attended_grad, grad_update, out_weight]
     return run(
         functools.partial(forward_kernel, heads // 2, features // heads),
-        scalars,
-        [(key_rows, None), (value_rows, None), (halo, ANYWHERE), (query_rows, None)],
-        [((2 * blocks, 8, columns), F32), ((2 * blocks, width, per), F32)],
+        (tile_block, tile_count, bias),
+        [(array, ANYWHERE) for array in (halo, key_rows, value_rows, *fourth)] + [(array, None) for array in arrays],
+        [
+            ((nodes, features), BF16),
+            ((8, features // 8, features), BF16),
+            ((2 * blocks, 8, columns), F32),
+            ((2 * blocks, width, per), F32),
+            ((3, 2 * heads, nodes), F32),
+        ],
         [
             pltpu.VMEM((blocks + halo.shape[0], per, 2 * features), BF16),
             pltpu.VMEM((1, slots * per, 2 * features), BF16),
-            pltpu.VMEM((BUFFERS, slots * per, columns), F32),
-            pltpu.VMEM((BUFFERS, slots * per, columns), BF16),
-            pltpu.SemaphoreType.DMA,
+            pltpu.VMEM((2, slots * per, columns), F32),
+            pltpu.VMEM((2, slots * per, columns), BF16),
+            pltpu.VMEM((features, features), F32),
+            pltpu.VMEM((nodes, 2 * features), BF16),
+            pltpu.VMEM((2 * features, nodes), BF16),
+            pltpu.SemaphoreType.DMA((2 * blocks + 1,)),
+            pltpu.SemaphoreType.DMA((4,)),
         ],
         FORWARD,
         "forward",
-    )
-
-
-def merge(bias, group, far, match_columns, query_rows, attended_grad, grad_update, out_weight, stats, mixed):
-    nodes, features = query_rows.shape
-    heads = bias.shape[0]
-    arrays = [match_columns, query_rows, attended_grad, grad_update, out_weight, stats, mixed]
+        60,
+    )
+
+
+def fetch_kernel(distance, group_ref, k_below, k_above, v_below, v_above, match_ref, found_ref, rows, sems):
+    nodes, both = rows.shape
+    features = both // 2
+    lanes = (pl.ds(0, features), pl.ds(features, features))
+    copies = []
+    below_is_partner = lax.rem(group_ref[0] // distance, 2) == 1
+    for which, (below, above) in enumerate(((k_below, k_above), (v_below, v_above))):
+        target = rows.at[:, lanes[which]]
+
+        @pl.when(below_is_partner)
+        def _():
+            pltpu.make_async_copy(below, target, sems.at[which]).start()
+
+        @pl.when(jnp.logical_not(below_is_partner))
+        def _():
+            pltpu.make_async_copy(above, target, sems.at[which]).start()
+
+        copies.append(pltpu.make_async_copy(below, target, sems.at[which]))
+    target_node = lax.broadcasted_iota(jnp.int32, (nodes, nodes), 0)
+    chosen = (target_node == match_ref[...]).astype(F32).astype(BF16)
+    for copy in copies:
+        copy.wait()
+    found_ref[...] = dot(rows[...], chosen, ROWS_DOWN).astype(BF16)
+
+
+def fetch(distance, group, arrays, match_row):
+    nodes = match_row.shape[1]
+    features = arrays[0].shape[1]
     return run(
-        functools.partial(merge_kernel, heads // 2, features // heads),
-        (bias, group),
-        [(array, ANYWHERE) for array in far] + [(array, None) for array in arrays],
-        [
-            ((nodes, features), BF16),
-            ((8, features // 8, features), BF16),
-            (stats.shape, F32),
-            (mixed.shape, F32),
-            ((3, 2 * heads, nodes), F32),
-        ],
-        [
-            pltpu.VMEM((features, features), F32),
-            pltpu.VMEM((3, nodes, 2 * features), BF16),
-            pltpu.SemaphoreType.DMA((4,)),
-        ],
-        MERGE,
-        "merge",
-    )
+        functools.partial(fetch_kernel, distance),
+        (group,),
+        [(array, ANYWHERE) for array in arrays] + [(match_row, None)],
+        [((2 * features, nodes), BF16)],
+        [pltpu.VMEM((nodes, 2 * features), BF16), pltpu.SemaphoreType.DMA((4,))],
+        FETCH,
+        "fetch",
+        60,
+    )[0]
+
+
+def place_kernel(match_ref, rows_ref, *placed):
+    nodes = match_ref.shape[1]
+    target_node = lax.broadcasted_iota(jnp.int32, (nodes, nodes), 0)
+    for turn, placed_ref in enumerate(placed):
+        chosen = (target_node == match_ref[turn : turn + 1, :]).astype(F32).astype(BF16)
+        placed_ref[...] = dot(rows_ref[turn].astype(BF16), chosen, ROWS_ACROSS)
+
+
+def place(matching, rows):
+    out = (rows.shape[1:], F32)
+    return run(place_kernel, (), [(matching, None), (rows, None)], [out] * 3, [], PLACE, "place", 60)
 
 
 def backward(scalars, key_rows, value_rows, halo, query_rows, attended_grad, stats, edge_part, spare, heads):
@@ -453,7 +475,7 @@
     return run(
         functools.partial(backward_kernel, heads // 2, features // heads),
         scalars,
-        [(key_rows, None), (value_rows, None), (halo, ANYWHERE), (query_rows, None)]
+        [(key_rows, ANYWHERE), (value_rows, ANYWHERE), (halo, ANYWHERE), (query_rows, None)]
         + [(attended_grad, None), (stats, None), (edge_part, None)],
         [
             ((count, per + spare, 2 * features), BF16),
@@ -466,10 +488,14 @@
             pltpu.VMEM((BUFFERS, slots * per, columns), BF16),
             pltpu.VMEM((BUFFERS, slots * per, columns), BF16),
             pltpu.VMEM((blocks + count, per, 2 * features), F32),
-            pltpu.SemaphoreType.DMA,
+            pltpu.VMEM((count, per, 2 * features), BF16),
+            pltpu.SemaphoreType.DMA((2 * blocks + 1,)),
+            pltpu.SemaphoreType.DMA((9,)),
         ],
         BACKWARD,
         "backward",
+        60,
+        (0, 1),
     )
 
 
@@ -510,6 +536,7 @@
         [],
         COLLECT,
         "collect",
+        60,
     )
 
 
@@ -537,6 +564,7 @@
         [],
         FINISH,
         "finish",
+        60,
     )
 
 
@@ -577,23 +605,34 @@
     top_bit = devices.bit_length() - 1
     groups = lax.axis_size("group")
 
-    sent, own_rows = outgoing(send_block, key_rows, value_rows, per)
-    halo = exchange(sent, "dom")
-    below_1, above_1 = ahead(own_rows, 1), ahead(own_rows, -1)
+    halo = exchange(outgoing(send_block, key_rows, value_rows, per), "dom")
     attended_grad, *placed = prepare(query_rows, grad_update, out_weight, matching)
-    below_1, above_1, attended_grad = lax.optimization_barrier((below_1, above_1, attended_grad))
-    below_2, above_2 = ahead(below_1, 1), ahead(above_1, -1)
-    below_4 = ahead(ahead(below_2[: nodes // 2], 1), 1)
-    above_4 = ahead(ahead(above_2[nodes // 2 :], -1), -1)
-    far = [below_1, above_1, below_2, above_2, below_4, above_4]
+    half = nodes // 2
+    near = [(ahead(rows, 1), ahead(rows, -1)) for rows in (key_rows, value_rows)]
+    near[0], attended_grad = lax.optimization_barrier((near[0], attended_grad))
     group = lax.axis_index("group").astype(jnp.int32).reshape(1)
+
+    def found(turn, distance, ring):
+        return fetch(distance, group, [rows for pair in ring for rows in pair], matching[turn : turn + 1])
+
+    next_near = [(ahead(below, 1), ahead(above, -1)) for below, above in near]
+    far_2 = found(2, 1, near)
+    next_near[1], far_2 = lax.optimization_barrier((next_near[1], far_2))
+    third = [(ahead(below[:half], 1), ahead(above[half:], -1)) for below, above in next_near]
+    fourth = [(ahead(below, 1), ahead(above, -1)) for below, above in third]
+    far_1 = found(1, 2, next_near)
+    fourth, far_1, placed[1], placed[2] = lax.optimization_barrier(
+        (fourth, far_1, placed[1], placed[2])
+    )
     placed = [from_partner(placed[turn], top_bit - 1 - turn) for turn in range(3)]
+    fourth = [rows for pair in fourth for rows in pair]
 
     scalars = (tile_block.reshape(-1), tile_count)
-    stats, mixed = forward(scalars, key_rows, value_rows, halo, query_rows, heads)
-    update, pieces, stats, edge_part, edges = merge(
-        expander_bias, group, far, matching.T, query_rows, attended_grad, grad_update, out_weight, stats, mixed
-    )
+    update, pieces, stats, edge_part, edges = forward(
+        scalars, expander_bias, halo, fourth, matching[:1], (far_1, far_2), key_rows, value_rows, query_rows,
+        attended_grad, grad_update, out_weight,
+    )
+    edges = place(matching, edges)
     edges = [from_partner(edges[turn], top_bit - 1 - turn) for turn in range(3)]
     pieces = exchange(pieces, "group")
     spare = features // 8 // 2

time: 231 us -> 222 us (0.961)
  waiting for transfers between devices: 93.1 us -> 71.3 us
  starting transfers between devices: 56.1 us -> 67.4 us
    ppermute x8 -> x16, waiting for transfers between devices: 39.3 us -> 20 us  [ahead(): lax.ppermute(array, 'group', [(i, (i + steps) % count) for i in range(cou...]
    ppermute x8 -> x16, starting transfers between devices: 15.8 us -> 26.8 us  [ahead(): lax.ppermute(array, 'group', [(i, (i + steps) % count) for i in range(cou...]
    pallas_call x5 -> x7, Pallas kernels: 63.9 us -> 66.6 us  [run(): pl.pallas_call(kernel, grid_spec=pltpu.PrefetchScalarGridSpec(num_scalar_...]
  transfers between devices with their start and end apart: 18 -> 26, of which waited for: 9 -> 14; matrix products, arithmetic and copies ran while one was open for 1% -> 1% of each run, Pallas kernels for 30% -> 32%
where the time goes in v2:
time: 222 us
  Pallas kernels  74.9 us (34%)
  waiting for transfers between devices  71.3 us (32%)
  starting transfers between devices  67.4 us (30%)
  local copies, waits for them, and re-layouts  5.81 us (3%)
    pallas_call x7, Pallas kernels, run(): pl.pallas_call(kernel, grid_spec=pltpu.PrefetchScalarGridSpec(num_scalar_...  66.6 us
    ppermute x6, waiting for transfers between devices, from_partner(): lax.ppermute(array, axes, [(i, i ^ 1 << apart) for i in range(lax.axis_si...  32.3 us
    all_to_all x4, starting transfers between devices, exchange(): return lax.all_to_all(array, axis, split_axis=0, concat_axis=0, tiled=True)  27.5 us
    ppermute x16, starting transfers between devices, ahead(): lax.ppermute(array, 'group', [(i, (i + steps) % count) for i in range(cou...  26.8 us
    ppermute x16, waiting for transfers between devices, ahead(): lax.ppermute(array, 'group', [(i, (i + steps) % count) for i in range(cou...  20 us
    all_to_all x4, waiting for transfers between devices, exchange(): return lax.all_to_all(array, axis, split_axis=0, concat_axis=0, tiled=True)  19.1 us
    ppermute x6, starting transfers between devices, from_partner(): lax.ppermute(array, axes, [(i, i ^ 1 << apart) for i in range(lax.axis_si...  13.1 us
  transfers between devices with their start and end apart: 26, of which 14 were waited for; matrix products, arithmetic and copies ran while one was open for 1% of the time, Pallas kernels for 32%

profile of v2, /device:TPU:8, one launch (start us, length us, event | category | flops | bytes accessed | tf_op | source)
XLA Modules:
  0.0 221.6 jit_solution(7637000678666204940)
XLA Ops:
  0.6 4.1 %gather_out.1 = bf16[32,128,512]{2,1,0:T(8,128)(2,1)} custom-call(s32[32]{0:T(128)} %bitcast.16, bf16[768,256]{1,0:T(8,128)(2,1)} %key_ref.5, bf16[768,256]{1,0:T(8,128)(2,1)} %value_ref.5), custom_call_target="tpu_custom_call" | custom-call | flops 575000000 | bytes 1024 | tf_op jit(solution)/shard_map/gather_out/pallas_call | solution.py:59
  4.8 7.7 %all-to-all-start = ((bf16[32,128,512]{2,1,0:T(8,128)(2,1)}), bf16[32,128,512]{2,1,0:T(8,128)(2,1)}, u32[]{:S(2)}, u32[]{:S(2)}) async-start(bf16[32,128,512]{2,1,0:T(8,128)(2,1)} %gather_out.1), calls=%async_computation | async-start | bytes 8388608 | tf_op jit(solution)/shard_map/all_to_all | solution.py:582
  12.6 5.9 %collective-permute-start.10 = (bf16[768,256]{1,0:T(8,128)(2,1)S(1)}, bf16[768,256]{1,0:T(8,128)(2,1)}, u32[]{:S(2)}, u32[]{:S(2)}) collective-permute-start(bf16[768,256]{1,0:T(8,128)(2,1)S(1)} %copy-done.1), channel_id=1, source_target_pairs={{0,224},{32,0},{64,32},{96,64},{128,96},{160,128},{192,160},{224,1... | collective-permute-start | bytes 1179656 | tf_op jit(solution)/shard_map/ppermute | solution.py:578
  18.5 3.2 %collective-permute-start.1 = (bf16[768,256]{1,0:T(8,128)(2,1)S(1)}, bf16[768,256]{1,0:T(8,128)(2,1)S(1)}, u32[]{:S(2)}, u32[]{:S(2)}) collective-permute-start(bf16[768,256]{1,0:T(8,128)(2,1)S(1)} %copy-done), channel_id=1, source_target_pairs={{0,224},{32,0},{64,32},{96,64},{128,96},{160,128},{192,160},{224,1... | collective-permute-start | bytes 1179656 | tf_op jit(solution)/shard_map/ppermute | solution.py:578
  22.4 5.6 %collective-permute-done.10.v_above = bf16[768,256]{1,0:T(8,128)(2,1)} collective-permute-done((bf16[768,256]{1,0:T(8,128)(2,1)S(1)}, bf16[768,256]{1,0:T(8,128)(2,1)}, u32[]{:S(2)}, u32[]{:S(2)}) %collective-permute-start.10) | collective-permute-done | bytes 393248 | tf_op jit(solution)/shard_map/ppermute | solution.py:578
  28.0 3.8 %collective-permute-start.11 = (bf16[768,256]{1,0:T(8,128)(2,1)}, bf16[768,256]{1,0:T(8,128)(2,1)S(1)}, u32[]{:S(2)}, u32[]{:S(2)}) collective-permute-start(bf16[768,256]{1,0:T(8,128)(2,1)} %collective-permute-done.10.v_above), channel_id=1, source_target_pairs={{0,224},{32,0},{64,32},{96,64},{128,96},{160,128},{192,160},{224,1... | collective-permute-start | bytes 1179656 | tf_op jit(solution)/shard_map/ppermute | solution.py:578
  31.8 4.2 %prepare.1 = (bf16[768,256]{1,0:T(8,128)(2,1)}, bf16[768,512]{1,0:T(8,128)(2,1)}, bf16[768,512]{1,0:T(8,128)(2,1)}, bf16[768,512]{1,0:T(8,128)(2,1)}) custom-call(bf16[768,256]{1,0:T(8,128)(2,1)} %query_ref.5, bf16[768,256]{1,0:T(8,128)(2,1)} %update_grad_ref.1, bf16[256,256]{1,0:T(8,128)(2,1)} %out_weight.1, s32[3,768]{1,0:T(4,128)} %bitcast.14), custom_call_target="tpu_custom_call" | custom-call | flops 1150000000 | bytes 1024 | tf_op jit(solution)/shard_map/prepare/pallas_call | solution.py:92
  36.4 3.8 %collective-permute-done.k_below = bf16[768,256]{1,0:T(8,128)(2,1)} collective-permute-done((bf16[768,256]{1,0:T(8,128)(2,1)S(1)}, bf16[768,256]{1,0:T(8,128)(2,1)}, u32[]{:S(2)}, u32[]{:S(2)}) %collective-permute-start) | collective-permute-done | bytes 393248 | tf_op jit(solution)/shard_map/ppermute | solution.py:578
  40.2 3.2 %collective-permute-start.5 = (bf16[768,256]{1,0:T(8,128)(2,1)S(1)}, bf16[768,256]{1,0:T(8,128)(2,1)S(1)}, u32[]{:S(2)}, u32[]{:S(2)}) collective-permute-start(bf16[768,256]{1,0:T(8,128)(2,1)S(1)} %collective-permute-done.1.k_above), channel_id=1, source_target_pairs={{0,224},{32,0},{64,32},{96,64},{128,96},{160,128},{192,160},{224,1... | collective-permute-start | bytes 1179656 | tf_op jit(solution)/shard_map/ppermute | solution.py:578
  44.1 3.7 %fetch.2.far_2 = bf16[512,768]{1,0:T(8,128)(2,1)} custom-call(s32[1]{0:T(128)} %bitcast.2.group_ref, bf16[768,256]{1,0:T(8,128)(2,1)} %collective-permute-done.k_below, bf16[768,256]{1,0:T(8,128)(2,1)} %copy-done.13, bf16[768,256]{1,0:T(8,128)(2,1)} %collective-permute-done.8.v_below, bf16[768,256]{1,0:T(8,128)(2,1)} %collective-permute-done.10.v_above, ...), custom_call_target="tpu_custom_call" | custom-call | flops 1150000000 | bytes 1024 | tf_op jit(solution)/shard_map/fetch/pallas_call | solution.py:360
  48.7 2.0 collective-permute-start.12
  50.7 6.3 %collective-permute-done.2.k_below = bf16[768,256]{1,0:T(8,128)(2,1)S(1)} collective-permute-done((bf16[768,256]{1,0:T(8,128)(2,1)}, bf16[768,256]{1,0:T(8,128)(2,1)S(1)}, u32[]{:S(2)}, u32[]{:S(2)}) %collective-permute-start.2) | collective-permute-done | bytes 393248 | tf_op jit(solution)/shard_map/ppermute | solution.py:578
  57.3 3.3 %collective-permute-start.6 = (bf16[384,256]{1,0:T(8,128)(2,1)S(1)}, bf16[384,256]{1,0:T(8,128)(2,1)}, u32[]{:S(2)}, u32[]{:S(2)}) collective-permute-start(bf16[384,256]{1,0:T(8,128)(2,1)S(1)} %slice.83), channel_id=1, source_target_pairs={{0,224},{32,0},{64,32},{96,64},{128,96},{160,128},{192,160},{224,1... | collective-permute-start | bytes 589832 | tf_op jit(solution)/shard_map/ppermute | solution.py:578
  62.6 2.5 %collective-permute-done.3 = bf16[384,256]{1,0:T(8,128)(2,1)} collective-permute-done((bf16[384,256]{1,0:T(8,128)(2,1)S(1)}, bf16[384,256]{1,0:T(8,128)(2,1)}, u32[]{:S(2)}, u32[]{:S(2)}) %collective-permute-start.3) | collective-permute-done | bytes 196640 | tf_op jit(solution)/shard_map/ppermute | solution.py:578
  65.2 3.4 %collective-permute-start.7 = (bf16[384,256]{1,0:T(8,128)(2,1)}, bf16[384,256]{1,0:T(8,128)(2,1)}, u32[]{:S(2)}, u32[]{:S(2)}) collective-permute-start(bf16[384,256]{1,0:T(8,128)(2,1)} %collective-permute-done.6), channel_id=1, source_target_pairs={{0,224},{32,0},{64,32},{96,64},{128,96},{160,128},{192,160},{224,1... | collective-permute-start | bytes 589832 | tf_op jit(solution)/shard_map/ppermute | solution.py:578
  69.3 3.5 %fetch.3.far_1 = bf16[512,768]{1,0:T(8,128)(2,1)} custom-call(s32[1]{0:T(128)} %bitcast.2.group_ref, bf16[768,256]{1,0:T(8,128)(2,1)} %copy-done.4, bf16[768,256]{1,0:T(8,128)(2,1)} %copy-done.5, bf16[768,256]{1,0:T(8,128)(2,1)} %copy-done.3, bf16[768,256]{1,0:T(8,128)(2,1)} %copy-done.2, s32[1,768]{1,0:T(1,128)} %get-tuple-element.99.match_ref), custom_call_target="tpu_custom_call" | custom-call | flops 1150000000 | bytes 1024 | tf_op jit(solution)/shard_map/fetch/pallas_call | solution.py:360
  73.0 2.6 %collective-permute-start.17 = (bf16[768,512]{1,0:T(8,128)(2,1)S(1)}, bf16[768,512]{1,0:T(8,128)(2,1)}, u32[]{:S(2)}, u32[]{:S(2)}) collective-permute-start(bf16[768,512]{1,0:T(8,128)(2,1)S(1)} %copy-done.9), channel_id=1, source_target_pairs={{0,32},{1,33},{2,34},{3,35},{4,36},{5,37},{6,38},{7,39},{8,40},{9,... | collective-permute-start | bytes 2359304 | tf_op jit(solution)/shard_map/ppermute | solution.py:573
  75.6 21.1 %forward.1 = (bf16[768,256]{1,0:T(8,128)(2,1)}, bf16[8,32,256]{2,1,0:T(8,128)(2,1)}, f32[12,8,512]{2,1,0:T(8,128)}, f32[12,128,128]{2,1,0:T(8,128)}, f32[3,16,768]{2,1,0:T(8,128)}) custom-call(s32[48]{0:T(128)} %reshape_squeeze.3.tile_block, s32[6]{0:T(128)} %bitcast.18, f32[8]{0:T(128)} %bias_ref.1, bf16[32,128,512]{2,1,0:T(8,128)(2,1)} %all-to-all-done.halo_ref, ...), custom_call_target="tpu_custom_call" | custom-call | flops 3449999872 | bytes 1024 | tf_op jit(solution)/shard_map/forward/pallas_call | solution.py:360
  96.7 5.3 %all-to-all-start.1 = ((bf16[8,32,256]{2,1,0:T(8,128)(2,1)}), bf16[8,32,256]{2,1,0:T(8,128)(2,1)S(1)}, u32[]{:S(2)}, u32[]{:S(2)}) async-start(bf16[8,32,256]{2,1,0:T(8,128)(2,1)} %get-tuple-element.74), calls=%async_computation.1 | async-start | bytes 262144 | tf_op jit(solution)/shard_map/all_to_all | solution.py:582
  101.9 26.3 %backward.1 = (bf16[32,144,512]{2,1,0:T(8,128)(2,1)}, f32[6,128,512]{2,1,0:T(8,128)}, f32[768,256]{1,0:T(8,128)}) custom-call(s32[48]{0:T(128)} %reshape_squeeze.3.tile_block, s32[6]{0:T(128)} %bitcast.19, bf16[768,256]{1,0:T(8,128)(2,1)} %key_ref.5, bf16[768,256]{1,0:T(8,128)(2,1)} %value_ref.5, bf16[32,128,512]{2,1,0:T(8,128)(2,1)} %all-to-all-done.halo_ref, ...), custom_call_target="tpu_custom_call" | custom-call | flops 23000000512 | bytes 1024 | tf_op jit(solution)/shard_map/backward/pallas_call | solution.py:360
  130.1 7.3 %all-to-all-start.2 = ((bf16[32,144,512]{2,1,0:T(8,128)(2,1)}), bf16[32,144,512]{2,1,0:T(8,128)(2,1)}, u32[]{:S(2)}, u32[]{:S(2)}) async-start(bf16[32,144,512]{2,1,0:T(8,128)(2,1)} %broadcast_dynamic-update-slice_fusion), calls=%async_computation.2 | async-start | bytes 9437184 | tf_op jit(solution)/shard_map/all_to_all | solution.py:582
  137.4 6.0 %collective-permute-start.18 = (bf16[768,512]{1,0:T(8,128)(2,1)S(1)}, bf16[768,512]{1,0:T(8,128)(2,1)S(1)}, u32[]{:S(2)}, u32[]{:S(2)}) collective-permute-start(bf16[768,512]{1,0:T(8,128)(2,1)S(1)} %copy-done.8), channel_id=1, source_target_pairs={{0,128},{1,129},{2,130},{3,131},{4,132},{5,133},{6,134},{7,135},{8... | collective-permute-start | bytes 2359304 | tf_op jit(solution)/shard_map/ppermute | solution.py:573
  143.4 2.6 %place.1 = (f32[16,768]{1,0:T(8,128)}, f32[16,768]{1,0:T(8,128)}, f32[16,768]{1,0:T(8,128)}) custom-call(s32[3,768]{1,0:T(4,128)} %bitcast.15, f32[3,16,768]{2,1,0:T(8,128)} %get-tuple-element.82.rows_ref), custom_call_target="tpu_custom_call" | custom-call | flops 1150000000 | bytes 1024 | tf_op jit(solution)/shard_map/place/pallas_call | solution.py:360
  146.1 2.9 %collective-permute-start.20 = (f32[16,768]{1,0:T(8,128)}, f32[16,768]{1,0:T(8,128)S(1)}, u32[]{:S(2)}, u32[]{:S(2)}) collective-permute-start(f32[16,768]{1,0:T(8,128)} %get-tuple-element.84), channel_id=1, source_target_pairs={{0,64},{1,65},{2,66},{3,67},{4,68},{5,69},{6,70},{7,71},{8,72},{9,... | collective-permute-start | bytes 147464 | tf_op jit(solution)/shard_map/ppermute | solution.py:573
  150.5 21.6 %collective-permute-done.18.refs_0_ = bf16[768,512]{1,0:T(8,128)(2,1)S(1)} collective-permute-done((bf16[768,512]{1,0:T(8,128)(2,1)S(1)}, bf16[768,512]{1,0:T(8,128)(2,1)S(1)}, u32[]{:S(2)}, u32[]{:S(2)}) %collective-permute-start.18) | collective-permute-done | bytes 786464 | tf_op jit(solution)/shard_map/ppermute | solution.py:573
  172.0 3.7 %collective-permute-done.19.refs_3_ = f32[16,768]{1,0:T(8,128)S(1)} collective-permute-done((f32[16,768]{1,0:T(8,128)}, f32[16,768]{1,0:T(8,128)S(1)}, u32[]{:S(2)}, u32[]{:S(2)}) %collective-permute-start.19) | collective-permute-done | bytes 49184 | tf_op jit(solution)/shard_map/ppermute | solution.py:573
  175.7 6.7 %collective-permute-done.20.refs_4_ = f32[16,768]{1,0:T(8,128)S(1)} collective-permute-done((f32[16,768]{1,0:T(8,128)}, f32[16,768]{1,0:T(8,128)S(1)}, u32[]{:S(2)}, u32[]{:S(2)}) %collective-permute-start.20) | collective-permute-done | bytes 49184 | tf_op jit(solution)/shard_map/ppermute | solution.py:573
  183.3 4.2 %collect.1 = (f32[768,256]{1,0:T(8,128)}, f32[768,256]{1,0:T(8,128)}) custom-call(f32[6,128,512]{2,1,0:T(8,128)} %get-tuple-element.78.own_ref, bf16[768,512]{1,0:T(8,128)(2,1)} %copy-done.12, bf16[768,512]{1,0:T(8,128)(2,1)} %copy-done.11, bf16[768,512]{1,0:T(8,128)(2,1)} %collective-permute-done.17.refs_2_, f32[16,768]{1,0:T(8,128)} %copy-done.16, ...), custom_call_target="tpu_custom_call" | custom-call | flops 1150000000 | bytes 1024 | tf_op jit(solution)/shard_map/collect/pallas_call | solution.py:360
  187.5 12.6 %all-to-all-done.2.home_ref = bf16[32,144,512]{2,1,0:T(8,128)(2,1)} async-done(((bf16[32,144,512]{2,1,0:T(8,128)(2,1)}), bf16[32,144,512]{2,1,0:T(8,128)(2,1)}, u32[]{:S(2)}, u32[]{:S(2)}) %all-to-all-start.2) | async-done | bytes 4718624 | tf_op jit(solution)/shard_map/all_to_all | solution.py:582
  202.0 7.2 %all-to-all-start.3 = ((f32[8,32,256]{2,1,0:T(8,128)}), f32[8,32,256]{2,1,0:T(8,128)S(1)}, u32[]{:S(2)}, u32[]{:S(2)}) async-start(f32[8,32,256]{2,1,0:T(8,128)} %broadcast_in_dim.2), calls=%async_computation.3 | async-start | bytes 524288 | tf_op jit(solution)/shard_map/all_to_all | solution.py:582
  209.2 5.2 %finish.1 = (f32[768,256]{1,0:T(8,128)}, f32[768,256]{1,0:T(8,128)}) custom-call(s32[32]{0:T(128)} %bitcast.17, bf16[32,144,512]{2,1,0:T(8,128)(2,1)} %all-to-all-done.2.home_ref, f32[768,256]{1,0:T(8,128)} %get-tuple-element.89.key_in, f32[768,256]{1,0:T(8,128)} %get-tuple-element.90.value_in), custom_call_target="tpu_custom_call" | custom-call | flops 1150000000 | bytes 1024 | tf_op jit(solution)/shard_map/finish/pallas_call | solution.py:360
  214.4 6.5 %all-to-all-done.3 = f32[8,32,256]{2,1,0:T(8,128)S(1)} async-done(((f32[8,32,256]{2,1,0:T(8,128)}), f32[8,32,256]{2,1,0:T(8,128)S(1)}, u32[]{:S(2)}, u32[]{:S(2)}) %all-to-all-start.3) | async-done | bytes 262176 | tf_op jit(solution)/shard_map/all_to_all | solution.py:582
  (85 shorter events, 12.5 us)
Async XLA Ops:
  4.8 16.9 %copy-start.6 = (s32[1,3,768]{2,0,1:T(1,128)S(1)}, s32[1,3,768]{2,0,1:T(1,128)}, u32[]{:S(2)}) copy-start(s32[1,3,768]{2,0,1:T(1,128)} %param.21) | copy-start | bytes 27652
  4.8 70.7 %all-to-all-start = ((bf16[32,128,512]{2,1,0:T(8,128)(2,1)}), bf16[32,128,512]{2,1,0:T(8,128)(2,1)}, u32[]{:S(2)}, u32[]{:S(2)}) async-start(bf16[32,128,512]{2,1,0:T(8,128)(2,1)} %gather_out.1), calls=%async_computation | async-start | bytes 8388608 | tf_op jit(solution)/shard_map/all_to_all | solution.py:582
  12.6 15.4 %collective-permute-start.10 = (bf16[768,256]{1,0:T(8,128)(2,1)S(1)}, bf16[768,256]{1,0:T(8,128)(2,1)}, u32[]{:S(2)}, u32[]{:S(2)}) collective-permute-start(bf16[768,256]{1,0:T(8,128)(2,1)S(1)} %copy-done.1), channel_id=1, source_target_pairs={{0,224},{32,0},{64,32},{96,64},{128,96},{160,128},{192,160},{224,1... | collective-permute-start | bytes 1179656 | tf_op jit(solution)/shard_map/ppermute | solution.py:578
  18.5 13.3 %collective-permute-start.8 = (bf16[768,256]{1,0:T(8,128)(2,1)S(1)}, bf16[768,256]{1,0:T(8,128)(2,1)}, u32[]{:S(2)}, u32[]{:S(2)}) collective-permute-start(bf16[768,256]{1,0:T(8,128)(2,1)S(1)} %copy-done.1), channel_id=1, source_target_pairs={{0,32},{32,64},{64,96},{96,128},{128,160},{160,192},{192,224},{224... | collective-permute-start | bytes 1179656 | tf_op jit(solution)/shard_map/ppermute | solution.py:578
  18.5 17.9 %collective-permute-start.1 = (bf16[768,256]{1,0:T(8,128)(2,1)S(1)}, bf16[768,256]{1,0:T(8,128)(2,1)S(1)}, u32[]{:S(2)}, u32[]{:S(2)}) collective-permute-start(bf16[768,256]{1,0:T(8,128)(2,1)S(1)} %copy-done), channel_id=1, source_target_pairs={{0,224},{32,0},{64,32},{96,64},{128,96},{160,128},{192,160},{224,1... | collective-permute-start | bytes 1179656 | tf_op jit(solution)/shard_map/ppermute | solution.py:578
  21.7 18.5 %collective-permute-start = (bf16[768,256]{1,0:T(8,128)(2,1)S(1)}, bf16[768,256]{1,0:T(8,128)(2,1)}, u32[]{:S(2)}, u32[]{:S(2)}) collective-permute-start(bf16[768,256]{1,0:T(8,128)(2,1)S(1)} %copy-done), channel_id=1, source_target_pairs={{0,32},{32,64},{64,96},{96,128},{128,160},{160,192},{192,224},{224... | collective-permute-start | bytes 1179656 | tf_op jit(solution)/shard_map/ppermute | solution.py:578
  28.0 19.8 %collective-permute-start.11 = (bf16[768,256]{1,0:T(8,128)(2,1)}, bf16[768,256]{1,0:T(8,128)(2,1)S(1)}, u32[]{:S(2)}, u32[]{:S(2)}) collective-permute-start(bf16[768,256]{1,0:T(8,128)(2,1)} %collective-permute-done.10.v_above), channel_id=1, source_target_pairs={{0,224},{32,0},{64,32},{96,64},{128,96},{160,128},{192,160},{224,1... | collective-permute-start | bytes 1179656 | tf_op jit(solution)/shard_map/ppermute | solution.py:578
  31.8 16.7 %collective-permute-start.9 = (bf16[768,256]{1,0:T(8,128)(2,1)}, bf16[768,256]{1,0:T(8,128)(2,1)S(1)}, u32[]{:S(2)}, u32[]{:S(2)}) collective-permute-start(bf16[768,256]{1,0:T(8,128)(2,1)} %collective-permute-done.8.v_below), channel_id=1, source_target_pairs={{0,32},{32,64},{64,96},{96,128},{128,160},{160,192},{192,224},{224... | collective-permute-start | bytes 1179656 | tf_op jit(solution)/shard_map/ppermute | solution.py:578
  31.8 36.7 %copy-start.7 = (s32[1,6,8]{2,0,1:T(1,128)S(1)}, s32[1,6,8]{2,0,1:T(1,128)}, u32[]{:S(2)}) copy-start(s32[1,6,8]{2,0,1:T(1,128)} %param.18) | copy-start | bytes 580
  40.2 16.7 %collective-permute-start.2 = (bf16[768,256]{1,0:T(8,128)(2,1)}, bf16[768,256]{1,0:T(8,128)(2,1)S(1)}, u32[]{:S(2)}, u32[]{:S(2)}) collective-permute-start(bf16[768,256]{1,0:T(8,128)(2,1)} %collective-permute-done.k_below), channel_id=1, source_target_pairs={{0,32},{32,64},{64,96},{96,128},{128,160},{160,192},{192,224},{224... | collective-permute-start | bytes 1179656 | tf_op jit(solution)/shard_map/ppermute | solution.py:578
  40.2 17.0 %collective-permute-start.5 = (bf16[768,256]{1,0:T(8,128)(2,1)S(1)}, bf16[768,256]{1,0:T(8,128)(2,1)S(1)}, u32[]{:S(2)}, u32[]{:S(2)}) collective-permute-start(bf16[768,256]{1,0:T(8,128)(2,1)S(1)} %collective-permute-done.1.k_above), channel_id=1, source_target_pairs={{0,224},{32,0},{64,32},{96,64},{128,96},{160,128},{192,160},{224,1... | collective-permute-start | bytes 1179656 | tf_op jit(solution)/shard_map/ppermute | solution.py:578
  44.1 28.8 %copy-start.10 = (bf16[768,512]{1,0:T(8,128)(2,1)S(1)}, bf16[768,512]{1,0:T(8,128)(2,1)}, u32[]{:S(2)}) copy-start(bf16[768,512]{1,0:T(8,128)(2,1)} %get-tuple-element.75) | copy-start | bytes 2359300
  44.1 28.9 %copy-start.9 = (bf16[768,512]{1,0:T(8,128)(2,1)S(1)}, bf16[768,512]{1,0:T(8,128)(2,1)}, u32[]{:S(2)}) copy-start(bf16[768,512]{1,0:T(8,128)(2,1)} %get-tuple-element.76) | copy-start | bytes 2359300
  47.8 21.5 %copy-start.2 = (bf16[768,256]{1,0:T(8,128)(2,1)}, bf16[768,256]{1,0:T(8,128)(2,1)S(1)}, u32[]{:S(2)}) copy-start(bf16[768,256]{1,0:T(8,128)(2,1)S(1)} %collective-permute-done.11.v_above) | copy-start | bytes 1179652
  48.6 20.7 %copy-start.3 = (bf16[768,256]{1,0:T(8,128)(2,1)}, bf16[768,256]{1,0:T(8,128)(2,1)S(1)}, u32[]{:S(2)}) copy-start(bf16[768,256]{1,0:T(8,128)(2,1)S(1)} %collective-permute-done.9.v_below) | copy-start | bytes 1179652
  48.6 12.0 %collective-permute-start.14 = (bf16[384,256]{1,0:T(8,128)(2,1)S(1)}, bf16[384,256]{1,0:T(8,128)(2,1)}, u32[]{:S(2)}, u32[]{:S(2)}) collective-permute-start(bf16[384,256]{1,0:T(8,128)(2,1)S(1)} %slice.72), channel_id=1, source_target_pairs={{0,224},{32,0},{64,32},{96,64},{128,96},{160,128},{192,160},{224,1... | collective-permute-start | bytes 589832 | tf_op jit(solution)/shard_map/ppermute | solution.py:578
  48.7 12.5 %collective-permute-start.12 = (bf16[384,256]{1,0:T(8,128)(2,1)S(1)}, bf16[384,256]{1,0:T(8,128)(2,1)}, u32[]{:S(2)}, u32[]{:S(2)}) collective-permute-start(bf16[384,256]{1,0:T(8,128)(2,1)S(1)} %slice.71), channel_id=1, source_target_pairs={{0,32},{32,64},{64,96},{96,128},{128,160},{160,192},{192,224},{224... | collective-permute-start | bytes 589832 | tf_op jit(solution)/shard_map/ppermute | solution.py:578
  57.0 8.1 %collective-permute-start.3 = (bf16[384,256]{1,0:T(8,128)(2,1)S(1)}, bf16[384,256]{1,0:T(8,128)(2,1)}, u32[]{:S(2)}, u32[]{:S(2)}) collective-permute-start(bf16[384,256]{1,0:T(8,128)(2,1)S(1)} %slice.82), channel_id=1, source_target_pairs={{0,32},{32,64},{64,96},{96,128},{128,160},{160,192},{192,224},{224... | collective-permute-start | bytes 589832 | tf_op jit(solution)/shard_map/ppermute | solution.py:578
  57.3 7.8 %collective-permute-start.6 = (bf16[384,256]{1,0:T(8,128)(2,1)S(1)}, bf16[384,256]{1,0:T(8,128)(2,1)}, u32[]{:S(2)}, u32[]{:S(2)}) collective-permute-start(bf16[384,256]{1,0:T(8,128)(2,1)S(1)} %slice.83), channel_id=1, source_target_pairs={{0,224},{32,0},{64,32},{96,64},{128,96},{160,128},{192,160},{224,1... | collective-permute-start | bytes 589832 | tf_op jit(solution)/shard_map/ppermute | solution.py:578
  60.6 12.2 %collective-permute-start.15 = (bf16[384,256]{1,0:T(8,128)(2,1)}, bf16[384,256]{1,0:T(8,128)(2,1)S(1)}, u32[]{:S(2)}, u32[]{:S(2)}) collective-permute-start(bf16[384,256]{1,0:T(8,128)(2,1)} %collective-permute-done.14), channel_id=1, source_target_pairs={{0,224},{32,0},{64,32},{96,64},{128,96},{160,128},{192,160},{224,1... | collective-permute-start | bytes 589832 | tf_op jit(solution)/shard_map/ppermute | solution.py:578
  61.2 11.7 %collective-permute-start.13 = (bf16[384,256]{1,0:T(8,128)(2,1)}, bf16[384,256]{1,0:T(8,128)(2,1)S(1)}, u32[]{:S(2)}, u32[]{:S(2)}) collective-permute-start(bf16[384,256]{1,0:T(8,128)(2,1)} %collective-permute-done.12), channel_id=1, source_target_pairs={{0,32},{32,64},{64,96},{96,128},{128,160},{160,192},{192,224},{224... | collective-permute-start | bytes 589832 | tf_op jit(solution)/shard_map/ppermute | solution.py:578
  65.1 7.7 %collective-permute-start.4 = (bf16[384,256]{1,0:T(8,128)(2,1)}, bf16[384,256]{1,0:T(8,128)(2,1)}, u32[]{:S(2)}, u32[]{:S(2)}) collective-permute-start(bf16[384,256]{1,0:T(8,128)(2,1)} %collective-permute-done.3), channel_id=1, source_target_pairs={{0,32},{32,64},{64,96},{96,128},{128,160},{160,192},{192,224},{224... | collective-permute-start | bytes 589832 | tf_op jit(solution)/shard_map/ppermute | solution.py:578
  65.2 7.7 %collective-permute-start.7 = (bf16[384,256]{1,0:T(8,128)(2,1)}, bf16[384,256]{1,0:T(8,128)(2,1)}, u32[]{:S(2)}, u32[]{:S(2)}) collective-permute-start(bf16[384,256]{1,0:T(8,128)(2,1)} %collective-permute-done.6), channel_id=1, source_target_pairs={{0,224},{32,0},{64,32},{96,64},{128,96},{160,128},{192,160},{224,1... | collective-permute-start | bytes 589832 | tf_op jit(solution)/shard_map/ppermute | solution.py:578
  72.9 56.3 %collective-permute-start.16 = (bf16[768,512]{1,0:T(8,128)(2,1)S(1)}, bf16[768,512]{1,0:T(8,128)(2,1)S(1)}, u32[]{:S(2)}, u32[]{:S(2)}) collective-permute-start(bf16[768,512]{1,0:T(8,128)(2,1)S(1)} %copy-done.10), channel_id=1, source_target_pairs={{0,64},{1,65},{2,66},{3,67},{4,68},{5,69},{6,70},{7,71},{8,72},{9,... | collective-permute-start | bytes 2359304 | tf_op jit(solution)/shard_map/ppermute | solution.py:573
  73.0 56.2 %collective-permute-start.17 = (bf16[768,512]{1,0:T(8,128)(2,1)S(1)}, bf16[768,512]{1,0:T(8,128)(2,1)}, u32[]{:S(2)}, u32[]{:S(2)}) collective-permute-start(bf16[768,512]{1,0:T(8,128)(2,1)S(1)} %copy-done.9), channel_id=1, source_target_pairs={{0,32},{1,33},{2,34},{3,35},{4,36},{5,37},{6,38},{7,39},{8,40},{9,... | collective-permute-start | bytes 2359304 | tf_op jit(solution)/shard_map/ppermute | solution.py:573
  96.7 31.6 %all-to-all-start.1 = ((bf16[8,32,256]{2,1,0:T(8,128)(2,1)}), bf16[8,32,256]{2,1,0:T(8,128)(2,1)S(1)}, u32[]{:S(2)}, u32[]{:S(2)}) async-start(bf16[8,32,256]{2,1,0:T(8,128)(2,1)} %get-tuple-element.74), calls=%async_computation.1 | async-start | bytes 262144 | tf_op jit(solution)/shard_map/all_to_all | solution.py:582
  130.1 70.0 %all-to-all-start.2 = ((bf16[32,144,512]{2,1,0:T(8,128)(2,1)}), bf16[32,144,512]{2,1,0:T(8,128)(2,1)}, u32[]{:S(2)}, u32[]{:S(2)}) async-start(bf16[32,144,512]{2,1,0:T(8,128)(2,1)} %broadcast_dynamic-update-slice_fusion), calls=%async_computation.2 | async-start | bytes 9437184 | tf_op jit(solution)/shard_map/all_to_all | solution.py:582
  137.4 34.6 %collective-permute-start.18 = (bf16[768,512]{1,0:T(8,128)(2,1)S(1)}, bf16[768,512]{1,0:T(8,128)(2,1)S(1)}, u32[]{:S(2)}, u32[]{:S(2)}) collective-permute-start(bf16[768,512]{1,0:T(8,128)(2,1)S(1)} %copy-done.8), channel_id=1, source_target_pairs={{0,128},{1,129},{2,130},{3,131},{4,132},{5,133},{6,134},{7,135},{8... | collective-permute-start | bytes 2359304 | tf_op jit(solution)/shard_map/ppermute | solution.py:573
  146.1 29.7 %collective-permute-start.19 = (f32[16,768]{1,0:T(8,128)}, f32[16,768]{1,0:T(8,128)S(1)}, u32[]{:S(2)}, u32[]{:S(2)}) collective-permute-start(f32[16,768]{1,0:T(8,128)} %get-tuple-element.83), channel_id=1, source_target_pairs={{0,128},{1,129},{2,130},{3,131},{4,132},{5,133},{6,134},{7,135},{8... | collective-permute-start | bytes 147464 | tf_op jit(solution)/shard_map/ppermute | solution.py:573
  146.1 36.4 %collective-permute-start.20 = (f32[16,768]{1,0:T(8,128)}, f32[16,768]{1,0:T(8,128)S(1)}, u32[]{:S(2)}, u32[]{:S(2)}) collective-permute-start(f32[16,768]{1,0:T(8,128)} %get-tuple-element.84), channel_id=1, source_target_pairs={{0,64},{1,65},{2,66},{3,67},{4,68},{5,69},{6,70},{7,71},{8,72},{9,... | collective-permute-start | bytes 147464 | tf_op jit(solution)/shard_map/ppermute | solution.py:573
  149.0 33.7 %collective-permute-start.21 = (f32[16,768]{1,0:T(8,128)}, f32[16,768]{1,0:T(8,128)S(1)}, u32[]{:S(2)}, u32[]{:S(2)}) collective-permute-start(f32[16,768]{1,0:T(8,128)} %get-tuple-element.85), channel_id=1, source_target_pairs={{0,32},{1,33},{2,34},{3,35},{4,36},{5,37},{6,38},{7,39},{8,40},{9,... | collective-permute-start | bytes 147464 | tf_op jit(solution)/shard_map/ppermute | solution.py:573
  202.0 18.9 %all-to-all-start.3 = ((f32[8,32,256]{2,1,0:T(8,128)}), f32[8,32,256]{2,1,0:T(8,128)S(1)}, u32[]{:S(2)}, u32[]{:S(2)}) async-start(f32[8,32,256]{2,1,0:T(8,128)} %broadcast_in_dim.2), calls=%async_computation.3 | async-start | bytes 524288 | tf_op jit(solution)/shard_map/all_to_all | solution.py:582
  (13 other events, 86.9 us)

commit v3 on v2

--- a/solution.py
+++ b/solution.py
@@ -10,7 +10,7 @@
 F32, BF16 = jnp.float32, jnp.bfloat16
 LOG2E = 1.4426950408889634
 GATHER, PREPARE, FETCH, FORWARD, BACKWARD, PLACE, COLLECT, FINISH = (
-    round(1.15e9 * us) for us in (0.5, 1, 1, 3, 20, 1, 1, 1)
+    round(1.15e9 * us) for us in (0.5, 1, 1, 3, 14, 1, 1, 1)
 )
 BUFFERS = 2
 ROWS_ACROSS = (((1,), (1,)), ((), ()))
@@ -149,17 +149,30 @@
     ).astype(BF16)
 
 
-def fill_table(table, key_ref, value_ref, halo_ref, sems):
-    blocks = table.shape[0] - halo_ref.shape[0]
-    per, width = table.shape[1], key_ref.shape[1]
-    copies = [
-        pltpu.make_async_copy(halo_ref, table.at[pl.ds(blocks, halo_ref.shape[0])], sems.at[2 * blocks])
-    ]
-    for block in range(blocks):
-        for which, ref in enumerate((key_ref, value_ref)):
-            source = ref.at[pl.ds(block * per, per)]
-            target = table.at[block, :, pl.ds(which * width, width)]
-            copies.append(pltpu.make_async_copy(source, target, sems.at[2 * block + which]))
+def fill_table(table, key_ref, value_ref, halo_ref, sems, half=None):
+    count = halo_ref.shape[0]
+    blocks = table.shape[0] - count
+    per, features = table.shape[1], key_ref.shape[1]
+    width = features if half is None else features // 2
+    first = 0 if half is None else half * width
+    copies = []
+    for which, ref in enumerate((key_ref, value_ref)):
+        target = pl.ds(which * width, width)
+        copies.append(
+            pltpu.make_async_copy(
+                halo_ref.at[:, :, pl.ds(which * features + first, width)],
+                table.at[pl.ds(blocks, count), :, target],
+                sems.at[2 * blocks + which],
+            )
+        )
+        for block in range(blocks):
+            copies.append(
+                pltpu.make_async_copy(
+                    ref.at[pl.ds(block * per, per), pl.ds(first, width)],
+                    table.at[block, :, target],
+                    sems.at[2 * block + which],
+                )
+            )
     for copy in copies:
         copy.start()
     return copies
@@ -287,19 +300,19 @@
 
 
 def backward_kernel(
-    heads, dim, tile_block, tile_count, key_ref, value_ref, halo_ref, query_ref, grad_ref,
+    half, heads, dim, tile_block, tile_count, key_ref, value_ref, halo_ref, query_ref, grad_ref,
     stats_ref, edge_ref, returned_ref, own_terms_ref, query_out,
     table, picked, weights, dscores, terms, packed, sem, out_sems,
 ):
     blocks, slots = tile_count.shape[0], tile_block.shape[0] // tile_count.shape[0]
-    nodes, features = query_ref.shape
+    nodes = query_ref.shape[0]
     per = nodes // blocks
     width = heads * dim
     scale = dim**-0.5
     scale2 = scale * LOG2E
     span = slots // 2 * per
     parts = [slice(0, span), slice(span, 2 * span)]
-    copies = fill_table(table, key_ref, value_ref, halo_ref, sem)
+    copies = fill_table(table, key_ref, value_ref, halo_ref, sem, half)
     terms[...] = jnp.zeros_like(terms)
     for copy in copies:
         copy.wait()
@@ -311,30 +324,29 @@
         for slot in range(slots):
             picked[buffer, slot * per : (slot + 1) * per, :] = table[entries[slot]]
         live_rows = tile_count[step] * per
-        for half in range(2):
-            unit = step * 2 + half
-            place = half
-            keys = slice(half * width, (half + 1) * width)
-            values = slice(features + half * width, features + (half + 1) * width)
-            query_masked = masked_heads(query_ref[at, keys], heads, dim)
-            grad_masked = masked_heads(grad_ref[at, keys], heads, dim)
-            log_total, delta = stats_ref[unit, 0:1, :], stats_ref[unit, 1:2, :]
-            for part in parts:
-                block = dot(picked[buffer, part, keys], query_masked, ROWS_ACROSS)
-                block = live(block, part.start, live_rows)
-                prob = jnp.exp2(block * scale2 - log_total)
-                weights[place, part, :] = prob.astype(BF16)
-                grad_prob = dot(picked[buffer, part, values], grad_masked, ROWS_ACROSS)
-                dscores[place, part, :] = (prob * scale * (grad_prob - delta)).astype(BF16)
-            query_grad = dot(picked[buffer, :, keys], dscores[place], ROWS_DOWN)
-            query_grad = diagonal(query_grad, heads, dim, per) + edge_ref[unit]
-            query_out[at, keys] = query_grad.T
-            key_terms = dot(dscores[place], query_masked)
-            value_terms = dot(weights[place], grad_masked)
-            for slot in range(slots):
-                rows = slice(slot * per, (slot + 1) * per)
-                terms[entries[slot], :, keys] += key_terms[rows]
-                terms[entries[slot], :, values] += value_terms[rows]
+        unit = step * 2 + half
+        place = 0
+        keys = slice(0, width)
+        values = slice(width, 2 * width)
+        query_masked = masked_heads(query_ref[at, :], heads, dim)
+        grad_masked = masked_heads(grad_ref[at, :], heads, dim)
+        log_total, delta = stats_ref[unit, 0:1, :], stats_ref[unit, 1:2, :]
+        for part in parts:
+            block = dot(picked[buffer, part, keys], query_masked, ROWS_ACROSS)
+            block = live(block, part.start, live_rows)
+            prob = jnp.exp2(block * scale2 - log_total)
+            weights[place, part, :] = prob.astype(BF16)
+            grad_prob = dot(picked[buffer, part, values], grad_masked, ROWS_ACROSS)
+            dscores[place, part, :] = (prob * scale * (grad_prob - delta)).astype(BF16)
+        query_grad = dot(picked[buffer, :, keys], dscores[place], ROWS_DOWN)
+        query_grad = diagonal(query_grad, heads, dim, per) + edge_ref[unit]
+        query_out[at, :] = query_grad.T
+        key_terms = dot(dscores[place], query_masked)
+        value_terms = dot(weights[place], grad_masked)
+        for slot in range(slots):
+            rows = slice(slot * per, (slot + 1) * per)
+            terms[entries[slot], :, keys] += key_terms[rows]
+            terms[entries[slot], :, values] += value_terms[rows]
         return 0
 
     lax.fori_loop(0, blocks, block_step, 0)
@@ -403,7 +415,7 @@
             pltpu.VMEM((features, features), F32),
             pltpu.VMEM((nodes, 2 * features), BF16),
             pltpu.VMEM((2 * features, nodes), BF16),
-            pltpu.SemaphoreType.DMA((2 * blocks + 1,)),
+            pltpu.SemaphoreType.DMA((2 * blocks + 2,)),
             pltpu.SemaphoreType.DMA((4,)),
         ],
         FORWARD,
@@ -465,31 +477,32 @@
     return run(place_kernel, (), [(matching, None), (rows, None)], [out] * 3, [], PLACE, "place", 60)
 
 
-def backward(scalars, key_rows, value_rows, halo, query_rows, attended_grad, stats, edge_part, spare, heads):
+def backward(half, scalars, key_rows, value_rows, halo, query_rows, attended_grad, stats, edge_part, spare, heads):
     tile_block, tile_count = scalars
     nodes, features = query_rows.shape
     blocks, slots = tile_count.shape[0], tile_block.shape[0] // tile_count.shape[0]
-    per = nodes // blocks
+    per, width = nodes // blocks, features // 2
     columns = heads // 2 * per
     count = halo.shape[0]
+    part = pl.BlockSpec((nodes, width), lambda *_: (0, half), pipeline_mode=pl.Buffered(1))
     return run(
-        functools.partial(backward_kernel, heads // 2, features // heads),
+        functools.partial(backward_kernel, half, heads // 2, features // heads),
         scalars,
-        [(key_rows, ANYWHERE), (value_rows, ANYWHERE), (halo, ANYWHERE), (query_rows, None)]
-        + [(attended_grad, None), (stats, None), (edge_part, None)],
+        [(key_rows, ANYWHERE), (value_rows, ANYWHERE), (halo, ANYWHERE), (query_rows, part)]
+        + [(attended_grad, part), (stats, None), (edge_part, None)],
         [
-            ((count, per + spare, 2 * features), BF16),
-            ((blocks, per, 2 * features), F32),
-            ((nodes, features), F32),
+            ((count, per + spare, features), BF16),
+            ((blocks, per, features), F32),
+            ((nodes, width), F32),
         ],
         [
-            pltpu.VMEM((blocks + count, per, 2 * features), BF16),
-            pltpu.VMEM((1, slots * per, 2 * features), BF16),
-            pltpu.VMEM((BUFFERS, slots * per, columns), BF16),
-            pltpu.VMEM((BUFFERS, slots * per, columns), BF16),
-            pltpu.VMEM((blocks + count, per, 2 * features), F32),
-            pltpu.VMEM((count, per, 2 * features), BF16),
-            pltpu.SemaphoreType.DMA((2 * blocks + 1,)),
+            pltpu.VMEM((blocks + count, per, features), BF16),
+            pltpu.VMEM((1, slots * per, features), BF16),
+            pltpu.VMEM((1, slots * per, columns), BF16),
+            pltpu.VMEM((1, slots * per, columns), BF16),
+            pltpu.VMEM((blocks + count, per, features), F32),
+            pltpu.VMEM((count, per, features), BF16),
+            pltpu.SemaphoreType.DMA((2 * blocks + 2,)),
             pltpu.SemaphoreType.DMA((9,)),
         ],
         BACKWARD,
@@ -499,16 +512,26 @@
     )
 
 
-def collect_kernel(heads, own_ref, *refs):
+def add_home(send_block, home_ref, key_ref, value_ref, width):
+    per = home_ref.shape[1]
+    for slot in range(home_ref.shape[0]):
+        rows = pl.ds(pl.multiple_of(send_block[slot] * per, per), per)
+        key_ref[rows, :width] += home_ref[slot, :, :width].astype(F32)
+        value_ref[rows, :width] += home_ref[slot, :, width:].astype(F32)
+
+
+def collect_kernel(heads, send_block, own_a, own_b, home_ref, *refs):
     placed, edges = refs[:3], refs[3:6]
     key_ref, value_ref = refs[6:]
-    blocks, per, both = own_ref.shape
-    two = both // 2
+    blocks, per, two = own_a.shape
     width = two // 2
     dim = width // heads
     for block in range(blocks):
-        key_ref[block * per : (block + 1) * per, :] = own_ref[block, :, :two]
-        value_ref[block * per : (block + 1) * per, :] = own_ref[block, :, two:]
+        at = slice(block * per, (block + 1) * per)
+        key_ref[at, :width] = own_a[block, :, :width]
+        key_ref[at, width:] = own_b[block, :, :width]
+        value_ref[at, :width] = own_a[block, :, width:]
+        value_ref[at, width:] = own_b[block, :, width:]
     row = lax.broadcasted_iota(jnp.int32, (4 * heads, two), 0)
     lane = lax.broadcasted_iota(jnp.int32, (4 * heads, two), 1)
     key_row = (lane // width) * (2 * heads) + lax.rem(lane, width) // dim
@@ -522,16 +545,18 @@
         value_term = weight * placed[turn][:, two:].astype(F32)
         key_ref[...] += key_term.astype(BF16).astype(F32)
         value_ref[...] += value_term.astype(BF16).astype(F32)
-
-
-def collect(own, placed, edges, heads):
-    blocks, per, both = own.shape
-    out = ((blocks * per, both // 2), F32)
-    arrays = [own, *placed, *edges]
+    add_home(send_block, home_ref, key_ref, value_ref, width)
+
+
+def collect(send_block, own_a, own_b, home, placed, edges, heads):
+    blocks, per, two = own_a.shape
+    slots = home.shape[0]
+    out = ((blocks * per, two), F32)
+    part = pl.BlockSpec((slots, per, two), lambda *_: (0, 0, 0), pipeline_mode=pl.Buffered(1))
     return run(
         functools.partial(collect_kernel, heads // 2),
-        (),
-        [(array, None) for array in arrays],
+        (send_block,),
+        [(own_a, None), (own_b, None), (home, part)] + [(array, None) for array in (*placed, *edges)],
         [out, out],
         [],
         COLLECT,
@@ -541,31 +566,28 @@
 
 
 def finish_kernel(send_block, home_ref, key_in, value_in, key_ref, value_ref):
-    slots, _, both = home_ref.shape
-    two = both // 2
-    per = home_ref.shape[1]
     key_ref[...] = key_in[...]
     value_ref[...] = value_in[...]
-    for slot in range(slots):
-        start = pl.multiple_of(send_block[slot] * per, per)
-        key_ref[pl.ds(start, per), :] += home_ref[slot, :, :two].astype(F32)
-        value_ref[pl.ds(start, per), :] += home_ref[slot, :, two:].astype(F32)
-
-
-def finish(send_block, home, key_sum, value_sum, per):
-    slots, _, both = home.shape
-    out = (key_sum.shape, F32)
-    part = pl.BlockSpec((slots, per, both), lambda *_: (0, 0, 0), pipeline_mode=pl.Buffered(1))
-    return run(
+    add_home(send_block, home_ref, key_ref, value_ref, key_ref.shape[1])
+
+
+def finish(send_block, home, key_sum, value_sum):
+    nodes, two = key_sum.shape
+    half = pl.BlockSpec((nodes, two // 2), lambda *_: (0, 1), pipeline_mode=pl.Buffered(1))
+    return pl.pallas_call(
         finish_kernel,
-        (send_block,),
-        [(home, part), (key_sum, None), (value_sum, None)],
-        [out, out],
-        [],
-        FINISH,
-        "finish",
-        60,
-    )
+        grid_spec=pltpu.PrefetchScalarGridSpec(
+            num_scalar_prefetch=1,
+            grid=(1,),
+            in_specs=[whole(home.shape), half, half],
+            out_specs=[half, half],
+        ),
+        out_shape=[jax.ShapeDtypeStruct((nodes, two), F32)] * 2,
+        input_output_aliases={2: 0, 3: 1},
+        compiler_params=params(),
+        cost_estimate=cost(FINISH, 1 << 10),
+        name="finish",
+    )(send_block, home, key_sum, value_sum)
 
 
 def from_partner(array, apart):
@@ -576,6 +598,10 @@
 def ahead(array, steps):
     count = lax.axis_size("group")
     return lax.ppermute(array, "group", [(i, (i + steps) % count) for i in range(count)])
+
+
+def across(array, axis, apart):
+    return lax.ppermute(array, axis, [(i, i ^ apart) for i in range(lax.axis_size(axis))])
 
 
 def exchange(array, axis):
@@ -632,26 +658,35 @@
         scalars, expander_bias, halo, fourth, matching[:1], (far_1, far_2), key_rows, value_rows, query_rows,
         attended_grad, grad_update, out_weight,
     )
+    pieces = exchange(pieces, "group")
+    spare = features // groups
+    common = (scalars, key_rows, value_rows, halo, query_rows, attended_grad)
+    back_a, own_a, query_a = backward(0, *common, stats, edge_part, spare, heads)
+    part = pieces.astype(F32).sum(axis=0).astype(BF16)
+    back_a = back_a.at[:, per:, :].set(part[None])
+    back_a, placed[1], placed[2] = lax.optimization_barrier((back_a, placed[1], placed[2]))
+    home_a = exchange(back_a, "dom")
+    back_b, own_b, query_b = backward(1, *common, stats, edge_part, 0, heads)
+    back_b, home_a, edges, placed[0] = lax.optimization_barrier((back_b, home_a, edges, placed[0]))
     edges = place(matching, edges)
     edges = [from_partner(edges[turn], top_bit - 1 - turn) for turn in range(3)]
-    pieces = exchange(pieces, "group")
-    spare = features // 8 // 2
-    back, own, query_grad = backward(
-        scalars, key_rows, value_rows, halo, query_rows, attended_grad, stats, edge_part, spare, heads
-    )
-    part = pieces.astype(F32).sum(axis=0).astype(BF16)
-    part = jnp.concatenate([part[:spare], part[spare:]], axis=1)
-    back = back.at[:, per:, :].set(part[None])
-    back, placed[1], placed[2] = lax.optimization_barrier((back, placed[1], placed[2]))
-    home = exchange(back, "dom")
-    key_sum, value_sum = collect(own, placed, edges, heads)
-    home, key_sum, value_sum = lax.optimization_barrier((home, key_sum, value_sum))
-    key_grad, value_grad = finish(send_block, home, key_sum, value_sum, per)
-
-    summed = home[:, per:, :].astype(F32).sum(axis=0) * (nodes * devices) ** (-0.5)
-    summed = jnp.concatenate([summed[:, :features], summed[:, features:]], axis=0)
-    copies = jnp.broadcast_to(summed[None], (groups,) + summed.shape)
-    weight_grad = exchange(copies, "group").reshape(features, features)
+    home_b = exchange(back_b, "dom")
+    query_grad = jnp.concatenate([query_a, query_b], axis=1)
+
+    weight_grad = home_a[:, per:, :].astype(F32).sum(axis=0) * (nodes * devices) ** (-0.5)
+    apart = 1
+    while apart < groups:
+        other = across(weight_grad, "group", apart)
+        upper = lax.rem(group[0] // apart, 2) == 1
+        weight_grad = jnp.where(
+            upper, jnp.concatenate([other, weight_grad]), jnp.concatenate([weight_grad, other])
+        )
+        apart *= 2
+    key_sum, value_sum = collect(send_block, own_a, own_b, home_a, placed, edges, heads)
+    home_b, key_sum, value_sum, weight_grad, query_grad = lax.optimization_barrier(
+        (home_b, key_sum, value_sum, weight_grad, query_grad)
+    )
+    key_grad, value_grad = finish(send_block, home_b, key_sum, value_sum)
     return (update, query_grad, key_grad, value_grad, weight_grad)
 
 

time: 222 us -> 211 us (0.950)
  waiting for transfers between devices: 71.3 us -> 44.2 us
  starting transfers between devices: 67.4 us -> 76 us
  Pallas kernels: 74.9 us -> 80.5 us
    all_to_all x4, waiting for transfers between devices: 19.1 us -> 0.01 us  [exchange(): return lax.all_to_all(array, axis, split_axis=0, concat_axis=0, tiled=True)]
    ppermute x6, waiting for transfers between devices: 32.3 us -> 22.3 us  [from_partner(): lax.ppermute(array, axes, [(i, i ^ 1 << apart) for i in range(lax.axis_si...]
    ppermute x0 -> x3, starting transfers between devices: none -> 6.82 us  [across(): lax.ppermute(array, axis, [(i, i ^ apart) for i in range(lax.axis_size(ax...]
    pallas_call x0 -> x1, Pallas kernels: none -> 3.67 us  [finish(): pl.pallas_call(finish_kernel, grid_spec=pltpu.PrefetchScalarGridSpec(num_...]
  transfers between devices with their start and end apart: 26 -> 29, of which waited for: 14 -> 11; matrix products, arithmetic and copies ran while one was open for 1% -> 3% of each run, Pallas kernels for 32% -> 35%
where the time goes in v3:
time: 211 us; the launch traced here: 210 us
  Pallas kernels  80.5 us (38%)
  starting transfers between devices  76 us (36%)
  waiting for transfers between devices  44.2 us (21%)
  local copies, waits for them, and re-layouts  5.38 us (3%)
  other arithmetic  2.8 us (1%)
    pallas_call x7, Pallas kernels, run(): pl.pallas_call(kernel, grid_spec=pltpu.PrefetchScalarGridSpec(num_scalar_...  68.4 us
    all_to_all x4, starting transfers between devices, exchange(): return lax.all_to_all(array, axis, split_axis=0, concat_axis=0, tiled=True)  27.9 us
    ppermute x16, starting transfers between devices, ahead(): lax.ppermute(array, 'group', [(i, (i + steps) % count) for i in range(cou...  26.7 us
    ppermute x6, waiting for transfers between devices, from_partner(): lax.ppermute(array, axes, [(i, i ^ 1 << apart) for i in range(lax.axis_si...  22.3 us
    ppermute x16, waiting for transfers between devices, ahead(): lax.ppermute(array, 'group', [(i, (i + steps) % count) for i in range(cou...  20 us
    ppermute x6, starting transfers between devices, from_partner(): lax.ppermute(array, axes, [(i, i ^ 1 << apart) for i in range(lax.axis_si...  14.6 us
    ppermute x3, starting transfers between devices, across(): lax.ppermute(array, axis, [(i, i ^ apart) for i in range(lax.axis_size(ax...  6.82 us
    pallas_call x1, Pallas kernels, prepare(): pl.pallas_call(prepare_kernel, grid=(1,), in_specs=[whole((nodes, width))...  4.28 us
  transfers between devices with their start and end apart: 29, of which 11 were waited for; matrix products, arithmetic and copies ran while one was open for 3% of the time, Pallas kernels for 35%

profile of v3, /device:TPU:8, one launch (start us, length us, event | category | flops | bytes accessed | tf_op | source)
XLA Modules:
  0.0 209.9 jit_solution(1801377188109191781)
XLA Ops:
  0.6 4.1 %gather_out.1 = bf16[32,128,512]{2,1,0:T(8,128)(2,1)} custom-call(s32[32]{0:T(128)} %bitcast.14, bf16[768,256]{1,0:T(8,128)(2,1)} %key_ref.7, bf16[768,256]{1,0:T(8,128)(2,1)} %value_ref.7), custom_call_target="tpu_custom_call" | custom-call | flops 575000000 | bytes 1024 | tf_op jit(solution)/shard_map/gather_out/pallas_call | solution.py:59
  4.8 7.7 %all-to-all-start = ((bf16[32,128,512]{2,1,0:T(8,128)(2,1)}), bf16[32,128,512]{2,1,0:T(8,128)(2,1)}, u32[]{:S(2)}, u32[]{:S(2)}) async-start(bf16[32,128,512]{2,1,0:T(8,128)(2,1)} %gather_out.1), calls=%async_computation | async-start | bytes 8388608 | tf_op jit(solution)/shard_map/all_to_all | solution.py:608
  12.6 5.9 %collective-permute-start.10 = (bf16[768,256]{1,0:T(8,128)(2,1)S(1)}, bf16[768,256]{1,0:T(8,128)(2,1)S(1)}, u32[]{:S(2)}, u32[]{:S(2)}) collective-permute-start(bf16[768,256]{1,0:T(8,128)(2,1)S(1)} %copy-done.5), channel_id=1, source_target_pairs={{0,224},{32,0},{64,32},{96,64},{128,96},{160,128},{192,160},{224,1... | collective-permute-start | bytes 1179656 | tf_op jit(solution)/shard_map/ppermute | solution.py:600
  18.5 3.2 %collective-permute-start.1 = (bf16[768,256]{1,0:T(8,128)(2,1)S(1)}, bf16[768,256]{1,0:T(8,128)(2,1)S(1)}, u32[]{:S(2)}, u32[]{:S(2)}) collective-permute-start(bf16[768,256]{1,0:T(8,128)(2,1)S(1)} %copy-done.4), channel_id=1, source_target_pairs={{0,224},{32,0},{64,32},{96,64},{128,96},{160,128},{192,160},{224,1... | collective-permute-start | bytes 1179656 | tf_op jit(solution)/shard_map/ppermute | solution.py:600
  22.3 5.6 %collective-permute-done.10.v_above = bf16[768,256]{1,0:T(8,128)(2,1)S(1)} collective-permute-done((bf16[768,256]{1,0:T(8,128)(2,1)S(1)}, bf16[768,256]{1,0:T(8,128)(2,1)S(1)}, u32[]{:S(2)}, u32[]{:S(2)}) %collective-permute-start.10) | collective-permute-done | bytes 393248 | tf_op jit(solution)/shard_map/ppermute | solution.py:600
  28.0 3.7 %collective-permute-start.11 = (bf16[768,256]{1,0:T(8,128)(2,1)S(1)}, bf16[768,256]{1,0:T(8,128)(2,1)S(1)}, u32[]{:S(2)}, u32[]{:S(2)}) collective-permute-start(bf16[768,256]{1,0:T(8,128)(2,1)S(1)} %collective-permute-done.10.v_above), channel_id=1, source_target_pairs={{0,224},{32,0},{64,32},{96,64},{128,96},{160,128},{192,160},{224,1... | collective-permute-start | bytes 1179656 | tf_op jit(solution)/shard_map/ppermute | solution.py:600
  31.7 4.3 %prepare.1 = (bf16[768,256]{1,0:T(8,128)(2,1)}, bf16[768,512]{1,0:T(8,128)(2,1)}, bf16[768,512]{1,0:T(8,128)(2,1)}, bf16[768,512]{1,0:T(8,128)(2,1)}) custom-call(bf16[768,256]{1,0:T(8,128)(2,1)} %query_ref.7, bf16[768,256]{1,0:T(8,128)(2,1)} %update_grad_ref.1, bf16[256,256]{1,0:T(8,128)(2,1)} %out_weight.1, s32[3,768]{1,0:T(4,128)} %bitcast.12), custom_call_target="tpu_custom_call" | custom-call | flops 1150000000 | bytes 1024 | tf_op jit(solution)/shard_map/prepare/pallas_call | solution.py:92
  36.4 3.7 %collective-permute-done.k_below = bf16[768,256]{1,0:T(8,128)(2,1)S(1)} collective-permute-done((bf16[768,256]{1,0:T(8,128)(2,1)S(1)}, bf16[768,256]{1,0:T(8,128)(2,1)S(1)}, u32[]{:S(2)}, u32[]{:S(2)}) %collective-permute-start) | collective-permute-done | bytes 393248 | tf_op jit(solution)/shard_map/ppermute | solution.py:600
  40.1 3.2 %collective-permute-start.5 = (bf16[768,256]{1,0:T(8,128)(2,1)S(1)}, bf16[768,256]{1,0:T(8,128)(2,1)S(1)}, u32[]{:S(2)}, u32[]{:S(2)}) collective-permute-start(bf16[768,256]{1,0:T(8,128)(2,1)S(1)} %collective-permute-done.1.k_above), channel_id=1, source_target_pairs={{0,224},{32,0},{64,32},{96,64},{128,96},{160,128},{192,160},{224,1... | collective-permute-start | bytes 1179656 | tf_op jit(solution)/shard_map/ppermute | solution.py:600
  44.0 3.5 %fetch.2.far_2 = bf16[512,768]{1,0:T(8,128)(2,1)} custom-call(s32[1]{0:T(128)} %bitcast.2.group_ref, bf16[768,256]{1,0:T(8,128)(2,1)} %copy-done.18, bf16[768,256]{1,0:T(8,128)(2,1)} %copy-done.17, bf16[768,256]{1,0:T(8,128)(2,1)} %copy-done.20, bf16[768,256]{1,0:T(8,128)(2,1)} %copy-done.19, s32[1,768]{1,0:T(1,128)} %get-tuple-element.112.match_ref), custom_call_target="tpu_custom_call" | custom-call | flops 1150000000 | bytes 1024 | tf_op jit(solution)/shard_map/fetch/pallas_call | solution.py:372
  48.7 2.0 collective-permute-start.12
  50.7 6.3 %collective-permute-done.2.k_below = bf16[768,256]{1,0:T(8,128)(2,1)S(1)} collective-permute-done((bf16[768,256]{1,0:T(8,128)(2,1)S(1)}, bf16[768,256]{1,0:T(8,128)(2,1)S(1)}, u32[]{:S(2)}, u32[]{:S(2)}) %collective-permute-start.2) | collective-permute-done | bytes 393248 | tf_op jit(solution)/shard_map/ppermute | solution.py:600
  57.3 3.3 %collective-permute-start.6 = (bf16[384,256]{1,0:T(8,128)(2,1)S(1)}, bf16[384,256]{1,0:T(8,128)(2,1)}, u32[]{:S(2)}, u32[]{:S(2)}) collective-permute-start(bf16[384,256]{1,0:T(8,128)(2,1)S(1)} %slice.67), channel_id=1, source_target_pairs={{0,224},{32,0},{64,32},{96,64},{128,96},{160,128},{192,160},{224,1... | collective-permute-start | bytes 589832 | tf_op jit(solution)/shard_map/ppermute | solution.py:600
  62.6 2.6 %collective-permute-done.3 = bf16[384,256]{1,0:T(8,128)(2,1)S(1)} collective-permute-done((bf16[384,256]{1,0:T(8,128)(2,1)S(1)}, bf16[384,256]{1,0:T(8,128)(2,1)S(1)}, u32[]{:S(2)}, u32[]{:S(2)}) %collective-permute-start.3) | collective-permute-done | bytes 196640 | tf_op jit(solution)/shard_map/ppermute | solution.py:600
  65.2 3.3 %collective-permute-start.7 = (bf16[384,256]{1,0:T(8,128)(2,1)}, bf16[384,256]{1,0:T(8,128)(2,1)}, u32[]{:S(2)}, u32[]{:S(2)}) collective-permute-start(bf16[384,256]{1,0:T(8,128)(2,1)} %collective-permute-done.6), channel_id=1, source_target_pairs={{0,224},{32,0},{64,32},{96,64},{128,96},{160,128},{192,160},{224,1... | collective-permute-start | bytes 589832 | tf_op jit(solution)/shard_map/ppermute | solution.py:600
  69.2 3.5 %fetch.3.far_1 = bf16[512,768]{1,0:T(8,128)(2,1)} custom-call(s32[1]{0:T(128)} %bitcast.2.group_ref, bf16[768,256]{1,0:T(8,128)(2,1)} %copy-done.9, bf16[768,256]{1,0:T(8,128)(2,1)} %copy-done.10, bf16[768,256]{1,0:T(8,128)(2,1)} %copy-done.8, bf16[768,256]{1,0:T(8,128)(2,1)} %copy-done.7, s32[1,768]{1,0:T(1,128)} %get-tuple-element.113.match_ref), custom_call_target="tpu_custom_call" | custom-call | flops 1150000000 | bytes 1024 | tf_op jit(solution)/shard_map/fetch/pallas_call | solution.py:372
  75.6 21.1 %forward.1 = (bf16[768,256]{1,0:T(8,128)(2,1)}, bf16[8,32,256]{2,1,0:T(8,128)(2,1)}, f32[12,8,512]{2,1,0:T(8,128)}, f32[12,128,128]{2,1,0:T(8,128)}, f32[3,16,768]{2,1,0:T(8,128)}) custom-call(s32[48]{0:T(128)} %reshape_squeeze.3.tile_block, s32[6]{0:T(128)} %bitcast.17, f32[8]{0:T(128)} %bias_ref.1, bf16[32,128,512]{2,1,0:T(8,128)(2,1)} %all-to-all-done.halo_ref, ...), custom_call_target="tpu_custom_call" | custom-call | flops 3449999872 | bytes 1024 | tf_op jit(solution)/shard_map/forward/pallas_call | solution.py:372
  96.6 5.3 %all-to-all-start.1 = ((bf16[8,32,256]{2,1,0:T(8,128)(2,1)}), bf16[8,32,256]{2,1,0:T(8,128)(2,1)S(1)}, u32[]{:S(2)}, u32[]{:S(2)}) async-start(bf16[8,32,256]{2,1,0:T(8,128)(2,1)} %get-tuple-element.83), calls=%async_computation.1 | async-start | bytes 262144 | tf_op jit(solution)/shard_map/all_to_all | solution.py:608
  101.9 16.0 %backward.3 = (bf16[32,160,256]{2,1,0:T(8,128)(2,1)}, f32[6,128,256]{2,1,0:T(8,128)}, f32[768,128]{1,0:T(8,128)}) custom-call(s32[48]{0:T(128)} %reshape_squeeze.3.tile_block, s32[6]{0:T(128)} %bitcast.18, bf16[768,256]{1,0:T(8,128)(2,1)} %key_ref.7, bf16[768,256]{1,0:T(8,128)(2,1)} %value_ref.7, bf16[32,128,512]{2,1,0:T(8,128)(2,1)} %all-to-all-done.halo_ref, ...), custom_call_target="tpu_custom_call" | custom-call | flops 16099999744 | bytes 1024 | tf_op jit(solution)/shard_map/backward/pallas_call | solution.py:372
  120.0 7.4 %all-to-all-start.2 = ((bf16[32,160,256]{2,1,0:T(8,128)(2,1)}), bf16[32,160,256]{2,1,0:T(8,128)(2,1)S(1)}, u32[]{:S(2)}, u32[]{:S(2)}) async-start(bf16[32,160,256]{2,1,0:T(8,128)(2,1)} %broadcast_dynamic-update-slice_fusion), calls=%async_computation.2 | async-start | bytes 5242880 | tf_op jit(solution)/shard_map/all_to_all | solution.py:608
  127.5 6.0 %collective-permute-start.18 = (bf16[768,512]{1,0:T(8,128)(2,1)}, bf16[768,512]{1,0:T(8,128)(2,1)S(1)}, u32[]{:S(2)}, u32[]{:S(2)}) collective-permute-start(bf16[768,512]{1,0:T(8,128)(2,1)} %get-tuple-element.88), channel_id=1, source_target_pairs={{0,128},{1,129},{2,130},{3,131},{4,132},{5,133},{6,134},{7,135},{8... | collective-permute-start | bytes 2359304 | tf_op jit(solution)/shard_map/ppermute | solution.py:595
  133.5 15.9 %backward.2 = (bf16[32,128,256]{2,1,0:T(8,128)(2,1)}, f32[6,128,256]{2,1,0:T(8,128)}, f32[768,128]{1,0:T(8,128)}) custom-call(s32[48]{0:T(128)} %reshape_squeeze.3.tile_block, s32[6]{0:T(128)} %bitcast.19, bf16[768,256]{1,0:T(8,128)(2,1)} %key_ref.7, bf16[768,256]{1,0:T(8,128)(2,1)} %value_ref.7, bf16[32,128,512]{2,1,0:T(8,128)(2,1)} %all-to-all-done.halo_ref, ...), custom_call_target="tpu_custom_call" | custom-call | flops 16099999744 | bytes 1024 | tf_op jit(solution)/shard_map/backward/pallas_call | solution.py:372
  149.4 18.5 %collective-permute-done.18.refs_0_ = bf16[768,512]{1,0:T(8,128)(2,1)S(1)} collective-permute-done((bf16[768,512]{1,0:T(8,128)(2,1)}, bf16[768,512]{1,0:T(8,128)(2,1)S(1)}, u32[]{:S(2)}, u32[]{:S(2)}) %collective-permute-start.18) | collective-permute-done | bytes 786464 | tf_op jit(solution)/shard_map/ppermute | solution.py:595
  167.9 7.4 %all-to-all-start.3 = ((bf16[32,128,256]{2,1,0:T(8,128)(2,1)}), bf16[32,128,256]{2,1,0:T(8,128)(2,1)}, u32[]{:S(2)}, u32[]{:S(2)}) async-start(bf16[32,128,256]{2,1,0:T(8,128)(2,1)} %get-tuple-element.89), calls=%async_computation.3 | async-start | bytes 4194304 | tf_op jit(solution)/shard_map/all_to_all | solution.py:608
  175.5 2.3 %collective-permute-start.22 = (f32[32,256]{1,0:T(8,128)S(1)}, f32[32,256]{1,0:T(8,128)S(1)}, u32[]{:S(2)}, u32[]{:S(2)}) collective-permute-start(f32[32,256]{1,0:T(8,128)S(1)} %broadcast_multiply_fusion), channel_id=1, source_target_pairs={{0,32},{32,0},{64,96},{96,64},{128,160},{160,128},{192,224},{224,1... | collective-permute-start | bytes 98312 | tf_op jit(solution)/shard_map/ppermute | solution.py:604
  179.7 2.9 %collective-permute-start.23 = (f32[64,256]{1,0:T(8,128)S(1)}, f32[64,256]{1,0:T(8,128)S(1)}, u32[]{:S(2)}, u32[]{:S(2)}) collective-permute-start(f32[64,256]{1,0:T(8,128)S(1)} %maximum_select_fusion.2), channel_id=1, source_target_pairs={{0,64},{32,96},{64,0},{96,32},{128,192},{160,224},{192,128},{224,1... | collective-permute-start | bytes 196616 | tf_op jit(solution)/shard_map/ppermute | solution.py:604
  182.6 2.6 %place.1 = (f32[16,768]{1,0:T(8,128)}, f32[16,768]{1,0:T(8,128)}, f32[16,768]{1,0:T(8,128)}) custom-call(s32[3,768]{1,0:T(4,128)} %bitcast.13, f32[3,16,768]{2,1,0:T(8,128)} %get-tuple-element.96.rows_ref), custom_call_target="tpu_custom_call" | custom-call | flops 1150000000 | bytes 1024 | tf_op jit(solution)/shard_map/place/pallas_call | solution.py:372
  185.2 3.4 %collective-permute-start.19 = (f32[16,768]{1,0:T(8,128)}, f32[16,768]{1,0:T(8,128)S(1)}, u32[]{:S(2)}, u32[]{:S(2)}) collective-permute-start(f32[16,768]{1,0:T(8,128)} %get-tuple-element.97), channel_id=1, source_target_pairs={{0,128},{1,129},{2,130},{3,131},{4,132},{5,133},{6,134},{7,135},{8... | collective-permute-start | bytes 147464 | tf_op jit(solution)/shard_map/ppermute | solution.py:595
  188.6 2.8 %collective-permute-start.20 = (f32[16,768]{1,0:T(8,128)}, f32[16,768]{1,0:T(8,128)S(1)}, u32[]{:S(2)}, u32[]{:S(2)}) collective-permute-start(f32[16,768]{1,0:T(8,128)} %get-tuple-element.98), channel_id=1, source_target_pairs={{0,64},{1,65},{2,66},{3,67},{4,68},{5,69},{6,70},{7,71},{8,72},{9,... | collective-permute-start | bytes 147464 | tf_op jit(solution)/shard_map/ppermute | solution.py:595
  195.9 3.3 %collective-permute-done.21.refs_5_ = f32[16,768]{1,0:T(8,128)S(1)} collective-permute-done((f32[16,768]{1,0:T(8,128)}, f32[16,768]{1,0:T(8,128)S(1)}, u32[]{:S(2)}, u32[]{:S(2)}) %collective-permute-start.21) | collective-permute-done | bytes 49184 | tf_op jit(solution)/shard_map/ppermute | solution.py:595
  199.8 5.8 %collect.1 = (f32[768,256]{1,0:T(8,128)}, f32[768,256]{1,0:T(8,128)}) custom-call(s32[32]{0:T(128)} %bitcast.15, f32[6,128,256]{2,1,0:T(8,128)} %get-tuple-element.90.own_a, f32[6,128,256]{2,1,0:T(8,128)} %get-tuple-element.91.own_b, bf16[32,160,256]{2,1,0:T(8,128)(2,1)} %copy-done, bf16[768,512]{1,0:T(8,128)(2,1)} %copy-done.3, bf16[768,512]{1,0:T(8,128)(2,1)} %copy-done.1, ...), custom_call_target="tpu_custom_call" | custom-call | flops 1150000000 | bytes 1024 | tf_op jit(solution)/shard_map/collect/pallas_call | solution.py:372
  206.3 3.7 %finish.1 = (f32[768,256]{1,0:T(8,128)}, f32[768,256]{1,0:T(8,128)}) custom-call(s32[32]{0:T(128)} %bitcast.16, bf16[32,128,256]{2,1,0:T(8,128)(2,1)} %all-to-all-done.3.home_ref, f32[768,256]{1,0:T(8,128)} %get-tuple-element.106.key_in, f32[768,256]{1,0:T(8,128)} %get-tuple-element.107.value_in), custom_call_target="tpu_custom_call", output_to_operand_aliasing={{0}: (2, {}), {1}: (3, {})} | custom-call | flops 1150000000 | bytes 1024 | tf_op jit(solution)/shard_map/finish/pallas_call | solution.py:577
  (100 shorter events, 18.4 us)
Async XLA Ops:
  4.8 70.7 %all-to-all-start = ((bf16[32,128,512]{2,1,0:T(8,128)(2,1)}), bf16[32,128,512]{2,1,0:T(8,128)(2,1)}, u32[]{:S(2)}, u32[]{:S(2)}) async-start(bf16[32,128,512]{2,1,0:T(8,128)(2,1)} %gather_out.1), calls=%async_computation | async-start | bytes 8388608 | tf_op jit(solution)/shard_map/all_to_all | solution.py:608
  12.6 15.4 %collective-permute-start.10 = (bf16[768,256]{1,0:T(8,128)(2,1)S(1)}, bf16[768,256]{1,0:T(8,128)(2,1)S(1)}, u32[]{:S(2)}, u32[]{:S(2)}) collective-permute-start(bf16[768,256]{1,0:T(8,128)(2,1)S(1)} %copy-done.5), channel_id=1, source_target_pairs={{0,224},{32,0},{64,32},{96,64},{128,96},{160,128},{192,160},{224,1... | collective-permute-start | bytes 1179656 | tf_op jit(solution)/shard_map/ppermute | solution.py:600
  18.5 13.2 %collective-permute-start.8 = (bf16[768,256]{1,0:T(8,128)(2,1)S(1)}, bf16[768,256]{1,0:T(8,128)(2,1)S(1)}, u32[]{:S(2)}, u32[]{:S(2)}) collective-permute-start(bf16[768,256]{1,0:T(8,128)(2,1)S(1)} %copy-done.5), channel_id=1, source_target_pairs={{0,32},{32,64},{64,96},{96,128},{128,160},{160,192},{192,224},{224... | collective-permute-start | bytes 1179656 | tf_op jit(solution)/shard_map/ppermute | solution.py:600
  18.5 17.9 %collective-permute-start.1 = (bf16[768,256]{1,0:T(8,128)(2,1)S(1)}, bf16[768,256]{1,0:T(8,128)(2,1)S(1)}, u32[]{:S(2)}, u32[]{:S(2)}) collective-permute-start(bf16[768,256]{1,0:T(8,128)(2,1)S(1)} %copy-done.4), channel_id=1, source_target_pairs={{0,224},{32,0},{64,32},{96,64},{128,96},{160,128},{192,160},{224,1... | collective-permute-start | bytes 1179656 | tf_op jit(solution)/shard_map/ppermute | solution.py:600
  21.7 18.4 %collective-permute-start = (bf16[768,256]{1,0:T(8,128)(2,1)S(1)}, bf16[768,256]{1,0:T(8,128)(2,1)S(1)}, u32[]{:S(2)}, u32[]{:S(2)}) collective-permute-start(bf16[768,256]{1,0:T(8,128)(2,1)S(1)} %copy-done.4), channel_id=1, source_target_pairs={{0,32},{32,64},{64,96},{96,128},{128,160},{160,192},{192,224},{224... | collective-permute-start | bytes 1179656 | tf_op jit(solution)/shard_map/ppermute | solution.py:600
  28.0 19.6 %collective-permute-start.11 = (bf16[768,256]{1,0:T(8,128)(2,1)S(1)}, bf16[768,256]{1,0:T(8,128)(2,1)S(1)}, u32[]{:S(2)}, u32[]{:S(2)}) collective-permute-start(bf16[768,256]{1,0:T(8,128)(2,1)S(1)} %collective-permute-done.10.v_above), channel_id=1, source_target_pairs={{0,224},{32,0},{64,32},{96,64},{128,96},{160,128},{192,160},{224,1... | collective-permute-start | bytes 1179656 | tf_op jit(solution)/shard_map/ppermute | solution.py:600
  31.7 16.9 %collective-permute-start.9 = (bf16[768,256]{1,0:T(8,128)(2,1)S(1)}, bf16[768,256]{1,0:T(8,128)(2,1)S(1)}, u32[]{:S(2)}, u32[]{:S(2)}) collective-permute-start(bf16[768,256]{1,0:T(8,128)(2,1)S(1)} %collective-permute-done.8.v_below), channel_id=1, source_target_pairs={{0,32},{32,64},{64,96},{96,128},{128,160},{160,192},{192,224},{224... | collective-permute-start | bytes 1179656 | tf_op jit(solution)/shard_map/ppermute | solution.py:600
  40.1 16.9 %collective-permute-start.2 = (bf16[768,256]{1,0:T(8,128)(2,1)S(1)}, bf16[768,256]{1,0:T(8,128)(2,1)S(1)}, u32[]{:S(2)}, u32[]{:S(2)}) collective-permute-start(bf16[768,256]{1,0:T(8,128)(2,1)S(1)} %collective-permute-done.k_below), channel_id=1, source_target_pairs={{0,32},{32,64},{64,96},{96,128},{128,160},{160,192},{192,224},{224... | collective-permute-start | bytes 1179656 | tf_op jit(solution)/shard_map/ppermute | solution.py:600
  40.1 17.1 %collective-permute-start.5 = (bf16[768,256]{1,0:T(8,128)(2,1)S(1)}, bf16[768,256]{1,0:T(8,128)(2,1)S(1)}, u32[]{:S(2)}, u32[]{:S(2)}) collective-permute-start(bf16[768,256]{1,0:T(8,128)(2,1)S(1)} %collective-permute-done.1.k_above), channel_id=1, source_target_pairs={{0,224},{32,0},{64,32},{96,64},{128,96},{160,128},{192,160},{224,1... | collective-permute-start | bytes 1179656 | tf_op jit(solution)/shard_map/ppermute | solution.py:600
  44.0 24.6 %copy-start.15 = (s32[1,6,8]{2,0,1:T(1,128)S(1)}, s32[1,6,8]{2,0,1:T(1,128)}, u32[]{:S(2)}) copy-start(s32[1,6,8]{2,0,1:T(1,128)} %param.18) | copy-start | bytes 580
  47.6 21.6 %copy-start.7 = (bf16[768,256]{1,0:T(8,128)(2,1)}, bf16[768,256]{1,0:T(8,128)(2,1)S(1)}, u32[]{:S(2)}) copy-start(bf16[768,256]{1,0:T(8,128)(2,1)S(1)} %collective-permute-done.11.v_above) | copy-start | bytes 1179652
  48.6 25.0 %copy-start.16 = (bf16[768,512]{1,0:T(8,128)(2,1)S(1)}, bf16[768,512]{1,0:T(8,128)(2,1)}, u32[]{:S(2)}) copy-start(bf16[768,512]{1,0:T(8,128)(2,1)} %get-tuple-element.85) | copy-start | bytes 2359300
  48.6 12.0 %collective-permute-start.14 = (bf16[384,256]{1,0:T(8,128)(2,1)S(1)}, bf16[384,256]{1,0:T(8,128)(2,1)S(1)}, u32[]{:S(2)}, u32[]{:S(2)}) collective-permute-start(bf16[384,256]{1,0:T(8,128)(2,1)S(1)} %slice.60), channel_id=1, source_target_pairs={{0,224},{32,0},{64,32},{96,64},{128,96},{160,128},{192,160},{224,1... | collective-permute-start | bytes 589832 | tf_op jit(solution)/shard_map/ppermute | solution.py:600
  48.7 12.3 %collective-permute-start.12 = (bf16[384,256]{1,0:T(8,128)(2,1)S(1)}, bf16[384,256]{1,0:T(8,128)(2,1)S(1)}, u32[]{:S(2)}, u32[]{:S(2)}) collective-permute-start(bf16[384,256]{1,0:T(8,128)(2,1)S(1)} %slice.59), channel_id=1, source_target_pairs={{0,32},{32,64},{64,96},{96,128},{128,160},{160,192},{192,224},{224... | collective-permute-start | bytes 589832 | tf_op jit(solution)/shard_map/ppermute | solution.py:600
  57.0 8.2 %collective-permute-start.3 = (bf16[384,256]{1,0:T(8,128)(2,1)S(1)}, bf16[384,256]{1,0:T(8,128)(2,1)S(1)}, u32[]{:S(2)}, u32[]{:S(2)}) collective-permute-start(bf16[384,256]{1,0:T(8,128)(2,1)S(1)} %slice.66), channel_id=1, source_target_pairs={{0,32},{32,64},{64,96},{96,128},{128,160},{160,192},{192,224},{224... | collective-permute-start | bytes 589832 | tf_op jit(solution)/shard_map/ppermute | solution.py:600
  57.3 7.9 %collective-permute-start.6 = (bf16[384,256]{1,0:T(8,128)(2,1)S(1)}, bf16[384,256]{1,0:T(8,128)(2,1)}, u32[]{:S(2)}, u32[]{:S(2)}) collective-permute-start(bf16[384,256]{1,0:T(8,128)(2,1)S(1)} %slice.67), channel_id=1, source_target_pairs={{0,224},{32,0},{64,32},{96,64},{128,96},{160,128},{192,160},{224,1... | collective-permute-start | bytes 589832 | tf_op jit(solution)/shard_map/ppermute | solution.py:600
  60.6 12.2 %collective-permute-start.15 = (bf16[384,256]{1,0:T(8,128)(2,1)S(1)}, bf16[384,256]{1,0:T(8,128)(2,1)S(1)}, u32[]{:S(2)}, u32[]{:S(2)}) collective-permute-start(bf16[384,256]{1,0:T(8,128)(2,1)S(1)} %collective-permute-done.14), channel_id=1, source_target_pairs={{0,224},{32,0},{64,32},{96,64},{128,96},{160,128},{192,160},{224,1... | collective-permute-start | bytes 589832 | tf_op jit(solution)/shard_map/ppermute | solution.py:600
  61.0 11.7 %collective-permute-start.13 = (bf16[384,256]{1,0:T(8,128)(2,1)S(1)}, bf16[384,256]{1,0:T(8,128)(2,1)S(1)}, u32[]{:S(2)}, u32[]{:S(2)}) collective-permute-start(bf16[384,256]{1,0:T(8,128)(2,1)S(1)} %collective-permute-done.12), channel_id=1, source_target_pairs={{0,32},{32,64},{64,96},{96,128},{128,160},{160,192},{192,224},{224... | collective-permute-start | bytes 589832 | tf_op jit(solution)/shard_map/ppermute | solution.py:600
  65.2 7.6 %collective-permute-start.4 = (bf16[384,256]{1,0:T(8,128)(2,1)S(1)}, bf16[384,256]{1,0:T(8,128)(2,1)S(1)}, u32[]{:S(2)}, u32[]{:S(2)}) collective-permute-start(bf16[384,256]{1,0:T(8,128)(2,1)S(1)} %collective-permute-done.3), channel_id=1, source_target_pairs={{0,32},{32,64},{64,96},{96,128},{128,160},{160,192},{192,224},{224... | collective-permute-start | bytes 589832 | tf_op jit(solution)/shard_map/ppermute | solution.py:600
  65.2 7.6 %collective-permute-start.7 = (bf16[384,256]{1,0:T(8,128)(2,1)}, bf16[384,256]{1,0:T(8,128)(2,1)}, u32[]{:S(2)}, u32[]{:S(2)}) collective-permute-start(bf16[384,256]{1,0:T(8,128)(2,1)} %collective-permute-done.6), channel_id=1, source_target_pairs={{0,224},{32,0},{64,32},{96,64},{128,96},{160,128},{192,160},{224,1... | collective-permute-start | bytes 589832 | tf_op jit(solution)/shard_map/ppermute | solution.py:600
  73.6 45.3 %collective-permute-start.16 = (bf16[768,512]{1,0:T(8,128)(2,1)}, bf16[768,512]{1,0:T(8,128)(2,1)S(1)}, u32[]{:S(2)}, u32[]{:S(2)}) collective-permute-start(bf16[768,512]{1,0:T(8,128)(2,1)} %get-tuple-element.84), channel_id=1, source_target_pairs={{0,64},{1,65},{2,66},{3,67},{4,68},{5,69},{6,70},{7,71},{8,72},{9,... | collective-permute-start | bytes 2359304 | tf_op jit(solution)/shard_map/ppermute | solution.py:595
  73.6 45.3 %collective-permute-start.17 = (bf16[768,512]{1,0:T(8,128)(2,1)S(1)}, bf16[768,512]{1,0:T(8,128)(2,1)S(1)}, u32[]{:S(2)}, u32[]{:S(2)}) collective-permute-start(bf16[768,512]{1,0:T(8,128)(2,1)S(1)} %copy-done.16), channel_id=1, source_target_pairs={{0,32},{1,33},{2,34},{3,35},{4,36},{5,37},{6,38},{7,39},{8,40},{9,... | collective-permute-start | bytes 2359304 | tf_op jit(solution)/shard_map/ppermute | solution.py:595
  96.6 21.3 %all-to-all-start.1 = ((bf16[8,32,256]{2,1,0:T(8,128)(2,1)}), bf16[8,32,256]{2,1,0:T(8,128)(2,1)S(1)}, u32[]{:S(2)}, u32[]{:S(2)}) async-start(bf16[8,32,256]{2,1,0:T(8,128)(2,1)} %get-tuple-element.83), calls=%async_computation.1 | async-start | bytes 262144 | tf_op jit(solution)/shard_map/all_to_all | solution.py:608
  120.0 47.9 %all-to-all-start.2 = ((bf16[32,160,256]{2,1,0:T(8,128)(2,1)}), bf16[32,160,256]{2,1,0:T(8,128)(2,1)S(1)}, u32[]{:S(2)}, u32[]{:S(2)}) async-start(bf16[32,160,256]{2,1,0:T(8,128)(2,1)} %broadcast_dynamic-update-slice_fusion), calls=%async_computation.2 | async-start | bytes 5242880 | tf_op jit(solution)/shard_map/all_to_all | solution.py:608
  127.5 40.5 %collective-permute-start.18 = (bf16[768,512]{1,0:T(8,128)(2,1)}, bf16[768,512]{1,0:T(8,128)(2,1)S(1)}, u32[]{:S(2)}, u32[]{:S(2)}) collective-permute-start(bf16[768,512]{1,0:T(8,128)(2,1)} %get-tuple-element.88), channel_id=1, source_target_pairs={{0,128},{1,129},{2,130},{3,131},{4,132},{5,133},{6,134},{7,135},{8... | collective-permute-start | bytes 2359304 | tf_op jit(solution)/shard_map/ppermute | solution.py:595
  167.9 38.3 %all-to-all-start.3 = ((bf16[32,128,256]{2,1,0:T(8,128)(2,1)}), bf16[32,128,256]{2,1,0:T(8,128)(2,1)}, u32[]{:S(2)}, u32[]{:S(2)}) async-start(bf16[32,128,256]{2,1,0:T(8,128)(2,1)} %get-tuple-element.89), calls=%async_computation.3 | async-start | bytes 4194304 | tf_op jit(solution)/shard_map/all_to_all | solution.py:608
  175.5 4.2 %collective-permute-start.22 = (f32[32,256]{1,0:T(8,128)S(1)}, f32[32,256]{1,0:T(8,128)S(1)}, u32[]{:S(2)}, u32[]{:S(2)}) collective-permute-start(f32[32,256]{1,0:T(8,128)S(1)} %broadcast_multiply_fusion), channel_id=1, source_target_pairs={{0,32},{32,0},{64,96},{96,64},{128,160},{160,128},{192,224},{224,1... | collective-permute-start | bytes 98312 | tf_op jit(solution)/shard_map/ppermute | solution.py:604
  179.7 12.1 %collective-permute-start.23 = (f32[64,256]{1,0:T(8,128)S(1)}, f32[64,256]{1,0:T(8,128)S(1)}, u32[]{:S(2)}, u32[]{:S(2)}) collective-permute-start(f32[64,256]{1,0:T(8,128)S(1)} %maximum_select_fusion.2), channel_id=1, source_target_pairs={{0,64},{32,96},{64,0},{96,32},{128,192},{160,224},{192,128},{224,1... | collective-permute-start | bytes 196616 | tf_op jit(solution)/shard_map/ppermute | solution.py:604
  185.2 10.1 %collective-permute-start.19 = (f32[16,768]{1,0:T(8,128)}, f32[16,768]{1,0:T(8,128)S(1)}, u32[]{:S(2)}, u32[]{:S(2)}) collective-permute-start(f32[16,768]{1,0:T(8,128)} %get-tuple-element.97), channel_id=1, source_target_pairs={{0,128},{1,129},{2,130},{3,131},{4,132},{5,133},{6,134},{7,135},{8... | collective-permute-start | bytes 147464 | tf_op jit(solution)/shard_map/ppermute | solution.py:595
  188.6 7.2 %collective-permute-start.20 = (f32[16,768]{1,0:T(8,128)}, f32[16,768]{1,0:T(8,128)S(1)}, u32[]{:S(2)}, u32[]{:S(2)}) collective-permute-start(f32[16,768]{1,0:T(8,128)} %get-tuple-element.98), channel_id=1, source_target_pairs={{0,64},{1,65},{2,66},{3,67},{4,68},{5,69},{6,70},{7,71},{8,72},{9,... | collective-permute-start | bytes 147464 | tf_op jit(solution)/shard_map/ppermute | solution.py:595
  191.4 7.7 %collective-permute-start.21 = (f32[16,768]{1,0:T(8,128)}, f32[16,768]{1,0:T(8,128)S(1)}, u32[]{:S(2)}, u32[]{:S(2)}) collective-permute-start(f32[16,768]{1,0:T(8,128)} %get-tuple-element.99), channel_id=1, source_target_pairs={{0,32},{1,33},{2,34},{3,35},{4,36},{5,37},{6,38},{7,39},{8,40},{9,... | collective-permute-start | bytes 147464 | tf_op jit(solution)/shard_map/ppermute | solution.py:595
  191.8 13.7 %collective-permute-start.24 = (f32[128,256]{1,0:T(8,128)S(1)}, f32[128,256]{1,0:T(8,128)S(1)}, u32[]{:S(2)}, u32[]{:S(2)}) collective-permute-start(f32[128,256]{1,0:T(8,128)S(1)} %maximum_select_fusion.1), channel_id=1, source_target_pairs={{0,128},{32,160},{64,192},{96,224},{128,0},{160,32},{192,64},{224,... | collective-permute-start | bytes 393224 | tf_op jit(solution)/shard_map/ppermute | solution.py:604
  (21 other events, 187.2 us)

commit v4 on v3

--- a/solution.py
+++ b/solution.py
@@ -647,9 +647,7 @@
     third = [(ahead(below[:half], 1), ahead(above[half:], -1)) for below, above in next_near]
     fourth = [(ahead(below, 1), ahead(above, -1)) for below, above in third]
     far_1 = found(1, 2, next_near)
-    fourth, far_1, placed[1], placed[2] = lax.optimization_barrier(
-        (fourth, far_1, placed[1], placed[2])
-    )
+    fourth, far_1, placed[0] = lax.optimization_barrier((fourth, far_1, placed[0]))
     placed = [from_partner(placed[turn], top_bit - 1 - turn) for turn in range(3)]
     fourth = [rows for pair in fourth for rows in pair]
 
@@ -664,11 +662,13 @@
     back_a, own_a, query_a = backward(0, *common, stats, edge_part, spare, heads)
     part = pieces.astype(F32).sum(axis=0).astype(BF16)
     back_a = back_a.at[:, per:, :].set(part[None])
-    back_a, placed[1], placed[2] = lax.optimization_barrier((back_a, placed[1], placed[2]))
+    back_a, placed[0] = lax.optimization_barrier((back_a, placed[0]))
     home_a = exchange(back_a, "dom")
     back_b, own_b, query_b = backward(1, *common, stats, edge_part, 0, heads)
-    back_b, home_a, edges, placed[0] = lax.optimization_barrier((back_b, home_a, edges, placed[0]))
     edges = place(matching, edges)
+    back_b, home_a, placed[1], placed[2], *edges = lax.optimization_barrier(
+        (back_b, home_a, placed[1], placed[2], *edges)
+    )
     edges = [from_partner(edges[turn], top_bit - 1 - turn) for turn in range(3)]
     home_b = exchange(back_b, "dom")
     query_grad = jnp.concatenate([query_a, query_b], axis=1)

time: 211 us -> 207 us (0.981)
  waiting for transfers between devices: 44.2 us -> 38 us
    ppermute x6, waiting for transfers between devices: 22.3 us -> 15.5 us  [from_partner(): lax.ppermute(array, axes, [(i, i ^ 1 << apart) for i in range(lax.axis_si...]
  transfers between devices with their start and end apart: 29 -> 29, of which waited for: 11 -> 12; matrix products, arithmetic and copies ran while one was open for 3% -> 3% of each run, Pallas kernels for 35% -> 36%
where the time goes in v4:
time: 207 us; the launch traced here: 204 us
  Pallas kernels  80.5 us (39%)
  starting transfers between devices  76.7 us (37%)
  waiting for transfers between devices  38 us (18%)
  local copies, waits for them, and re-layouts  5.08 us (2%)
  other arithmetic  2.92 us (1%)
    pallas_call x7, Pallas kernels, run(): pl.pallas_call(kernel, grid_spec=pltpu.PrefetchScalarGridSpec(num_scalar_...  68.4 us
    all_to_all x4, starting transfers between devices, exchange(): return lax.all_to_all(array, axis, split_axis=0, concat_axis=0, tiled=True)  28 us
    ppermute x16, starting transfers between devices, ahead(): lax.ppermute(array, 'group', [(i, (i + steps) % count) for i in range(cou...  26.7 us
    ppermute x16, waiting for transfers between devices, ahead(): lax.ppermute(array, 'group', [(i, (i + steps) % count) for i in range(cou...  20.1 us
    ppermute x6, waiting for transfers between devices, from_partner(): lax.ppermute(array, axes, [(i, i ^ 1 << apart) for i in range(lax.axis_si...  15.5 us
    ppermute x6, starting transfers between devices, from_partner(): lax.ppermute(array, axes, [(i, i ^ 1 << apart) for i in range(lax.axis_si...  13.1 us
    ppermute x3, starting transfers between devices, across(): lax.ppermute(array, axis, [(i, i ^ apart) for i in range(lax.axis_size(ax...  8.9 us
    pallas_call x1, Pallas kernels, prepare(): pl.pallas_call(prepare_kernel, grid=(1,), in_specs=[whole((nodes, width))...  4.26 us
  transfers between devices with their start and end apart: 29, of which 12 were waited for; matrix products, arithmetic and copies ran while one was open for 3% of the time, Pallas kernels for 36%

profile of v4, /device:TPU:8, one launch (start us, length us, event | category | flops | bytes accessed | tf_op | source)
XLA Modules:
  0.0 204.1 jit_solution(8879241893838095560)
XLA Ops:
  0.6 4.1 %gather_out.1 = bf16[32,128,512]{2,1,0:T(8,128)(2,1)} custom-call(s32[32]{0:T(128)} %bitcast.14, bf16[768,256]{1,0:T(8,128)(2,1)} %key_ref.7, bf16[768,256]{1,0:T(8,128)(2,1)} %value_ref.7), custom_call_target="tpu_custom_call" | custom-call | flops 575000000 | bytes 1024 | tf_op jit(solution)/shard_map/gather_out/pallas_call | solution.py:59
  4.8 7.7 %all-to-all-start = ((bf16[32,128,512]{2,1,0:T(8,128)(2,1)}), bf16[32,128,512]{2,1,0:T(8,128)(2,1)}, u32[]{:S(2)}, u32[]{:S(2)}) async-start(bf16[32,128,512]{2,1,0:T(8,128)(2,1)} %gather_out.1), calls=%async_computation | async-start | bytes 8388608 | tf_op jit(solution)/shard_map/all_to_all | solution.py:608
  12.6 5.9 %collective-permute-start.10 = (bf16[768,256]{1,0:T(8,128)(2,1)S(1)}, bf16[768,256]{1,0:T(8,128)(2,1)S(1)}, u32[]{:S(2)}, u32[]{:S(2)}) collective-permute-start(bf16[768,256]{1,0:T(8,128)(2,1)S(1)} %copy-done.4), channel_id=1, source_target_pairs={{0,224},{32,0},{64,32},{96,64},{128,96},{160,128},{192,160},{224,1... | collective-permute-start | bytes 1179656 | tf_op jit(solution)/shard_map/ppermute | solution.py:600
  18.5 3.2 %collective-permute-start.1 = (bf16[768,256]{1,0:T(8,128)(2,1)S(1)}, bf16[768,256]{1,0:T(8,128)(2,1)S(1)}, u32[]{:S(2)}, u32[]{:S(2)}) collective-permute-start(bf16[768,256]{1,0:T(8,128)(2,1)S(1)} %copy-done.3), channel_id=1, source_target_pairs={{0,224},{32,0},{64,32},{96,64},{128,96},{160,128},{192,160},{224,1... | collective-permute-start | bytes 1179656 | tf_op jit(solution)/shard_map/ppermute | solution.py:600
  22.3 5.6 %collective-permute-done.10.v_above = bf16[768,256]{1,0:T(8,128)(2,1)S(1)} collective-permute-done((bf16[768,256]{1,0:T(8,128)(2,1)S(1)}, bf16[768,256]{1,0:T(8,128)(2,1)S(1)}, u32[]{:S(2)}, u32[]{:S(2)}) %collective-permute-start.10) | collective-permute-done | bytes 393248 | tf_op jit(solution)/shard_map/ppermute | solution.py:600
  28.0 3.7 %collective-permute-start.11 = (bf16[768,256]{1,0:T(8,128)(2,1)S(1)}, bf16[768,256]{1,0:T(8,128)(2,1)S(1)}, u32[]{:S(2)}, u32[]{:S(2)}) collective-permute-start(bf16[768,256]{1,0:T(8,128)(2,1)S(1)} %collective-permute-done.10.v_above), channel_id=1, source_target_pairs={{0,224},{32,0},{64,32},{96,64},{128,96},{160,128},{192,160},{224,1... | collective-permute-start | bytes 1179656 | tf_op jit(solution)/shard_map/ppermute | solution.py:600
  31.7 4.3 %prepare.1 = (bf16[768,256]{1,0:T(8,128)(2,1)}, bf16[768,512]{1,0:T(8,128)(2,1)}, bf16[768,512]{1,0:T(8,128)(2,1)}, bf16[768,512]{1,0:T(8,128)(2,1)}) custom-call(bf16[768,256]{1,0:T(8,128)(2,1)} %query_ref.7, bf16[768,256]{1,0:T(8,128)(2,1)} %update_grad_ref.1, bf16[256,256]{1,0:T(8,128)(2,1)} %out_weight.1, s32[3,768]{1,0:T(4,128)} %bitcast.12), custom_call_target="tpu_custom_call" | custom-call | flops 1150000000 | bytes 1024 | tf_op jit(solution)/shard_map/prepare/pallas_call | solution.py:92
  36.4 3.7 %collective-permute-done.k_below = bf16[768,256]{1,0:T(8,128)(2,1)S(1)} collective-permute-done((bf16[768,256]{1,0:T(8,128)(2,1)S(1)}, bf16[768,256]{1,0:T(8,128)(2,1)S(1)}, u32[]{:S(2)}, u32[]{:S(2)}) %collective-permute-start) | collective-permute-done | bytes 393248 | tf_op jit(solution)/shard_map/ppermute | solution.py:600
  40.1 3.2 %collective-permute-start.5 = (bf16[768,256]{1,0:T(8,128)(2,1)S(1)}, bf16[768,256]{1,0:T(8,128)(2,1)S(1)}, u32[]{:S(2)}, u32[]{:S(2)}) collective-permute-start(bf16[768,256]{1,0:T(8,128)(2,1)S(1)} %collective-permute-done.1.k_above), channel_id=1, source_target_pairs={{0,224},{32,0},{64,32},{96,64},{128,96},{160,128},{192,160},{224,1... | collective-permute-start | bytes 1179656 | tf_op jit(solution)/shard_map/ppermute | solution.py:600
  44.0 3.5 %fetch.2.far_2 = bf16[512,768]{1,0:T(8,128)(2,1)} custom-call(s32[1]{0:T(128)} %bitcast.2.group_ref, bf16[768,256]{1,0:T(8,128)(2,1)} %copy-done.16, bf16[768,256]{1,0:T(8,128)(2,1)} %copy-done.15, bf16[768,256]{1,0:T(8,128)(2,1)} %copy-done.18, bf16[768,256]{1,0:T(8,128)(2,1)} %copy-done.17, s32[1,768]{1,0:T(1,128)} %get-tuple-element.114.match_ref), custom_call_target="tpu_custom_call" | custom-call | flops 1150000000 | bytes 1024 | tf_op jit(solution)/shard_map/fetch/pallas_call | solution.py:372
  48.7 2.0 collective-permute-start.12
  50.7 6.3 %collective-permute-done.2.k_below = bf16[768,256]{1,0:T(8,128)(2,1)S(1)} collective-permute-done((bf16[768,256]{1,0:T(8,128)(2,1)S(1)}, bf16[768,256]{1,0:T(8,128)(2,1)S(1)}, u32[]{:S(2)}, u32[]{:S(2)}) %collective-permute-start.2) | collective-permute-done | bytes 393248 | tf_op jit(solution)/shard_map/ppermute | solution.py:600
  57.3 3.3 %collective-permute-start.6 = (bf16[384,256]{1,0:T(8,128)(2,1)S(1)}, bf16[384,256]{1,0:T(8,128)(2,1)S(1)}, u32[]{:S(2)}, u32[]{:S(2)}) collective-permute-start(bf16[384,256]{1,0:T(8,128)(2,1)S(1)} %slice.67), channel_id=1, source_target_pairs={{0,224},{32,0},{64,32},{96,64},{128,96},{160,128},{192,160},{224,1... | collective-permute-start | bytes 589832 | tf_op jit(solution)/shard_map/ppermute | solution.py:600
  62.6 2.6 %collective-permute-done.3 = bf16[384,256]{1,0:T(8,128)(2,1)S(1)} collective-permute-done((bf16[384,256]{1,0:T(8,128)(2,1)S(1)}, bf16[384,256]{1,0:T(8,128)(2,1)S(1)}, u32[]{:S(2)}, u32[]{:S(2)}) %collective-permute-start.3) | collective-permute-done | bytes 196640 | tf_op jit(solution)/shard_map/ppermute | solution.py:600
  65.2 3.2 %collective-permute-start.7 = (bf16[384,256]{1,0:T(8,128)(2,1)S(1)}, bf16[384,256]{1,0:T(8,128)(2,1)}, u32[]{:S(2)}, u32[]{:S(2)}) collective-permute-start(bf16[384,256]{1,0:T(8,128)(2,1)S(1)} %collective-permute-done.6), channel_id=1, source_target_pairs={{0,224},{32,0},{64,32},{96,64},{128,96},{160,128},{192,160},{224,1... | collective-permute-start | bytes 589832 | tf_op jit(solution)/shard_map/ppermute | solution.py:600
  69.2 3.5 %fetch.3.far_1 = bf16[512,768]{1,0:T(8,128)(2,1)} custom-call(s32[1]{0:T(128)} %bitcast.2.group_ref, bf16[768,256]{1,0:T(8,128)(2,1)} %copy-done.7, bf16[768,256]{1,0:T(8,128)(2,1)} %copy-done.8, bf16[768,256]{1,0:T(8,128)(2,1)} %copy-done.6, bf16[768,256]{1,0:T(8,128)(2,1)} %copy-done.5, s32[1,768]{1,0:T(1,128)} %get-tuple-element.115.match_ref), custom_call_target="tpu_custom_call" | custom-call | flops 1150000000 | bytes 1024 | tf_op jit(solution)/shard_map/fetch/pallas_call | solution.py:372
  75.3 21.0 %forward.1 = (bf16[768,256]{1,0:T(8,128)(2,1)}, bf16[8,32,256]{2,1,0:T(8,128)(2,1)}, f32[12,8,512]{2,1,0:T(8,128)}, f32[12,128,128]{2,1,0:T(8,128)}, f32[3,16,768]{2,1,0:T(8,128)}) custom-call(s32[48]{0:T(128)} %reshape_squeeze.3.tile_block, s32[6]{0:T(128)} %bitcast.17, f32[8]{0:T(128)} %bias_ref.1, bf16[32,128,512]{2,1,0:T(8,128)(2,1)} %all-to-all-done.halo_ref, ...), custom_call_target="tpu_custom_call" | custom-call | flops 3449999872 | bytes 1024 | tf_op jit(solution)/shard_map/forward/pallas_call | solution.py:372
  96.4 5.4 %all-to-all-start.1 = ((bf16[8,32,256]{2,1,0:T(8,128)(2,1)}), bf16[8,32,256]{2,1,0:T(8,128)(2,1)S(1)}, u32[]{:S(2)}, u32[]{:S(2)}) async-start(bf16[8,32,256]{2,1,0:T(8,128)(2,1)} %get-tuple-element.83), calls=%async_computation.1 | async-start | bytes 262144 | tf_op jit(solution)/shard_map/all_to_all | solution.py:608
  101.7 15.9 %backward.3 = (bf16[32,160,256]{2,1,0:T(8,128)(2,1)}, f32[6,128,256]{2,1,0:T(8,128)}, f32[768,128]{1,0:T(8,128)}) custom-call(s32[48]{0:T(128)} %reshape_squeeze.3.tile_block, s32[6]{0:T(128)} %bitcast.18, bf16[768,256]{1,0:T(8,128)(2,1)} %key_ref.7, bf16[768,256]{1,0:T(8,128)(2,1)} %value_ref.7, bf16[32,128,512]{2,1,0:T(8,128)(2,1)} %all-to-all-done.halo_ref, ...), custom_call_target="tpu_custom_call" | custom-call | flops 16099999744 | bytes 1024 | tf_op jit(solution)/shard_map/backward/pallas_call | solution.py:372
  119.6 7.5 %all-to-all-start.2 = ((bf16[32,160,256]{2,1,0:T(8,128)(2,1)}), bf16[32,160,256]{2,1,0:T(8,128)(2,1)S(1)}, u32[]{:S(2)}, u32[]{:S(2)}) async-start(bf16[32,160,256]{2,1,0:T(8,128)(2,1)} %broadcast_dynamic-update-slice_fusion), calls=%async_computation.2 | async-start | bytes 5242880 | tf_op jit(solution)/shard_map/all_to_all | solution.py:608
  127.1 3.2 %collective-permute-start.17 = (bf16[768,512]{1,0:T(8,128)(2,1)}, bf16[768,512]{1,0:T(8,128)(2,1)S(1)}, u32[]{:S(2)}, u32[]{:S(2)}) collective-permute-start(bf16[768,512]{1,0:T(8,128)(2,1)} %get-tuple-element.86), channel_id=1, source_target_pairs={{0,64},{1,65},{2,66},{3,67},{4,68},{5,69},{6,70},{7,71},{8,72},{9,... | collective-permute-start | bytes 2359304 | tf_op jit(solution)/shard_map/ppermute | solution.py:595
  131.8 16.0 %backward.2 = (bf16[32,128,256]{2,1,0:T(8,128)(2,1)}, f32[6,128,256]{2,1,0:T(8,128)}, f32[768,128]{1,0:T(8,128)}) custom-call(s32[48]{0:T(128)} %reshape_squeeze.3.tile_block, s32[6]{0:T(128)} %bitcast.19, bf16[768,256]{1,0:T(8,128)(2,1)} %key_ref.7, bf16[768,256]{1,0:T(8,128)(2,1)} %value_ref.7, bf16[32,128,512]{2,1,0:T(8,128)(2,1)} %all-to-all-done.halo_ref, ...), custom_call_target="tpu_custom_call" | custom-call | flops 16099999744 | bytes 1024 | tf_op jit(solution)/shard_map/backward/pallas_call | solution.py:372
  147.8 2.6 %place.1 = (f32[16,768]{1,0:T(8,128)}, f32[16,768]{1,0:T(8,128)}, f32[16,768]{1,0:T(8,128)}) custom-call(s32[3,768]{1,0:T(4,128)} %bitcast.13, f32[3,16,768]{2,1,0:T(8,128)} %get-tuple-element.88.rows_ref), custom_call_target="tpu_custom_call" | custom-call | flops 1150000000 | bytes 1024 | tf_op jit(solution)/shard_map/place/pallas_call | solution.py:372
  150.4 15.0 %collective-permute-done.17.refs_1_ = bf16[768,512]{1,0:T(8,128)(2,1)S(1)} collective-permute-done((bf16[768,512]{1,0:T(8,128)(2,1)}, bf16[768,512]{1,0:T(8,128)(2,1)S(1)}, u32[]{:S(2)}, u32[]{:S(2)}) %collective-permute-start.17) | collective-permute-done | bytes 786464 | tf_op jit(solution)/shard_map/ppermute | solution.py:595
  165.6 7.4 %all-to-all-start.3 = ((bf16[32,128,256]{2,1,0:T(8,128)(2,1)}), bf16[32,128,256]{2,1,0:T(8,128)(2,1)}, u32[]{:S(2)}, u32[]{:S(2)}) async-start(bf16[32,128,256]{2,1,0:T(8,128)(2,1)} %get-tuple-element.92), calls=%async_computation.3 | async-start | bytes 4194304 | tf_op jit(solution)/shard_map/all_to_all | solution.py:608
  174.8 2.3 %collective-permute-done.22 = f32[32,256]{1,0:T(8,128)S(1)} collective-permute-done((f32[32,256]{1,0:T(8,128)S(1)}, f32[32,256]{1,0:T(8,128)S(1)}, u32[]{:S(2)}, u32[]{:S(2)}) %collective-permute-start.22) | collective-permute-done | bytes 32800 | tf_op jit(solution)/shard_map/ppermute | solution.py:604
  179.0 4.3 %collective-permute-start.19 = (f32[16,768]{1,0:T(8,128)}, f32[16,768]{1,0:T(8,128)S(1)}, u32[]{:S(2)}, u32[]{:S(2)}) collective-permute-start(f32[16,768]{1,0:T(8,128)} %get-tuple-element.99), channel_id=1, source_target_pairs={{0,128},{1,129},{2,130},{3,131},{4,132},{5,133},{6,134},{7,135},{8... | collective-permute-start | bytes 147464 | tf_op jit(solution)/shard_map/ppermute | solution.py:595
  183.3 2.2 %collective-permute-start.20 = (f32[16,768]{1,0:T(8,128)}, f32[16,768]{1,0:T(8,128)S(1)}, u32[]{:S(2)}, u32[]{:S(2)}) collective-permute-start(f32[16,768]{1,0:T(8,128)} %get-tuple-element.100), channel_id=1, source_target_pairs={{0,64},{1,65},{2,66},{3,67},{4,68},{5,69},{6,70},{7,71},{8,72},{9,... | collective-permute-start | bytes 147464 | tf_op jit(solution)/shard_map/ppermute | solution.py:595
  185.6 5.3 %collective-permute-start.24 = (f32[128,256]{1,0:T(8,128)S(1)}, f32[128,256]{1,0:T(8,128)S(1)}, u32[]{:S(2)}, u32[]{:S(2)}) collective-permute-start(f32[128,256]{1,0:T(8,128)S(1)} %maximum_select_fusion.1), channel_id=1, source_target_pairs={{0,128},{32,160},{64,192},{96,224},{128,0},{160,32},{192,64},{224,... | collective-permute-start | bytes 393224 | tf_op jit(solution)/shard_map/ppermute | solution.py:604
  190.9 2.0 %pad_maximum_fusion = f32[768,256]{1,0:T(8,128)} fusion(f32[768,128]{1,0:T(8,128)} %get-tuple-element.105, f32[768,128]{1,0:T(8,128)} %get-tuple-element.104), kind=kLoop, calls=%fused_computation.1 | loop fusion | flops 196608 | bytes 1572864 | tf_op jit(solution)/shard_map/concatenate | solution.py:674
  193.9 5.8 %collect.1 = (f32[768,256]{1,0:T(8,128)}, f32[768,256]{1,0:T(8,128)}) custom-call(s32[32]{0:T(128)} %bitcast.15, f32[6,128,256]{2,1,0:T(8,128)} %get-tuple-element.93.own_a, f32[6,128,256]{2,1,0:T(8,128)} %get-tuple-element.94.own_b, bf16[32,160,256]{2,1,0:T(8,128)(2,1)} %copy-done, bf16[768,512]{1,0:T(8,128)(2,1)} %copy-done.1, bf16[768,512]{1,0:T(8,128)(2,1)} %copy-done.2, ...), custom_call_target="tpu_custom_call" | custom-call | flops 1150000000 | bytes 1024 | tf_op jit(solution)/shard_map/collect/pallas_call | solution.py:372
  200.4 3.7 %finish.1 = (f32[768,256]{1,0:T(8,128)}, f32[768,256]{1,0:T(8,128)}) custom-call(s32[32]{0:T(128)} %bitcast.16, bf16[32,128,256]{2,1,0:T(8,128)(2,1)} %all-to-all-done.3.home_ref, f32[768,256]{1,0:T(8,128)} %get-tuple-element.108.key_in, f32[768,256]{1,0:T(8,128)} %get-tuple-element.109.value_in), custom_call_target="tpu_custom_call", output_to_operand_aliasing={{0}: (2, {}), {1}: (3, {})} | custom-call | flops 1150000000 | bytes 1024 | tf_op jit(solution)/shard_map/finish/pallas_call | solution.py:577
  (94 shorter events, 17.4 us)
Async XLA Ops:
  4.8 70.5 %all-to-all-start = ((bf16[32,128,512]{2,1,0:T(8,128)(2,1)}), bf16[32,128,512]{2,1,0:T(8,128)(2,1)}, u32[]{:S(2)}, u32[]{:S(2)}) async-start(bf16[32,128,512]{2,1,0:T(8,128)(2,1)} %gather_out.1), calls=%async_computation | async-start | bytes 8388608 | tf_op jit(solution)/shard_map/all_to_all | solution.py:608
  12.6 15.4 %collective-permute-start.10 = (bf16[768,256]{1,0:T(8,128)(2,1)S(1)}, bf16[768,256]{1,0:T(8,128)(2,1)S(1)}, u32[]{:S(2)}, u32[]{:S(2)}) collective-permute-start(bf16[768,256]{1,0:T(8,128)(2,1)S(1)} %copy-done.4), channel_id=1, source_target_pairs={{0,224},{32,0},{64,32},{96,64},{128,96},{160,128},{192,160},{224,1... | collective-permute-start | bytes 1179656 | tf_op jit(solution)/shard_map/ppermute | solution.py:600
  18.5 13.2 %collective-permute-start.8 = (bf16[768,256]{1,0:T(8,128)(2,1)S(1)}, bf16[768,256]{1,0:T(8,128)(2,1)S(1)}, u32[]{:S(2)}, u32[]{:S(2)}) collective-permute-start(bf16[768,256]{1,0:T(8,128)(2,1)S(1)} %copy-done.4), channel_id=1, source_target_pairs={{0,32},{32,64},{64,96},{96,128},{128,160},{160,192},{192,224},{224... | collective-permute-start | bytes 1179656 | tf_op jit(solution)/shard_map/ppermute | solution.py:600
  18.5 17.9 %collective-permute-start.1 = (bf16[768,256]{1,0:T(8,128)(2,1)S(1)}, bf16[768,256]{1,0:T(8,128)(2,1)S(1)}, u32[]{:S(2)}, u32[]{:S(2)}) collective-permute-start(bf16[768,256]{1,0:T(8,128)(2,1)S(1)} %copy-done.3), channel_id=1, source_target_pairs={{0,224},{32,0},{64,32},{96,64},{128,96},{160,128},{192,160},{224,1... | collective-permute-start | bytes 1179656 | tf_op jit(solution)/shard_map/ppermute | solution.py:600
  21.7 18.4 %collective-permute-start = (bf16[768,256]{1,0:T(8,128)(2,1)S(1)}, bf16[768,256]{1,0:T(8,128)(2,1)S(1)}, u32[]{:S(2)}, u32[]{:S(2)}) collective-permute-start(bf16[768,256]{1,0:T(8,128)(2,1)S(1)} %copy-done.3), channel_id=1, source_target_pairs={{0,32},{32,64},{64,96},{96,128},{128,160},{160,192},{192,224},{224... | collective-permute-start | bytes 1179656 | tf_op jit(solution)/shard_map/ppermute | solution.py:600
  28.0 19.6 %collective-permute-start.11 = (bf16[768,256]{1,0:T(8,128)(2,1)S(1)}, bf16[768,256]{1,0:T(8,128)(2,1)S(1)}, u32[]{:S(2)}, u32[]{:S(2)}) collective-permute-start(bf16[768,256]{1,0:T(8,128)(2,1)S(1)} %collective-permute-done.10.v_above), channel_id=1, source_target_pairs={{0,224},{32,0},{64,32},{96,64},{128,96},{160,128},{192,160},{224,1... | collective-permute-start | bytes 1179656 | tf_op jit(solution)/shard_map/ppermute | solution.py:600
  31.7 16.9 %collective-permute-start.9 = (bf16[768,256]{1,0:T(8,128)(2,1)S(1)}, bf16[768,256]{1,0:T(8,128)(2,1)S(1)}, u32[]{:S(2)}, u32[]{:S(2)}) collective-permute-start(bf16[768,256]{1,0:T(8,128)(2,1)S(1)} %collective-permute-done.8.v_below), channel_id=1, source_target_pairs={{0,32},{32,64},{64,96},{96,128},{128,160},{160,192},{192,224},{224... | collective-permute-start | bytes 1179656 | tf_op jit(solution)/shard_map/ppermute | solution.py:600
  40.1 16.9 %collective-permute-start.2 = (bf16[768,256]{1,0:T(8,128)(2,1)S(1)}, bf16[768,256]{1,0:T(8,128)(2,1)S(1)}, u32[]{:S(2)}, u32[]{:S(2)}) collective-permute-start(bf16[768,256]{1,0:T(8,128)(2,1)S(1)} %collective-permute-done.k_below), channel_id=1, source_target_pairs={{0,32},{32,64},{64,96},{96,128},{128,160},{160,192},{192,224},{224... | collective-permute-start | bytes 1179656 | tf_op jit(solution)/shard_map/ppermute | solution.py:600
  40.1 17.1 %collective-permute-start.5 = (bf16[768,256]{1,0:T(8,128)(2,1)S(1)}, bf16[768,256]{1,0:T(8,128)(2,1)S(1)}, u32[]{:S(2)}, u32[]{:S(2)}) collective-permute-start(bf16[768,256]{1,0:T(8,128)(2,1)S(1)} %collective-permute-done.1.k_above), channel_id=1, source_target_pairs={{0,224},{32,0},{64,32},{96,64},{128,96},{160,128},{192,160},{224,1... | collective-permute-start | bytes 1179656 | tf_op jit(solution)/shard_map/ppermute | solution.py:600
  44.0 24.5 %copy-start.13 = (s32[1,6,8]{2,0,1:T(1,128)S(1)}, s32[1,6,8]{2,0,1:T(1,128)}, u32[]{:S(2)}) copy-start(s32[1,6,8]{2,0,1:T(1,128)} %param.18) | copy-start | bytes 580
  47.6 21.6 %copy-start.5 = (bf16[768,256]{1,0:T(8,128)(2,1)}, bf16[768,256]{1,0:T(8,128)(2,1)S(1)}, u32[]{:S(2)}) copy-start(bf16[768,256]{1,0:T(8,128)(2,1)S(1)} %collective-permute-done.11.v_above) | copy-start | bytes 1179652
  48.6 24.9 %copy-start.14 = (bf16[768,512]{1,0:T(8,128)(2,1)S(1)}, bf16[768,512]{1,0:T(8,128)(2,1)}, u32[]{:S(2)}) copy-start(bf16[768,512]{1,0:T(8,128)(2,1)} %get-tuple-element.84) | copy-start | bytes 2359300
  48.6 12.0 %collective-permute-start.14 = (bf16[384,256]{1,0:T(8,128)(2,1)S(1)}, bf16[384,256]{1,0:T(8,128)(2,1)S(1)}, u32[]{:S(2)}, u32[]{:S(2)}) collective-permute-start(bf16[384,256]{1,0:T(8,128)(2,1)S(1)} %slice.60), channel_id=1, source_target_pairs={{0,224},{32,0},{64,32},{96,64},{128,96},{160,128},{192,160},{224,1... | collective-permute-start | bytes 589832 | tf_op jit(solution)/shard_map/ppermute | solution.py:600
  48.7 12.3 %collective-permute-start.12 = (bf16[384,256]{1,0:T(8,128)(2,1)S(1)}, bf16[384,256]{1,0:T(8,128)(2,1)S(1)}, u32[]{:S(2)}, u32[]{:S(2)}) collective-permute-start(bf16[384,256]{1,0:T(8,128)(2,1)S(1)} %slice.59), channel_id=1, source_target_pairs={{0,32},{32,64},{64,96},{96,128},{128,160},{160,192},{192,224},{224... | collective-permute-start | bytes 589832 | tf_op jit(solution)/shard_map/ppermute | solution.py:600
  57.0 8.2 %collective-permute-start.3 = (bf16[384,256]{1,0:T(8,128)(2,1)S(1)}, bf16[384,256]{1,0:T(8,128)(2,1)S(1)}, u32[]{:S(2)}, u32[]{:S(2)}) collective-permute-start(bf16[384,256]{1,0:T(8,128)(2,1)S(1)} %slice.66), channel_id=1, source_target_pairs={{0,32},{32,64},{64,96},{96,128},{128,160},{160,192},{192,224},{224... | collective-permute-start | bytes 589832 | tf_op jit(solution)/shard_map/ppermute | solution.py:600
  57.3 7.9 %collective-permute-start.6 = (bf16[384,256]{1,0:T(8,128)(2,1)S(1)}, bf16[384,256]{1,0:T(8,128)(2,1)S(1)}, u32[]{:S(2)}, u32[]{:S(2)}) collective-permute-start(bf16[384,256]{1,0:T(8,128)(2,1)S(1)} %slice.67), channel_id=1, source_target_pairs={{0,224},{32,0},{64,32},{96,64},{128,96},{160,128},{192,160},{224,1... | collective-permute-start | bytes 589832 | tf_op jit(solution)/shard_map/ppermute | solution.py:600
  60.6 12.1 %collective-permute-start.15 = (bf16[384,256]{1,0:T(8,128)(2,1)S(1)}, bf16[384,256]{1,0:T(8,128)(2,1)S(1)}, u32[]{:S(2)}, u32[]{:S(2)}) collective-permute-start(bf16[384,256]{1,0:T(8,128)(2,1)S(1)} %collective-permute-done.14), channel_id=1, source_target_pairs={{0,224},{32,0},{64,32},{96,64},{128,96},{160,128},{192,160},{224,1... | collective-permute-start | bytes 589832 | tf_op jit(solution)/shard_map/ppermute | solution.py:600
  61.0 11.7 %collective-permute-start.13 = (bf16[384,256]{1,0:T(8,128)(2,1)S(1)}, bf16[384,256]{1,0:T(8,128)(2,1)S(1)}, u32[]{:S(2)}, u32[]{:S(2)}) collective-permute-start(bf16[384,256]{1,0:T(8,128)(2,1)S(1)} %collective-permute-done.12), channel_id=1, source_target_pairs={{0,32},{32,64},{64,96},{96,128},{128,160},{160,192},{192,224},{224... | collective-permute-start | bytes 589832 | tf_op jit(solution)/shard_map/ppermute | solution.py:600
  65.2 7.6 %collective-permute-start.4 = (bf16[384,256]{1,0:T(8,128)(2,1)S(1)}, bf16[384,256]{1,0:T(8,128)(2,1)}, u32[]{:S(2)}, u32[]{:S(2)}) collective-permute-start(bf16[384,256]{1,0:T(8,128)(2,1)S(1)} %collective-permute-done.3), channel_id=1, source_target_pairs={{0,32},{32,64},{64,96},{96,128},{128,160},{160,192},{192,224},{224... | collective-permute-start | bytes 589832 | tf_op jit(solution)/shard_map/ppermute | solution.py:600
  65.2 7.6 %collective-permute-start.7 = (bf16[384,256]{1,0:T(8,128)(2,1)S(1)}, bf16[384,256]{1,0:T(8,128)(2,1)}, u32[]{:S(2)}, u32[]{:S(2)}) collective-permute-start(bf16[384,256]{1,0:T(8,128)(2,1)S(1)} %collective-permute-done.6), channel_id=1, source_target_pairs={{0,224},{32,0},{64,32},{96,64},{128,96},{160,128},{192,160},{224,1... | collective-permute-start | bytes 589832 | tf_op jit(solution)/shard_map/ppermute | solution.py:600
  73.5 45.2 %collective-permute-start.16 = (bf16[768,512]{1,0:T(8,128)(2,1)S(1)}, bf16[768,512]{1,0:T(8,128)(2,1)S(1)}, u32[]{:S(2)}, u32[]{:S(2)}) collective-permute-start(bf16[768,512]{1,0:T(8,128)(2,1)S(1)} %copy-done.14), channel_id=1, source_target_pairs={{0,128},{1,129},{2,130},{3,131},{4,132},{5,133},{6,134},{7,135},{8... | collective-permute-start | bytes 2359304 | tf_op jit(solution)/shard_map/ppermute | solution.py:595
  96.4 21.3 %all-to-all-start.1 = ((bf16[8,32,256]{2,1,0:T(8,128)(2,1)}), bf16[8,32,256]{2,1,0:T(8,128)(2,1)S(1)}, u32[]{:S(2)}, u32[]{:S(2)}) async-start(bf16[8,32,256]{2,1,0:T(8,128)(2,1)} %get-tuple-element.83), calls=%async_computation.1 | async-start | bytes 262144 | tf_op jit(solution)/shard_map/all_to_all | solution.py:608
  119.6 46.0 %all-to-all-start.2 = ((bf16[32,160,256]{2,1,0:T(8,128)(2,1)}), bf16[32,160,256]{2,1,0:T(8,128)(2,1)S(1)}, u32[]{:S(2)}, u32[]{:S(2)}) async-start(bf16[32,160,256]{2,1,0:T(8,128)(2,1)} %broadcast_dynamic-update-slice_fusion), calls=%async_computation.2 | async-start | bytes 5242880 | tf_op jit(solution)/shard_map/all_to_all | solution.py:608
  127.1 38.3 %collective-permute-start.17 = (bf16[768,512]{1,0:T(8,128)(2,1)}, bf16[768,512]{1,0:T(8,128)(2,1)S(1)}, u32[]{:S(2)}, u32[]{:S(2)}) collective-permute-start(bf16[768,512]{1,0:T(8,128)(2,1)} %get-tuple-element.86), channel_id=1, source_target_pairs={{0,64},{1,65},{2,66},{3,67},{4,68},{5,69},{6,70},{7,71},{8,72},{9,... | collective-permute-start | bytes 2359304 | tf_op jit(solution)/shard_map/ppermute | solution.py:595
  130.4 35.2 %collective-permute-start.18 = (bf16[768,512]{1,0:T(8,128)(2,1)}, bf16[768,512]{1,0:T(8,128)(2,1)}, u32[]{:S(2)}, u32[]{:S(2)}) collective-permute-start(bf16[768,512]{1,0:T(8,128)(2,1)} %get-tuple-element.87), channel_id=1, source_target_pairs={{0,32},{1,33},{2,34},{3,35},{4,36},{5,37},{6,38},{7,39},{8,40},{9,... | collective-permute-start | bytes 2359304 | tf_op jit(solution)/shard_map/ppermute | solution.py:595
  165.6 34.8 %all-to-all-start.3 = ((bf16[32,128,256]{2,1,0:T(8,128)(2,1)}), bf16[32,128,256]{2,1,0:T(8,128)(2,1)}, u32[]{:S(2)}, u32[]{:S(2)}) async-start(bf16[32,128,256]{2,1,0:T(8,128)(2,1)} %get-tuple-element.92), calls=%async_computation.3 | async-start | bytes 4194304 | tf_op jit(solution)/shard_map/all_to_all | solution.py:608
  173.1 4.0 %collective-permute-start.22 = (f32[32,256]{1,0:T(8,128)S(1)}, f32[32,256]{1,0:T(8,128)S(1)}, u32[]{:S(2)}, u32[]{:S(2)}) collective-permute-start(f32[32,256]{1,0:T(8,128)S(1)} %broadcast_multiply_fusion), channel_id=1, source_target_pairs={{0,32},{32,0},{64,96},{96,64},{128,160},{160,128},{192,224},{224,1... | collective-permute-start | bytes 98312 | tf_op jit(solution)/shard_map/ppermute | solution.py:604
  177.1 8.4 %collective-permute-start.23 = (f32[64,256]{1,0:T(8,128)S(1)}, f32[64,256]{1,0:T(8,128)S(1)}, u32[]{:S(2)}, u32[]{:S(2)}) collective-permute-start(f32[64,256]{1,0:T(8,128)S(1)} %maximum_select_fusion.2), channel_id=1, source_target_pairs={{0,64},{32,96},{64,0},{96,32},{128,192},{160,224},{192,128},{224,1... | collective-permute-start | bytes 196616 | tf_op jit(solution)/shard_map/ppermute | solution.py:604
  179.0 13.9 %collective-permute-start.19 = (f32[16,768]{1,0:T(8,128)}, f32[16,768]{1,0:T(8,128)S(1)}, u32[]{:S(2)}, u32[]{:S(2)}) collective-permute-start(f32[16,768]{1,0:T(8,128)} %get-tuple-element.99), channel_id=1, source_target_pairs={{0,128},{1,129},{2,130},{3,131},{4,132},{5,133},{6,134},{7,135},{8... | collective-permute-start | bytes 147464 | tf_op jit(solution)/shard_map/ppermute | solution.py:595
  183.3 9.6 %collective-permute-start.20 = (f32[16,768]{1,0:T(8,128)}, f32[16,768]{1,0:T(8,128)S(1)}, u32[]{:S(2)}, u32[]{:S(2)}) collective-permute-start(f32[16,768]{1,0:T(8,128)} %get-tuple-element.100), channel_id=1, source_target_pairs={{0,64},{1,65},{2,66},{3,67},{4,68},{5,69},{6,70},{7,71},{8,72},{9,... | collective-permute-start | bytes 147464 | tf_op jit(solution)/shard_map/ppermute | solution.py:595
  185.5 7.8 %collective-permute-start.21 = (f32[16,768]{1,0:T(8,128)}, f32[16,768]{1,0:T(8,128)S(1)}, u32[]{:S(2)}, u32[]{:S(2)}) collective-permute-start(f32[16,768]{1,0:T(8,128)} %get-tuple-element.101), channel_id=1, source_target_pairs={{0,32},{1,33},{2,34},{3,35},{4,36},{5,37},{6,38},{7,39},{8,40},{9,... | collective-permute-start | bytes 147464 | tf_op jit(solution)/shard_map/ppermute | solution.py:595
  185.6 14.1 %collective-permute-start.24 = (f32[128,256]{1,0:T(8,128)S(1)}, f32[128,256]{1,0:T(8,128)S(1)}, u32[]{:S(2)}, u32[]{:S(2)}) collective-permute-start(f32[128,256]{1,0:T(8,128)S(1)} %maximum_select_fusion.1), channel_id=1, source_target_pairs={{0,128},{32,160},{64,192},{96,224},{128,0},{160,32},{192,64},{224,... | collective-permute-start | bytes 393224 | tf_op jit(solution)/shard_map/ppermute | solution.py:604
  (18 other events, 169.1 us)
